TPU v7x, 256 devices: a whole 4x4x8 slice. The times are simulated.
256 devices in a mesh: dp: 8 (over x, core), shard: 32 (over y, z).
Axes of the slice: x: 4, y: 4, z: 8, core: 2. Of those that a mesh axis runs over, the one named last changes fastest.
Arguments:
- grads: bfloat16 [8, 256, 512, 512], P('dp', None, 'shard'), may hold values from -120 to 120
- owned: int32 [8, 32], replicated, may hold values from 0 to 31, as said below
- left_stat: float32 [8, 32, 512, 512], P('dp', 'shard'), may hold values from -1 to 16, as said below
- right_stat: float32 [8, 32, 512, 512], P('dp', 'shard'), may hold values from -1 to 16, as said below
Outputs:
- update: float32 [256, 512, 512], P('dp', 'shard')
- left_new: float32 [8, 32, 512, 512], P('dp', 'shard')
- right_new: float32 [8, 32, 512, 512], P('dp', 'shard')
Inputs may be any that keep to these rules, and one draw needn't show every extreme that they name: `owned`: each row is a permutation of 0 to 31. `left_stat`: symmetric with a positive diagonal larger than the sum of its row's other magnitudes. `right_stat`: symmetric with a positive diagonal larger than the sum of its row's other magnitudes.
All inputs are finite; a program needn't handle non-finite values.
Results may differ from a plain program's by a relative error of at most 0.0003.
Values may be sent and summed in bfloat16 or wider, within the bound.
No kernel may reach another device: no remote copies, remote signals or barrier semaphores. Data moves between devices by JAX's collectives and lax.ppermute only.
A program may use at most 64 MiB of HBM per device.

v0:
```python
import jax
import jax.numpy as jnp
from jax import lax
from jax.sharding import PartitionSpec as P

NEWTON = 2


def product(left, right):
    return jnp.dot(left, right, precision=lax.Precision.HIGHEST, preferred_element_type=jnp.float32)


def inverse_root(stat):
    eye = jnp.eye(stat.shape[0], dtype=jnp.float32)
    shifted = stat + 1e-06 * eye
    norm_value = jnp.sqrt(jnp.sum(shifted * shifted))
    matrix = shifted / norm_value
    root = eye * norm_value ** (-0.25)
    for step in range(NEWTON):
        factor = (5.0 * eye - matrix) * 0.25
        root = product(root, factor)
        square = product(factor, factor)
        matrix = product(product(square, square), matrix)
    return root


def precondition(grad, left_old, right_old):
    order = grad.shape[0]
    left_fresh = 0.95 * left_old + product(grad, grad.T) / order
    right_fresh = 0.95 * right_old + product(grad.T, grad) / order
    shaped = product(product(inverse_root(left_fresh), grad), inverse_root(right_fresh))
    graft = jnp.sqrt(jnp.mean(grad * grad) + 1e-06) / jnp.sqrt(jnp.mean(shaped * shaped) + 1e-06)
    return (left_fresh, right_fresh, shaped * graft)


def invert(home, source):
    return jnp.zeros_like(home).at[home].set(source)


def body(grads, owned, left_stat, right_stat):
    shards = lax.axis_size("shard")
    group = lax.axis_index("dp")
    local_part = grads[0]
    blocks = local_part.shape[0]
    strip = local_part.shape[1]
    width = local_part.shape[2]
    my_row = lax.dynamic_index_in_dim(owned, group, 0, keepdims=False)
    mine = lax.psum_scatter(local_part.astype(jnp.float32), "dp", scatter_dimension=0, tiled=True)
    ordered = jnp.take(mine, my_row, axis=0)
    grad = lax.all_to_all(ordered, "shard", split_axis=0, concat_axis=1, tiled=True)[0]
    total = lax.psum(jnp.sum(grad * grad), ("dp", "shard"))
    left_fresh, right_fresh, shaped = precondition(grad, left_stat[0, 0], right_stat[0, 0])
    layer = 1.0 / jnp.sqrt(total / (blocks * width * width) + 1e-06)
    scaled = shaped * layer
    pieces = lax.all_to_all(
        scaled.reshape(shards, strip, width), "shard", split_axis=0, concat_axis=0, tiled=True
    )
    slot = invert(my_row, jnp.arange(shards, dtype=jnp.int32))
    update = jnp.take(pieces, slot, axis=0)
    return (update, left_fresh[None, None], right_fresh[None, None])


def solution(mesh):
    return jax.shard_map(
        body,
        mesh=mesh,
        in_specs=(
            P("dp", None, "shard", None),
            P(),
            P("dp", "shard", None, None),
            P("dp", "shard", None, None),
        ),
        out_specs=(
            P("dp", "shard", None),
            P("dp", "shard", None, None),
            P("dp", "shard", None, None),
        ),
        check_vma=False,
    )
```

profile of v0, /device:TPU:32, one launch (start us, length us, event | category | flops | bytes accessed | tf_op | source)
XLA Modules:
  0.0 268.6 jit_solution(12866554214592818691)
XLA Ops:
  7.2 0.0 reduce-scatter.2.cloned.1.call-start
  7.2 6.6 %bitcast_convert_fusion = f32[256,16,512]{2,1,0:T(8,128)} fusion(bf16[1,256,16,512]{3,2,1,0:T(8,128)(2,1)} %param.6), kind=kLoop, calls=%fused_computation.3 | loop fusion | flops 2097152 | bytes 12582912 | tf_op jit(solution)/shard_map/convert_element_type | solution.py:48
  13.8 0.0 copy-start
  13.8 0.0 reduce-scatter.2.cloned.1.call-update
  13.9 0.8 compare_and_fusion.1
  14.7 56.9 %reduce-scatter.2.cloned.1.call-done = f32[32,16,512]{2,1,0:T(8,128)} async-done(((f32[256,16,512]{2,1,0:T(8,128)}), f32[32,16,512]{2,1,0:T(8,128)}) %reduce-scatter.2.cloned.1.call-update) | async-done | bytes 1048592 | tf_op jit(solution)/shard_map/reduce_scatter | solution.py:48
  71.6 1.8 gather_fusion
  73.4 0.1 broadcast_select_fusion.1
  73.5 37.9 %all_to_all.14 = f32[32,16,512]{2,1,0:T(8,128)S(1)} all-to-all(f32[32,16,512]{2,1,0:T(8,128)S(1)} %broadcast_select_fusion.1), channel_id=1, replica_groups=mesh['dp'=8,'shard'=32] {'shard'}, dimensions={0} | all-to-all | bytes 2097152 | tf_op jit(solution)/shard_map/all_to_all | solution.py:50
  111.4 0.0 copy-done
  111.4 2.6 multiply_reduce_fusion.3
  114.1 0.0 copy-start.1
  114.8 2.0 fusion.16
  116.8 0.0 copy-start.4
  116.8 2.9 %fusion.9 = f32[512,512]{1,0:T(8,128)} fusion(f32[]{:T(128)S(6)} %pow.6, f32[512,512]{1,0:T(8,128)S(1)} %get-tuple-element.7, f32[]{:T(128)S(6)} %sqrt.15), kind=kOutput, calls=%fused_computation.25 | convolution fusion | flops 1612972032 | bytes 2097160 | tf_op jit(solution)/shard_map/dot_general | solution.py:10
  119.7 1.8 fusion.54
  121.6 2.9 %fusion.1 = f32[512,512]{1,0:T(8,128)} fusion(f32[512,512]{1,0:T(8,128)S(1)} %fusion.54, f32[512,512]{1,0:T(8,128)S(1)} %get-tuple-element.7, f32[]{:T(128)S(6)} %sqrt.15), kind=kOutput, calls=%fused_computation.13 | convolution fusion | flops 1612709888 | bytes 3145732 | tf_op jit(solution)/shard_map/dot_general | solution.py:10
  124.5 0.0 copy-done.1
  124.5 0.0 copy-done.4
  124.5 2.7 %multiply_reduce_fusion.2 = (f32[]{:T(128)}, f32[512,512]{1,0:T(8,128)S(1)}) fusion(f32[32,16,512]{2,1,0:T(8,128)S(1)} %all_to_all.14, f32[1,1,512,512]{3,2,1,0:T(8,128)S(1)} %copy-done.4), kind=kOutput, calls=%fused_computation.24 | convolution fusion | flops 1612709888 | bytes 3145732 | tf_op jit(solution)/shard_map/dot_general | solution.py:10
  127.2 0.0 copy-start.5
  128.0 0.2 copy-done.5
  128.2 2.2 fusion.13
  130.4 0.0 copy-start.6
  130.4 0.0 copy-start.2
  130.4 0.0 copy-start.3
  130.4 3.3 %fusion.7 = f32[512,512]{1,0:T(8,128)S(1)} fusion(f32[]{:T(128)S(6)} %pow.7, f32[512,512]{1,0:T(8,128)} %copy-done.5, f32[]{:T(128)S(6)} %sqrt.16), kind=kOutput, calls=%fused_computation.22 | convolution fusion | flops 1612972032 | bytes 2097160 | tf_op jit(solution)/shard_map/dot_general | solution.py:10
  133.7 1.8 fusion.57
  135.5 0.0 copy-done.6
  135.5 2.9 %fusion.2 = f32[512,512]{1,0:T(8,128)} fusion(f32[512,512]{1,0:T(8,128)S(1)} %fusion.57, f32[512,512]{1,0:T(8,128)S(1)} %copy-done.6, f32[]{:T(128)S(6)} %sqrt.16), kind=kOutput, calls=%fused_computation.14 | convolution fusion | flops 1612709888 | bytes 3145732 | tf_op jit(solution)/shard_map/dot_general | solution.py:10
  138.5 0.0 copy-done.2
  138.5 0.0 copy-done.3
  138.5 1.8 fusion.55
  140.3 0.9 multiply_reduce_fusion.1
  141.2 1.8 fusion.56
  143.1 72.8 %psum.7 = f32[]{:T(128)} all-reduce(f32[]{:T(128)} %multiply_reduce_fusion.1), channel_id=1, replica_groups=mesh['dp'=8,'shard'=32] {'dp','shard'}, use_global_device_ids=true, to_apply=%region_5.7 | all-reduce | flops 1 | bytes 8 | tf_op jit(solution)/shard_map/psum | solution.py:51
  217.3 3.1 %fusion.58 = f32[512,512]{1,0:T(8,128)S(1)} fusion(f32[512,512]{1,0:T(8,128)S(1)} %fusion.7, f32[512,512]{1,0:T(8,128)} %fusion.2), kind=kOutput, calls=%fused_computation.76 | convolution fusion | flops 1610612736 | bytes 3145728 | tf_op jit(solution)/shard_map/dot_general | solution.py:10
  220.4 2.6 multiply_reduce_fusion
  223.7 1.1 multiply_multiply_fusion
  224.8 6.7 %all-to-all-start.1 = ((f32[32,16,512]{2,1,0:T(8,128)}), f32[32,16,512]{2,1,0:T(8,128)S(1)}, u32[]{:S(2)}, u32[]{:S(2)}) async-start(f32[32,16,512]{2,1,0:T(8,128)} %bitcast.8), calls=%async_computation.2 | async-start | bytes 2097152 | tf_op jit(solution)/shard_map/all_to_all | solution.py:55
  231.5 0.7 fusion.33
  232.2 0.7 scatter_custom_fusion
  232.9 27.1 %all-to-all-done.1 = f32[32,16,512]{2,1,0:T(8,128)S(1)} async-done(((f32[32,16,512]{2,1,0:T(8,128)}), f32[32,16,512]{2,1,0:T(8,128)S(1)}, u32[]{:S(2)}, u32[]{:S(2)}) %all-to-all-start.1) | async-done | bytes 1048608 | tf_op jit(solution)/shard_map/all_to_all | solution.py:55
  260.0 0.6 gather_fusion.1
  260.7 1.1 broadcast_select_fusion
  (5 shorter events, 0.0 us)
Async XLA Ops:
  7.2 64.4 %reduce-scatter.2.cloned.1.call-start = ((), (), s32[]{:S(2)}) async-start(), calls=%async_computation.3 | async-start | bytes 9437184 | tf_op jit(solution)/shard_map/reduce_scatter | solution.py:48
  13.8 97.6 %copy-start = (f32[1,1,512,512]{3,2,1,0:T(8,128)S(1)}, f32[1,1,512,512]{3,2,1,0:T(8,128)}, u32[]{:S(2)}) copy-start(f32[1,1,512,512]{3,2,1,0:T(8,128)} %param.8) | copy-start | bytes 3145732
  114.1 10.4 %copy-start.1 = (f32[512,512]{1,0:T(8,128)}, f32[512,512]{1,0:T(8,128)S(1)}, u32[]{:S(2)}) copy-start(f32[512,512]{1,0:T(8,128)S(1)} %get-tuple-element.7) | copy-start | bytes 3145732
  116.8 7.6 %copy-start.4 = (f32[1,1,512,512]{3,2,1,0:T(8,128)S(1)}, f32[1,1,512,512]{3,2,1,0:T(8,128)}, u32[]{:S(2)}) copy-start(f32[1,1,512,512]{3,2,1,0:T(8,128)} %param.9) | copy-start | bytes 3145732
  127.2 1.0 copy-start.5
  130.4 5.2 %copy-start.6 = (f32[512,512]{1,0:T(8,128)S(1)}, f32[512,512]{1,0:T(8,128)}, u32[]{:S(2)}) copy-start(f32[512,512]{1,0:T(8,128)} %copy-done.5) | copy-start | bytes 3145732
  130.4 8.1 %copy-start.2 = (f32[512,512]{1,0:T(8,128)S(1)}, f32[512,512]{1,0:T(8,128)}, u32[]{:S(2)}) copy-start(f32[512,512]{1,0:T(8,128)} %fusion.9) | copy-start | bytes 3145732
  130.4 8.1 %copy-start.3 = (f32[512,512]{1,0:T(8,128)S(1)}, f32[512,512]{1,0:T(8,128)}, u32[]{:S(2)}) copy-start(f32[512,512]{1,0:T(8,128)} %fusion.1) | copy-start | bytes 3145732
  224.8 35.3 %all-to-all-start.1 = ((f32[32,16,512]{2,1,0:T(8,128)}), f32[32,16,512]{2,1,0:T(8,128)S(1)}, u32[]{:S(2)}, u32[]{:S(2)}) async-start(f32[32,16,512]{2,1,0:T(8,128)} %bitcast.8), calls=%async_computation.2 | async-start | bytes 2097152 | tf_op jit(solution)/shard_map/all_to_all | solution.py:55
Sparse Core Ops, SparseCore 0:
  14.0 57.5 reduce-scatter.1
where the time goes:
time: 269 us
  blocking collectives  111 us (41%)
  waiting for transfers between devices  84 us (31%)
  matrix products  34.6 us (13%)
  between operations  17.9 us (7%)
  other arithmetic  11.3 us (4%)
  starting transfers between devices  6.75 us (3%)
  local copies, waits for them, and re-layouts  3.34 us (1%)
    psum x1, blocking collectives, body(): total = lax.psum(jnp.sum(grad * grad), ('dp', 'shard'))  72.8 us
    reduce_scatter x1, waiting for transfers between devices, body(): lax.psum_scatter(local_part.astype(jnp.float32), 'dp', scatter_dimension=...  56.9 us
    all_to_all x1, blocking collectives, body(): lax.all_to_all(ordered, 'shard', split_axis=0, concat_axis=1, tiled=True)[0]  37.9 us
    dot_general x14, matrix products, product(): jnp.dot(left, right, precision=lax.Precision.HIGHEST, preferred_element_t...  34.6 us
    all_to_all x1, waiting for transfers between devices, body(): lax.all_to_all(scaled.reshape(shards, strip, width), 'shard', split_axis=...  27.1 us
    all_to_all x1, starting transfers between devices, body(): lax.all_to_all(scaled.reshape(shards, strip, width), 'shard', split_axis=...  6.72 us
    convert_element_type x1, other arithmetic, body(): local_part.astype(jnp.float32)  6.62 us
  transfers between devices with their start and end apart: 2, of which 2 were waited for; matrix products, arithmetic and copies ran while one was open for 1% of the time, Pallas kernels for 0%

commit v1 on v0

v1 whole, which is shorter than its diff:
```python
import jax
import jax.numpy as jnp
from jax import lax
from jax.experimental import pallas as pl
from jax.experimental.pallas import tpu as pltpu
from jax.sharding import PartitionSpec as P

LIMIT = 32700.0
STEPS = 128.0
K = 1.25**6
EPS = 1e-06
f32, bf16 = jnp.float32, jnp.bfloat16
VMEM = pl.BlockSpec(memory_space=pltpu.VMEM)
SMEM = pl.BlockSpec(memory_space=pltpu.SMEM)


def params(**more):
    return pltpu.CompilerParams(vmem_limit_bytes=48 << 20, **more)


def encode(strip):
    columns = [strip[:, c : c + 128] for c in range(0, strip.shape[1], 128)]
    top = columns[0]
    top = jnp.abs(top)
    for column in columns[1:]:
        top = jnp.maximum(top, jnp.abs(column))
    top = jnp.maximum(jnp.maximum(top[:8], top[8:]), 1e-30)
    code = jnp.ceil(jnp.log2(top) * STEPS)
    gain = jnp.exp2(code * (-1.0 / STEPS)) * LIMIT
    gain = jnp.concatenate([gain, gain], axis=0)
    coded = [jnp.round(column * gain).astype(jnp.int32) for column in columns]
    return coded, code.astype(jnp.int32)


def decode_gain(code):
    gain = jnp.exp2(code * (1.0 / STEPS)) * (1.0 / LIMIT)
    return jnp.concatenate([gain, gain], axis=0)


def encode_number(number):
    power = jnp.ceil(jnp.log2(jnp.maximum(number, 1e-30))) + 1.0
    digits = number * jnp.exp2(-power) * 16384.0
    high = jnp.floor(digits)
    low = jnp.floor((digits - high) * 16384.0)
    row = lax.broadcasted_iota(jnp.int32, number.shape, 0)
    return jnp.where(row == 0, power, jnp.where(row == 1, high, low)).astype(jnp.int32)


def decode_numbers(rows):
    power, high, low = rows[:, 0:1], rows[:, 1:2], rows[:, 2:3]
    return jnp.sum((high + low * (1.0 / 16384.0)) * (1.0 / 16384.0) * jnp.exp2(power), axis=0)


def split(matrix):
    high = matrix.astype(bf16)
    return high, (matrix - high.astype(f32)).astype(bf16)


def dot3(left, right, dims=((1,), (0,))):
    dims = (dims, ((), ()))
    lh, ll = left
    rh, rl = right
    out = lax.dot_general(lh, rl, dims, preferred_element_type=f32)
    out += lax.dot_general(ll, rh, dims, preferred_element_type=f32)
    return out + lax.dot_general(lh, rh, dims, preferred_element_type=f32)


def eye_like(matrix):
    row = lax.broadcasted_iota(jnp.int32, matrix.shape, 0)
    column = lax.broadcasted_iota(jnp.int32, matrix.shape, 1)
    return row == column


def inverse_root(stat):
    diagonal = eye_like(stat)
    shifted = stat + jnp.where(diagonal, EPS, 0.0)
    norm = jnp.sqrt(jnp.sum(shifted * shifted, keepdims=True))
    u = shifted * (0.2 / norm)
    us = split(u)
    u2 = dot3(us, us)
    u3 = dot3(split(u2), us)
    inner = jnp.where(diagonal, -10.0 * K, 0.0) + 10.0 * K * u - 5.0 * K * u2 + K * u3
    outer = jnp.where(diagonal, 1.5625, 0.0) - (1.5625 + K) * u + 5.0 * K * u2
    root = outer + dot3(split(u3), split(inner))
    return root * lax.rsqrt(jnp.sqrt(norm))


def invert(order_ref, slot_ref):
    def step(j, _):
        slot_ref[order_ref[j]] = j
        return 0

    lax.fori_loop(0, order_ref.shape[0], step, 0)


def sum_kernel(order_ref, parts_ref, out_ref, slot_ref, code_ref, square_ref):
    step, steps = pl.program_id(0), pl.num_programs(0)
    count = parts_ref.shape[1]

    @pl.when(step == 0)
    def _():
        invert(order_ref, slot_ref)
        square_ref[...] = jnp.zeros_like(square_ref)

    for b in range(count):
        strip = parts_ref[0, b].astype(f32)
        for i in range(1, parts_ref.shape[0]):
            strip += parts_ref[i, b].astype(f32)
        square = strip * strip
        for c in range(0, strip.shape[1], 128):
            square_ref[...] += square[:8, c : c + 128] + square[8:, c : c + 128]
        slot = slot_ref[step * count + b]
        coded, code = encode(strip)
        for c, column in enumerate(coded):
            out_ref[slot, 16 * c : 16 * c + 16, :] = column.astype(jnp.int16)
        code_ref[slot] = code

    @pl.when(step == steps - 1)
    def _():
        whole = jnp.broadcast_to(jnp.sum(square_ref[...], keepdims=True), square_ref.shape)
        number = encode_number(whole)
        for j in range(out_ref.shape[0]):
            tail = jnp.concatenate([code_ref[j], number], axis=0)
            out_ref[j, 64:80, :] = tail.astype(jnp.int16)


def left_kernel(coded_ref, stat_ref, high_ref, low_ref, stat_out, root_out, sums_ref, grad_ref):
    shards = coded_ref.shape[0]
    square = jnp.zeros((16, 128), f32)
    for j in range(shards):
        tail = coded_ref[j, 64:80, :].astype(jnp.int32).astype(f32)
        gain = decode_gain(tail[:8])
        for c in range(4):
            piece = coded_ref[j, 16 * c : 16 * c + 16, :].astype(jnp.int32).astype(f32) * gain
            square += piece * piece
            grad_ref[16 * j : 16 * j + 16, 128 * c : 128 * c + 128] = piece
    tails = jnp.stack([coded_ref[j, 64:80, :].astype(jnp.int32).astype(f32)[8:] for j in range(shards)])
    sums_ref[0:8] = jnp.broadcast_to(decode_numbers(tails), (8, 128))
    sums_ref[8:16] = jnp.broadcast_to(jnp.sum(square, keepdims=True), (8, 128))
    pair = split(grad_ref[...])
    high_ref[...], low_ref[...] = pair
    fresh = 0.95 * stat_ref[...] + dot3(pair, pair, ((1,), (1,))) * (1.0 / grad_ref.shape[0])
    stat_out[...] = fresh
    root_out[...] = inverse_root(fresh)


def right_kernel(high_ref, low_ref, stat_ref, stat_out, root_out):
    pair = (high_ref[...], low_ref[...])
    fresh = 0.95 * stat_ref[...] + dot3(pair, pair, ((0,), (0,))) * (1.0 / stat_ref.shape[0])
    stat_out[...] = fresh
    root_out[...] = inverse_root(fresh)


def shape_kernel(high_ref, low_ref, left_ref, right_ref, sums_ref, total_ref, out_ref, shaped_ref):
    order = high_ref.shape[0]
    half = dot3(split(left_ref[...]), (high_ref[...], low_ref[...]))
    shaped = dot3(split(half), split(right_ref[...]))
    cells = 1.0 / (order * order)
    mean = jnp.sum(shaped * shaped, keepdims=True) * cells
    graft = jnp.sqrt(sums_ref[8:9, 0:1] * cells + EPS) / jnp.sqrt(mean + EPS)
    shaped_ref[...] = shaped * graft
    number = encode_number(total_ref[...])
    for j in range(out_ref.shape[0]):
        coded, code = encode(shaped_ref[16 * j : 16 * j + 16, :])
        for c, column in enumerate(coded):
            out_ref[j, 16 * c : 16 * c + 16, :] = column.astype(jnp.int16)
        out_ref[j, 64:80, :] = jnp.concatenate([code, number], axis=0).astype(jnp.int16)


def update_kernel(groups, cells, order_ref, coded_ref, out_ref):
    tails = jnp.stack([coded_ref[j, 64:80, :].astype(jnp.int32).astype(f32)[8:] for j in range(groups)])
    layer = 1.0 / jnp.sqrt(decode_numbers(tails) * (1.0 / cells) + EPS)
    for j in range(coded_ref.shape[0]):
        slot = order_ref[j]
        tail = coded_ref[j, 64:80, :].astype(jnp.int32).astype(f32)
        gain = decode_gain(tail[:8]) * layer
        for c in range(4):
            piece = coded_ref[j, 16 * c : 16 * c + 16, :].astype(jnp.int32).astype(f32) * gain
            out_ref[slot, :, 128 * c : 128 * c + 128] = piece


def body(grads, owned, left_stat, right_stat):
    shards, groups = lax.axis_size("shard"), lax.axis_size("dp")
    group = lax.axis_index("dp")
    blocks, strip, width = grads.shape[1:]
    mine = lax.dynamic_index_in_dim(owned, group, 0, keepdims=False)
    square = jax.ShapeDtypeStruct((width, width), f32)
    halves = jax.ShapeDtypeStruct((width, width), bf16)
    wire = jax.ShapeDtypeStruct((shards, 80, 128), jnp.int16)

    parts = lax.all_to_all(grads[0], "dp", split_axis=0, concat_axis=0, tiled=True)
    parts = parts.reshape(groups, shards, strip, width)
    chunk = 8
    strips = pl.pallas_call(
        sum_kernel,
        grid=(shards // chunk,),
        in_specs=[SMEM, pl.BlockSpec((groups, chunk, strip, width), lambda i: (0, i, 0, 0))],
        out_specs=pl.BlockSpec((shards, 80, 128), lambda i: (0, 0, 0)),
        out_shape=wire,
        scratch_shapes=[
            pltpu.SMEM((shards,), jnp.int32),
            pltpu.VMEM((shards, 8, 128), jnp.int32),
            pltpu.VMEM((8, 128), f32),
        ],
        compiler_params=params(),
        name="sum_strips",
    )(mine, parts)
    strips = lax.all_to_all(strips, "shard", split_axis=0, concat_axis=0, tiled=True)
    high, low, left_fresh, left_root, sums = pl.pallas_call(
        left_kernel,
        in_specs=[VMEM, VMEM],
        out_specs=[VMEM] * 5,
        out_shape=[halves, halves, square, square, jax.ShapeDtypeStruct((16, 128), f32)],
        scratch_shapes=[pltpu.VMEM((width, width), f32)],
        compiler_params=params(),
        name="left",
    )(strips, left_stat[0, 0])
    pairs = [
        (((d + s) % groups) * shards + s, d * shards + s) for d in range(groups) for s in range(shards)
    ]
    total = lax.ppermute(sums[:8], ("dp", "shard"), pairs)
    right_fresh, right_root = pl.pallas_call(
        right_kernel,
        in_specs=[VMEM] * 3,
        out_specs=[VMEM] * 2,
        out_shape=[square, square],
        compiler_params=params(),
        cost_estimate=pl.CostEstimate(flops=10 * 2 * width**3, bytes_accessed=5 << 20, transcendentals=0),
        name="right",
    )(high, low, right_stat[0, 0])
    pieces = pl.pallas_call(
        shape_kernel,
        in_specs=[VMEM] * 6,
        out_specs=VMEM,
        out_shape=wire,
        scratch_shapes=[pltpu.VMEM((width, width), f32)],
        compiler_params=params(),
        name="shape",
    )(high, low, left_root, right_root, sums, total)
    pieces = lax.all_to_all(pieces, "shard", split_axis=0, concat_axis=0, tiled=True)
    update = pl.pallas_call(
        lambda *refs: update_kernel(groups, blocks * width * width, *refs),
        in_specs=[SMEM, VMEM],
        out_specs=VMEM,
        out_shape=jax.ShapeDtypeStruct((shards, strip, width), f32),
        compiler_params=params(),
        name="update",
    )(mine, pieces)
    return update, left_fresh[None, None], right_fresh[None, None]


def solution(mesh):
    return jax.shard_map(
        body,
        mesh=mesh,
        in_specs=(
            P("dp", None, "shard", None),
            P(),
            P("dp", "shard", None, None),
            P("dp", "shard", None, None),
        ),
        out_specs=(
            P("dp", "shard", None),
            P("dp", "shard", None, None),
            P("dp", "shard", None, None),
        ),
        check_vma=False,
    )
```

time: 269 us -> 131 us (0.49)
  blocking collectives: 111 us -> 57.8 us
  matrix products: 34.6 us -> 0 us
  waiting for transfers between devices: 84 us -> 49.6 us
  between operations: 17.9 us -> 0.74 us
  Pallas kernels: 0 us -> 16.3 us
  other arithmetic: 11.3 us -> 0 us
  local copies, waits for them, and re-layouts: 3.34 us -> 0.03 us
    psum x1 -> x0, blocking collectives: 72.8 us -> none  [body(): total = lax.psum(jnp.sum(grad * grad), ('dp', 'shard'))]
    reduce_scatter x1 -> x0, waiting for transfers between devices: 56.9 us -> none  [body(): lax.psum_scatter(local_part.astype(jnp.float32), 'dp', scatter_dimension=...]
    dot_general x14 -> x0, matrix products: 34.6 us -> none  [product(): jnp.dot(left, right, precision=lax.Precision.HIGHEST, preferred_element_t...]
    all_to_all x1, waiting for transfers between devices: 27.1 us -> 49.6 us  [body(): lax.all_to_all(grads[0], 'dp', split_axis=0, concat_axis=0, tiled=True)]
    all_to_all x1 -> x2, blocking collectives: 37.9 us -> 57.8 us  [the longest x1 31.2 us: body(): lax.all_to_all(strips, 'shard', split_axis=0, concat_axis=0, tiled=True)]
    pallas_call x0 -> x5, Pallas kernels: none -> 16.3 us  [the longest x1 4.33 us: body(): pl.pallas_call(left_kernel, in_specs=[VMEM, VMEM], out_specs=[VMEM] * 5,...]
    convert_element_type x1 -> x0, other arithmetic: 6.62 us -> none  [body(): local_part.astype(jnp.float32)]
  transfers between devices with their start and end apart: 2 -> 2, of which waited for: 2 -> 1; matrix products, arithmetic and copies ran while one was open for 1% -> 0% of each run, Pallas kernels for 0% -> 3%
where the time goes in v1:
time: 131 us
  blocking collectives  57.8 us (44%)
  waiting for transfers between devices  49.6 us (38%)
  Pallas kernels  16.3 us (12%)
  starting transfers between devices  6.48 us (5%)
    all_to_all x1, waiting for transfers between devices, body(): lax.all_to_all(grads[0], 'dp', split_axis=0, concat_axis=0, tiled=True)  49.6 us
    all_to_all x1, blocking collectives, body(): lax.all_to_all(strips, 'shard', split_axis=0, concat_axis=0, tiled=True)  31.2 us
    all_to_all x1, blocking collectives, body(): lax.all_to_all(pieces, 'shard', split_axis=0, concat_axis=0, tiled=True)  26.6 us
    all_to_all x1, starting transfers between devices, body(): lax.all_to_all(grads[0], 'dp', split_axis=0, concat_axis=0, tiled=True)  4.56 us
    pallas_call x1, Pallas kernels, body(): pl.pallas_call(left_kernel, in_specs=[VMEM, VMEM], out_specs=[VMEM] * 5,...  4.33 us
    pallas_call x1, Pallas kernels, body(): pl.pallas_call(right_kernel, in_specs=[VMEM] * 3, out_specs=[VMEM] * 2, o...  4.24 us
    pallas_call x1, Pallas kernels, body(): pl.pallas_call(sum_kernel, grid=(shards // chunk,), in_specs=[SMEM, pl.Bl...  3.7 us
  transfers between devices with their start and end apart: 2, of which 1 were waited for; matrix products, arithmetic and copies ran while one was open for 0% of the time, Pallas kernels for 3%

profile of v1, /device:TPU:32, one launch (start us, length us, event | category | flops | bytes accessed | tf_op | source)
XLA Modules:
  0.0 131.0 jit_solution(13181908062353638106)
XLA Ops:
  0.6 0.0 copy-start
  0.6 4.6 %all-to-all-start = ((bf16[256,16,512]{2,1,0:T(8,128)(2,1)}), bf16[256,16,512]{2,1,0:T(8,128)(2,1)}, u32[]{:S(2)}, u32[]{:S(2)}) async-start(bf16[256,16,512]{2,1,0:T(8,128)(2,1)} %bitcast.10), calls=%async_computation | async-start | bytes 8388608 | tf_op jit(solution)/shard_map/all_to_all | solution.py:191
  5.2 0.0 copy-start.1
  5.2 0.0 copy-start.2
  5.2 0.0 copy-done
  5.3 49.6 %all-to-all-done = bf16[256,16,512]{2,1,0:T(8,128)(2,1)} async-done(((bf16[256,16,512]{2,1,0:T(8,128)(2,1)}), bf16[256,16,512]{2,1,0:T(8,128)(2,1)}, u32[]{:S(2)}, u32[]{:S(2)}) %all-to-all-start) | async-done | bytes 4194336 | tf_op jit(solution)/shard_map/all_to_all | solution.py:191
  54.9 3.7 %sum_strips.1 = s16[32,80,128]{2,1,0:T(8,128)(2,1)S(1)} custom-call(s32[32]{0:T(128)S(1)} %dynamic-slice_bitcast_fusion.order_ref.refs_0_, bf16[8,32,16,512]{3,2,1,0:T(8,128)(2,1)} %bitcast.2.parts_ref), custom_call_target="tpu_custom_call" | custom-call | tf_op jit(solution)/shard_map/sum_strips/pallas_call | solution.py:194
  58.6 31.2 %all_to_all.15.coded_ref = s16[32,80,128]{2,1,0:T(8,128)(2,1)S(1)} all-to-all(s16[32,80,128]{2,1,0:T(8,128)(2,1)S(1)} %sum_strips.1), channel_id=1, replica_groups=mesh['dp'=8,'shard'=32] {'shard'}, dimensions={0} | all-to-all | bytes 1310720 | tf_op jit(solution)/shard_map/all_to_all | solution.py:208
  89.8 0.0 copy-done.1
  89.8 4.3 %left.1 = (bf16[512,512]{1,0:T(8,128)(2,1)S(1)}, bf16[512,512]{1,0:T(8,128)(2,1)S(1)}, f32[512,512]{1,0:T(8,128)}, f32[512,512]{1,0:T(8,128)S(1)}, f32[16,128]{1,0:T(8,128)S(1)}) custom-call(s16[32,80,128]{2,1,0:T(8,128)(2,1)S(1)} %all_to_all.15.coded_ref, f32[512,512]{1,0:T(8,128)S(1)} %bitcast.8), custom_call_target="tpu_custom_call" | custom-call | tf_op jit(solution)/shard_map/left/pallas_call | solution.py:209
  94.2 1.9 %collective-permute-start = (f32[8,128]{1,0:T(8,128)S(1)}, f32[8,128]{1,0:T(8,128)S(1)}, u32[]{:S(2)}, u32[]{:S(2)}) collective-permute-start(f32[8,128]{1,0:T(8,128)S(1)} %slice.3), channel_id=1, source_target_pairs={{0,0},{33,1},{66,2},{99,3},{132,4},{165,5},{198,6},{231,7},{8,8},{... | collective-permute-start | bytes 12296 | tf_op jit(solution)/shard_map/ppermute | solution.py:221
  96.1 0.0 copy-done.2
  96.1 4.2 %right.1 = (f32[512,512]{1,0:T(8,128)}, f32[512,512]{1,0:T(8,128)S(1)}) custom-call(bf16[512,512]{1,0:T(8,128)(2,1)S(1)} %get-tuple-element.10.high_ref, bf16[512,512]{1,0:T(8,128)(2,1)S(1)} %get-tuple-element.11.low_ref, f32[512,512]{1,0:T(8,128)S(1)} %bitcast.9), custom_call_target="tpu_custom_call" | custom-call | flops 2684354560 | bytes 5242880 | tf_op jit(solution)/shard_map/right/pallas_call | solution.py:222
  100.3 0.0 collective-permute-done.total_ref
  100.4 2.4 %shape.1 = s16[32,80,128]{2,1,0:T(8,128)(2,1)S(1)} custom-call(bf16[512,512]{1,0:T(8,128)(2,1)S(1)} %get-tuple-element.10.high_ref, bf16[512,512]{1,0:T(8,128)(2,1)S(1)} %get-tuple-element.11.low_ref, f32[512,512]{1,0:T(8,128)S(1)} %get-tuple-element.12.left_ref, f32[512,512]{1,0:T(8,128)S(1)} %get-tuple-element.13.right_ref, ...), custom_call_target="tpu_custom_call" | custom-call | tf_op jit(solution)/shard_map/shape/pallas_call | solution.py:231
  102.7 26.6 %all_to_all.16.refs_1_ = s16[32,80,128]{2,1,0:T(8,128)(2,1)S(1)} all-to-all(s16[32,80,128]{2,1,0:T(8,128)(2,1)S(1)} %shape.1), channel_id=1, replica_groups=mesh['dp'=8,'shard'=32] {'shard'}, dimensions={0} | all-to-all | bytes 1310720 | tf_op jit(solution)/shard_map/all_to_all | solution.py:240
  129.3 1.7 %update.1 = f32[32,16,512]{2,1,0:T(8,128)} custom-call(s32[32]{0:T(128)S(1)} %dynamic-slice_bitcast_fusion.order_ref.refs_0_, s16[32,80,128]{2,1,0:T(8,128)(2,1)S(1)} %all_to_all.16.refs_1_), custom_call_target="tpu_custom_call" | custom-call | tf_op jit(solution)/shard_map/update/pallas_call | solution.py:241
  (2 shorter events, 0.0 us)
Async XLA Ops:
  0.6 4.6 %copy-start = (s32[8,32]{1,0:T(8,128)S(1)}, s32[8,32]{1,0:T(8,128)}, u32[]{:S(2)}) copy-start(s32[8,32]{1,0:T(8,128)} %param.5) | copy-start | bytes 3076
  0.6 54.2 %all-to-all-start = ((bf16[256,16,512]{2,1,0:T(8,128)(2,1)}), bf16[256,16,512]{2,1,0:T(8,128)(2,1)}, u32[]{:S(2)}, u32[]{:S(2)}) async-start(bf16[256,16,512]{2,1,0:T(8,128)(2,1)} %bitcast.10), calls=%async_computation | async-start | bytes 8388608 | tf_op jit(solution)/shard_map/all_to_all | solution.py:191
  5.2 84.6 %copy-start.1 = (f32[1,1,512,512]{3,2,1,0:T(8,128)S(1)}, f32[1,1,512,512]{3,2,1,0:T(8,128)}, u32[]{:S(2)}) copy-start(f32[1,1,512,512]{3,2,1,0:T(8,128)} %param.6) | copy-start | bytes 3145732
  5.2 90.9 %copy-start.2 = (f32[1,1,512,512]{3,2,1,0:T(8,128)S(1)}, f32[1,1,512,512]{3,2,1,0:T(8,128)}, u32[]{:S(2)}) copy-start(f32[1,1,512,512]{3,2,1,0:T(8,128)} %param.7) | copy-start | bytes 3145732
  94.2 6.2 %collective-permute-start = (f32[8,128]{1,0:T(8,128)S(1)}, f32[8,128]{1,0:T(8,128)S(1)}, u32[]{:S(2)}, u32[]{:S(2)}) collective-permute-start(f32[8,128]{1,0:T(8,128)S(1)} %slice.3), channel_id=1, source_target_pairs={{0,0},{33,1},{66,2},{99,3},{132,4},{165,5},{198,6},{231,7},{8,8},{... | collective-permute-start | bytes 12296 | tf_op jit(solution)/shard_map/ppermute | solution.py:221

commit v2 on v1

--- a/solution.py
+++ b/solution.py
@@ -5,6 +5,7 @@
 from jax.experimental.pallas import tpu as pltpu
 from jax.sharding import PartitionSpec as P
 
+ROWS = 72
 LIMIT = 32700.0
 STEPS = 128.0
 K = 1.25**6
@@ -18,23 +19,46 @@
     return pltpu.CompilerParams(vmem_limit_bytes=48 << 20, **more)
 
 
-def encode(strip):
+def upper_rows():
+    return lax.broadcasted_iota(jnp.int32, (8, 128), 0) < 4
+
+
+def encode(strip, number=None):
     columns = [strip[:, c : c + 128] for c in range(0, strip.shape[1], 128)]
-    top = columns[0]
-    top = jnp.abs(top)
+    top = jnp.abs(columns[0])
     for column in columns[1:]:
         top = jnp.maximum(top, jnp.abs(column))
-    top = jnp.maximum(jnp.maximum(top[:8], top[8:]), 1e-30)
+    top = jnp.maximum(top[:8], top[8:])
+    top = jnp.maximum(jnp.maximum(top, pltpu.roll(top, 4, 0)), 1e-30)
     code = jnp.ceil(jnp.log2(top) * STEPS)
     gain = jnp.exp2(code * (-1.0 / STEPS)) * LIMIT
     gain = jnp.concatenate([gain, gain], axis=0)
-    coded = [jnp.round(column * gain).astype(jnp.int32) for column in columns]
-    return coded, code.astype(jnp.int32)
-
-
-def decode_gain(code):
+    coded = [jnp.round(column * gain) for column in columns]
+    tail = code if number is None else jnp.where(upper_rows(), code, number)
+    return jnp.concatenate(coded + [tail], axis=0).astype(jnp.int32)
+
+
+def decode_gain(tail):
+    code = jnp.where(upper_rows(), tail, pltpu.roll(tail, 4, 0))
     gain = jnp.exp2(code * (1.0 / STEPS)) * (1.0 / LIMIT)
     return jnp.concatenate([gain, gain], axis=0)
+
+
+def decode(coded, factor=None):
+    gain = decode_gain(coded[64:])
+    if factor is not None:
+        gain = gain * factor
+    return [coded[r : r + 16] * gain for r in range(0, 64, 16)]
+
+
+def load(ref, pair):
+    both = ref[2 * ROWS * pair : 2 * ROWS * (pair + 1), :].astype(jnp.int32).astype(f32)
+    return both[:ROWS], both[ROWS:]
+
+
+def store(ref, pair, first, second):
+    both = jnp.concatenate([first, second], axis=0)
+    ref[2 * ROWS * pair : 2 * ROWS * (pair + 1), :] = both.astype(jnp.int16)
 
 
 def encode_number(number):
@@ -43,12 +67,12 @@
     high = jnp.floor(digits)
     low = jnp.floor((digits - high) * 16384.0)
     row = lax.broadcasted_iota(jnp.int32, number.shape, 0)
-    return jnp.where(row == 0, power, jnp.where(row == 1, high, low)).astype(jnp.int32)
-
-
-def decode_numbers(rows):
-    power, high, low = rows[:, 0:1], rows[:, 1:2], rows[:, 2:3]
-    return jnp.sum((high + low * (1.0 / 16384.0)) * (1.0 / 16384.0) * jnp.exp2(power), axis=0)
+    return jnp.where(row == 4, power, jnp.where(row == 5, high, low))
+
+
+def decode_number(tail):
+    power, high, low = tail[4:5], tail[5:6], tail[6:7]
+    return (high + low * (1.0 / 16384.0)) * (1.0 / 16384.0) * jnp.exp2(power)
 
 
 def split(matrix):
@@ -93,49 +117,62 @@
     lax.fori_loop(0, order_ref.shape[0], step, 0)
 
 
-def sum_kernel(order_ref, parts_ref, out_ref, slot_ref, code_ref, square_ref):
+def pair_kernel(pick_ref, own_ref, other_ref, out_ref):
+    for p in range(other_ref.shape[0] // 2):
+        coded = [encode(own_ref[0, b].astype(f32) + other_ref[b].astype(f32)) for b in (2 * p, 2 * p + 1)]
+        store(out_ref, p, *coded)
+
+
+def sum_kernel(pick_ref, order_ref, own_ref, other_ref, *refs):
+    part_refs, (out_ref, slot_ref, coded_ref, square_ref) = refs[:-4], refs[-4:]
     step, steps = pl.program_id(0), pl.num_programs(0)
-    count = parts_ref.shape[1]
+    count = other_ref.shape[0]
 
     @pl.when(step == 0)
     def _():
         invert(order_ref, slot_ref)
         square_ref[...] = jnp.zeros_like(square_ref)
 
-    for b in range(count):
-        strip = parts_ref[0, b].astype(f32)
-        for i in range(1, parts_ref.shape[0]):
-            strip += parts_ref[i, b].astype(f32)
-        square = strip * strip
-        for c in range(0, strip.shape[1], 128):
-            square_ref[...] += square[:8, c : c + 128] + square[8:, c : c + 128]
-        slot = slot_ref[step * count + b]
-        coded, code = encode(strip)
-        for c, column in enumerate(coded):
-            out_ref[slot, 16 * c : 16 * c + 16, :] = column.astype(jnp.int16)
-        code_ref[slot] = code
+    total = jnp.zeros((8, 128), f32)
+    for p in range(count // 2):
+        parts = [load(ref, p) for ref in part_refs]
+        for i in range(2):
+            b = 2 * p + i
+            strip = own_ref[0, b].astype(f32) + other_ref[b].astype(f32)
+            pieces = [decode(part[i]) for part in parts]
+            columns = [
+                strip[:, 128 * c : 128 * c + 128] + sum(piece[c] for piece in pieces[1:]) + pieces[0][c]
+                for c in range(4)
+            ]
+            for column in columns:
+                square = column * column
+                total += square[:8] + square[8:]
+            coded_ref[slot_ref[step * count + b]] = encode(jnp.concatenate(columns, axis=1))
+    square_ref[...] += total
 
     @pl.when(step == steps - 1)
     def _():
         whole = jnp.broadcast_to(jnp.sum(square_ref[...], keepdims=True), square_ref.shape)
-        number = encode_number(whole)
-        for j in range(out_ref.shape[0]):
-            tail = jnp.concatenate([code_ref[j], number], axis=0)
-            out_ref[j, 64:80, :] = tail.astype(jnp.int16)
+        number = encode_number(whole).astype(jnp.int32)
+        for p in range(coded_ref.shape[0] // 2):
+            both = []
+            for j in (2 * p, 2 * p + 1):
+                tail = jnp.where(upper_rows(), coded_ref[j, 64:72, :], number)
+                both.append(jnp.concatenate([coded_ref[j, 0:64, :], tail], axis=0))
+            store(out_ref, p, *both)
 
 
 def left_kernel(coded_ref, stat_ref, high_ref, low_ref, stat_out, root_out, sums_ref, grad_ref):
-    shards = coded_ref.shape[0]
     square = jnp.zeros((16, 128), f32)
-    for j in range(shards):
-        tail = coded_ref[j, 64:80, :].astype(jnp.int32).astype(f32)
-        gain = decode_gain(tail[:8])
-        for c in range(4):
-            piece = coded_ref[j, 16 * c : 16 * c + 16, :].astype(jnp.int32).astype(f32) * gain
-            square += piece * piece
-            grad_ref[16 * j : 16 * j + 16, 128 * c : 128 * c + 128] = piece
-    tails = jnp.stack([coded_ref[j, 64:80, :].astype(jnp.int32).astype(f32)[8:] for j in range(shards)])
-    sums_ref[0:8] = jnp.broadcast_to(decode_numbers(tails), (8, 128))
+    group = jnp.zeros((1, 128), f32)
+    for p in range(coded_ref.shape[0] // (2 * ROWS)):
+        for i, coded in enumerate(load(coded_ref, p)):
+            row = 16 * (2 * p + i)
+            group += decode_number(coded[64:])
+            for c, piece in enumerate(decode(coded)):
+                square += piece * piece
+                grad_ref[row : row + 16, 128 * c : 128 * c + 128] = piece
+    sums_ref[0:8] = jnp.broadcast_to(group, (8, 128))
     sums_ref[8:16] = jnp.broadcast_to(jnp.sum(square, keepdims=True), (8, 128))
     pair = split(grad_ref[...])
     high_ref[...], low_ref[...] = pair
@@ -160,51 +197,84 @@
     graft = jnp.sqrt(sums_ref[8:9, 0:1] * cells + EPS) / jnp.sqrt(mean + EPS)
     shaped_ref[...] = shaped * graft
     number = encode_number(total_ref[...])
-    for j in range(out_ref.shape[0]):
-        coded, code = encode(shaped_ref[16 * j : 16 * j + 16, :])
-        for c, column in enumerate(coded):
-            out_ref[j, 16 * c : 16 * c + 16, :] = column.astype(jnp.int16)
-        out_ref[j, 64:80, :] = jnp.concatenate([code, number], axis=0).astype(jnp.int16)
+    for p in range(order // 32):
+        rows = 32 * p
+        store(
+            out_ref,
+            p,
+            encode(shaped_ref[rows : rows + 16, :], number),
+            encode(shaped_ref[rows + 16 : rows + 32, :], number),
+        )
 
 
 def update_kernel(groups, cells, order_ref, coded_ref, out_ref):
-    tails = jnp.stack([coded_ref[j, 64:80, :].astype(jnp.int32).astype(f32)[8:] for j in range(groups)])
-    layer = 1.0 / jnp.sqrt(decode_numbers(tails) * (1.0 / cells) + EPS)
-    for j in range(coded_ref.shape[0]):
-        slot = order_ref[j]
-        tail = coded_ref[j, 64:80, :].astype(jnp.int32).astype(f32)
-        gain = decode_gain(tail[:8]) * layer
-        for c in range(4):
-            piece = coded_ref[j, 16 * c : 16 * c + 16, :].astype(jnp.int32).astype(f32) * gain
-            out_ref[slot, :, 128 * c : 128 * c + 128] = piece
+    total = jnp.zeros((1, 128), f32)
+    for p in range(groups // 2):
+        for coded in load(coded_ref, p):
+            total += decode_number(coded[64:])
+    layer = 1.0 / jnp.sqrt(total * (1.0 / cells) + EPS)
+    for p in range(out_ref.shape[0] // 2):
+        for i, coded in enumerate(load(coded_ref, p)):
+            slot = order_ref[2 * p + i]
+            for c, piece in enumerate(decode(coded, layer)):
+                out_ref[slot, :, 128 * c : 128 * c + 128] = piece
 
 
 def body(grads, owned, left_stat, right_stat):
     shards, groups = lax.axis_size("shard"), lax.axis_size("dp")
     group = lax.axis_index("dp")
     blocks, strip, width = grads.shape[1:]
+    core, chip, chips = group % 2, group // 2, groups // 2
     mine = lax.dynamic_index_in_dim(owned, group, 0, keepdims=False)
     square = jax.ShapeDtypeStruct((width, width), f32)
     halves = jax.ShapeDtypeStruct((width, width), bf16)
-    wire = jax.ShapeDtypeStruct((shards, 80, 128), jnp.int16)
-
-    parts = lax.all_to_all(grads[0], "dp", split_axis=0, concat_axis=0, tiled=True)
-    parts = parts.reshape(groups, shards, strip, width)
+    wire = jax.ShapeDtypeStruct((shards * ROWS, 128), jnp.int16)
+    grouped = grads[0].reshape(groups, shards, strip, width)
+    swap = [(d, d ^ 1) for d in range(groups)]
     chunk = 8
+    own_block = pl.BlockSpec((1, chunk, strip, width), lambda i, pick, *_: (pick[0], i, 0, 0))
+    other_block = pl.BlockSpec((chunk, strip, width), lambda i, *_: (i, 0, 0))
+    wire_block = pl.BlockSpec((chunk * ROWS, 128), lambda i, *_: (i, 0))
+
+    received = []
+    for ahead in (2, 1, 3, 0):
+        target = 2 * ((chip + ahead) % chips)
+        other = lax.dynamic_index_in_dim(grouped, target + 1 - core, 0, keepdims=False)
+        other = lax.ppermute(other, "dp", swap)
+        pick = (target + core).reshape(1)
+        if ahead == 0:
+            break
+        sums = pl.pallas_call(
+            pair_kernel,
+            grid_spec=pltpu.PrefetchScalarGridSpec(
+                num_scalar_prefetch=1,
+                grid=(shards // chunk,),
+                in_specs=[own_block, other_block],
+                out_specs=wire_block,
+            ),
+            out_shape=wire,
+            compiler_params=params(),
+            name=f"pair_{ahead}",
+        )(pick, grouped, other)
+        along = [(d, (d + 2 * ahead) % groups) for d in range(groups)]
+        received.append(lax.ppermute(sums, "dp", along))
     strips = pl.pallas_call(
         sum_kernel,
-        grid=(shards // chunk,),
-        in_specs=[SMEM, pl.BlockSpec((groups, chunk, strip, width), lambda i: (0, i, 0, 0))],
-        out_specs=pl.BlockSpec((shards, 80, 128), lambda i: (0, 0, 0)),
+        grid_spec=pltpu.PrefetchScalarGridSpec(
+            num_scalar_prefetch=2,
+            grid=(shards // chunk,),
+            in_specs=[own_block, other_block] + [wire_block] * len(received),
+            out_specs=pl.BlockSpec((shards * ROWS, 128), lambda i, *_: (0, 0)),
+            scratch_shapes=[
+                pltpu.SMEM((shards,), jnp.int32),
+                pltpu.VMEM((shards, ROWS, 128), jnp.int32),
+                pltpu.VMEM((8, 128), f32),
+            ],
+        ),
         out_shape=wire,
-        scratch_shapes=[
-            pltpu.SMEM((shards,), jnp.int32),
-            pltpu.VMEM((shards, 8, 128), jnp.int32),
-            pltpu.VMEM((8, 128), f32),
-        ],
         compiler_params=params(),
         name="sum_strips",
-    )(mine, parts)
+    )(pick, mine, grouped, other, *received)
     strips = lax.all_to_all(strips, "shard", split_axis=0, concat_axis=0, tiled=True)
     high, low, left_fresh, left_root, sums = pl.pallas_call(
         left_kernel,

time: 131 us -> 113 us (0.86)
  waiting for transfers between devices: 49.6 us -> 22.8 us
  local copies, waits for them, and re-layouts: 0.03 us -> 4.95 us
  starting transfers between devices: 6.48 us -> 9.07 us
  Pallas kernels: 16.3 us -> 18.6 us
    all_to_all x1 -> x0, waiting for transfers between devices: 49.6 us -> none  [body(): lax.all_to_all(grads[0], 'dp', split_axis=0, concat_axis=0, tiled=True)]
    ppermute x0 -> x7, waiting for transfers between devices: none -> 22.8 us  [the longest x3 19.2 us: body(): received.append(lax.ppermute(sums, 'dp', along))]
    ppermute x0 -> x7, starting transfers between devices: none -> 6.94 us  [the longest x3 6.42 us: body(): received.append(lax.ppermute(sums, 'dp', along))]
    all_to_all x1 -> x0, starting transfers between devices: 4.56 us -> none  [body(): lax.all_to_all(grads[0], 'dp', split_axis=0, concat_axis=0, tiled=True)]
    squeeze x0 -> x1, local copies, waits for them, and re-layouts: none -> 2.74 us  [body(): lax.dynamic_index_in_dim(grouped, target + 1 - core, 0, keepdims=False)]
    pallas_call x1 -> x4, Pallas kernels: 3.7 us -> 5.9 us  [the longest x1 3.57 us: body(): pl.pallas_call(sum_kernel, grid_spec=pltpu.PrefetchScalarGridSpec(num_sca...]
    unnamed x6 -> x8, local copies, waits for them, and re-layouts: 0.02 us -> 2.2 us
  transfers between devices with their start and end apart: 2 -> 8, of which waited for: 1 -> 5; matrix products, arithmetic and copies ran while one was open for 0% -> 0% of each run, Pallas kernels for 3% -> 6%
where the time goes in v2:
time: 113 us
  blocking collectives  56.8 us (50%)
  waiting for transfers between devices  22.8 us (20%)
  Pallas kernels  18.6 us (16%)
  starting transfers between devices  9.07 us (8%)
  local copies, waits for them, and re-layouts  4.95 us (4%)
    all_to_all x1, blocking collectives, body(): lax.all_to_all(strips, 'shard', split_axis=0, concat_axis=0, tiled=True)  30.1 us
    all_to_all x1, blocking collectives, body(): lax.all_to_all(pieces, 'shard', split_axis=0, concat_axis=0, tiled=True)  26.6 us
    ppermute x3, waiting for transfers between devices, body(): received.append(lax.ppermute(sums, 'dp', along))  19.2 us
    ppermute x3, starting transfers between devices, body(): received.append(lax.ppermute(sums, 'dp', along))  6.42 us
    pallas_call x1, Pallas kernels, body(): pl.pallas_call(left_kernel, in_specs=[VMEM, VMEM], out_specs=[VMEM] * 5,...  4.37 us
    pallas_call x1, Pallas kernels, body(): pl.pallas_call(right_kernel, in_specs=[VMEM] * 3, out_specs=[VMEM] * 2, o...  4.27 us
    ppermute x4, waiting for transfers between devices, body(): other = lax.ppermute(other, 'dp', swap)  3.64 us
    pallas_call x1, Pallas kernels, body(): pl.pallas_call(sum_kernel, grid_spec=pltpu.PrefetchScalarGridSpec(num_sca...  3.57 us
  transfers between devices with their start and end apart: 8, of which 5 were waited for; matrix products, arithmetic and copies ran while one was open for 0% of the time, Pallas kernels for 6%

profile of v2, /device:TPU:32, one launch (start us, length us, event | category | flops | bytes accessed | tf_op | source)
XLA Modules:
  0.0 113.0 jit_solution(3345703640221580572)
XLA Ops:
  0.6 0.0 copy-start
  0.8 2.7 %dynamic-slice_bitcast_fusion = (bf16[32,16,512]{2,1,0:T(8,128)(2,1)}, bf16[32,16,512]{2,1,0:T(8,128)(2,1)S(1)}, bf16[32,16,512]{2,1,0:T(8,128)(2,1)S(1)}, bf16[32,16,512]{2,1,0:T(8,128)(2,1)}) fusion(bf16[8,32,16,512]{3,2,1,0:T(8,128)(2,1)} %bitcast.23, s32[]{:T(128)S(6)} %select_n.54, s32[]{:T(128)S(6)} %select_n.52, s32[]{:T(128)S(6)} %select_n.50, ...), kind=kLoop, calls=%fused_computation | loop fusion | bytes 4194320 | tf_op jit(solution)/shard_map/jit(dynamic_index_in_dim)/squeeze | solution.py:242
  3.5 0.0 collective-permute-start.1
  3.5 0.5 collective-permute-start.3
  4.0 0.0 collective-permute-start.5
  4.0 1.4 %collective-permute-done.1.other_ref = bf16[32,16,512]{2,1,0:T(8,128)(2,1)S(1)} collective-permute-done((bf16[32,16,512]{2,1,0:T(8,128)(2,1)S(1)}, bf16[32,16,512]{2,1,0:T(8,128)(2,1)S(1)}, u32[]{:S(2)}, u32[]{:S(2)}) %collective-permute-start.1) | collective-permute-done | bytes 524320 | tf_op jit(solution)/shard_map/ppermute | solution.py:243
  5.4 0.0 copy-start.1
  5.4 2.2 %copy-done.1 = bf16[1,256,16,512]{3,2,1,0:T(8,128)(2,1)S(1)} copy-done((bf16[1,256,16,512]{3,2,1,0:T(8,128)(2,1)S(1)}, bf16[1,256,16,512]{3,2,1,0:T(8,128)(2,1)}, u32[]{:S(2)}) %copy-start.1) | copy-done | bytes 4194328
  7.6 0.4 pair_2.1
  8.0 3.1 %collective-permute-start.2 = (s16[2304,128]{1,0:T(8,128)(2,1)S(1)}, s16[2304,128]{1,0:T(8,128)(2,1)S(1)}, u32[]{:S(2)}, u32[]{:S(2)}) collective-permute-start(s16[2304,128]{1,0:T(8,128)(2,1)S(1)} %pair_2.1), channel_id=1, source_target_pairs={{0,128},{32,160},{64,192},{96,224},{128,0},{160,32},{192,64},{224,... | collective-permute-start | bytes 1769480 | tf_op jit(solution)/shard_map/ppermute | solution.py:260
  11.1 0.0 collective-permute-done.3.other_ref
  11.1 0.4 pair_1.1
  11.5 0.7 collective-permute-start.4
  12.1 0.0 collective-permute-done.5.other_ref
  12.1 1.6 %pair_3.1 = s16[2304,128]{1,0:T(8,128)(2,1)} custom-call(s32[1]{0:T(128)} %bitcast.8.pick_ref, bf16[8,32,16,512]{3,2,1,0:T(8,128)(2,1)S(1)} %bitcast.27, bf16[32,16,512]{2,1,0:T(8,128)(2,1)S(1)} %collective-permute-done.5.other_ref), custom_call_target="tpu_custom_call" | custom-call | tf_op jit(solution)/shard_map/pair_3/pallas_call | solution.py:247
  13.7 0.0 copy-start.2
  13.7 2.6 %collective-permute-start.6 = (s16[2304,128]{1,0:T(8,128)(2,1)}, s16[2304,128]{1,0:T(8,128)(2,1)}, u32[]{:S(2)}, u32[]{:S(2)}) collective-permute-start(s16[2304,128]{1,0:T(8,128)(2,1)} %pair_3.1), channel_id=1, source_target_pairs={{0,192},{32,224},{64,0},{96,32},{128,64},{160,96},{192,128},{224,1... | collective-permute-start | bytes 1769480 | tf_op jit(solution)/shard_map/ppermute | solution.py:260
  16.4 0.0 collective-permute-start
  16.4 0.0 copy-done
  16.4 2.2 %collective-permute-done.other_ref = bf16[32,16,512]{2,1,0:T(8,128)(2,1)} collective-permute-done((bf16[32,16,512]{2,1,0:T(8,128)(2,1)}, bf16[32,16,512]{2,1,0:T(8,128)(2,1)}, u32[]{:S(2)}, u32[]{:S(2)}) %collective-permute-start) | collective-permute-done | bytes 524320 | tf_op jit(solution)/shard_map/ppermute | solution.py:243
  18.6 7.1 %collective-permute-done.2.refs_0_ = s16[2304,128]{1,0:T(8,128)(2,1)S(1)} collective-permute-done((s16[2304,128]{1,0:T(8,128)(2,1)S(1)}, s16[2304,128]{1,0:T(8,128)(2,1)S(1)}, u32[]{:S(2)}, u32[]{:S(2)}) %collective-permute-start.2) | collective-permute-done | bytes 589856 | tf_op jit(solution)/shard_map/ppermute | solution.py:260
  25.8 11.8 %collective-permute-done.4.refs_1_ = s16[2304,128]{1,0:T(8,128)(2,1)S(1)} collective-permute-done((s16[2304,128]{1,0:T(8,128)(2,1)S(1)}, s16[2304,128]{1,0:T(8,128)(2,1)S(1)}, u32[]{:S(2)}, u32[]{:S(2)}) %collective-permute-start.4) | collective-permute-done | bytes 589856 | tf_op jit(solution)/shard_map/ppermute | solution.py:260
  37.6 0.2 collective-permute-done.6.refs_2_
  37.8 0.0 copy-start.3
  37.8 3.6 %sum_strips.1 = s16[2304,128]{1,0:T(8,128)(2,1)S(1)} custom-call(s32[1]{0:T(128)} %bitcast.1.pick_ref, s32[32]{0:T(128)S(1)} %fusion.order_ref.refs_0_, bf16[8,32,16,512]{3,2,1,0:T(8,128)(2,1)} %bitcast.24, bf16[32,16,512]{2,1,0:T(8,128)(2,1)} %collective-permute-done.other_ref, s16[2304,128]{1,0:T(8,128)(2,1)S(1)} %collective-permute-done.2.refs_0_, ...), custom_call_target="tpu_custom_call" | custom-call | tf_op jit(solution)/shard_map/sum_strips/pallas_call | solution.py:261
  41.4 30.1 %all_to_all.22 = s16[32,72,128]{2,1,0:T(8,128)(2,1)S(1)} all-to-all(s16[32,72,128]{2,1,0:T(8,128)(2,1)S(1)} %bitcast.31), channel_id=1, replica_groups=mesh['dp'=8,'shard'=32] {'shard'}, dimensions={0} | all-to-all | bytes 1179648 | tf_op jit(solution)/shard_map/all_to_all | solution.py:278
  71.5 0.0 copy-done.2
  71.5 4.4 %left.1 = (bf16[512,512]{1,0:T(8,128)(2,1)S(1)}, bf16[512,512]{1,0:T(8,128)(2,1)S(1)}, f32[512,512]{1,0:T(8,128)}, f32[512,512]{1,0:T(8,128)S(1)}, f32[16,128]{1,0:T(8,128)S(1)}) custom-call(s16[2304,128]{1,0:T(8,128)(2,1)S(1)} %bitcast.28, f32[512,512]{1,0:T(8,128)S(1)} %bitcast.32), custom_call_target="tpu_custom_call" | custom-call | tf_op jit(solution)/shard_map/left/pallas_call | solution.py:279
  75.9 2.1 %collective-permute-start.7 = (f32[8,128]{1,0:T(8,128)S(1)}, f32[8,128]{1,0:T(8,128)S(1)}, u32[]{:S(2)}, u32[]{:S(2)}) collective-permute-start(f32[8,128]{1,0:T(8,128)S(1)} %slice.3), channel_id=1, source_target_pairs={{0,0},{33,1},{66,2},{99,3},{132,4},{165,5},{198,6},{231,7},{8,8},{... | collective-permute-start | bytes 12296 | tf_op jit(solution)/shard_map/ppermute | solution.py:291
  78.0 0.0 copy-done.3
  78.1 4.3 %right.1 = (f32[512,512]{1,0:T(8,128)}, f32[512,512]{1,0:T(8,128)S(1)}) custom-call(bf16[512,512]{1,0:T(8,128)(2,1)S(1)} %get-tuple-element.10.high_ref, bf16[512,512]{1,0:T(8,128)(2,1)S(1)} %get-tuple-element.11.low_ref, f32[512,512]{1,0:T(8,128)S(1)} %bitcast.33), custom_call_target="tpu_custom_call" | custom-call | flops 2684354560 | bytes 5242880 | tf_op jit(solution)/shard_map/right/pallas_call | solution.py:292
  82.3 0.0 collective-permute-done.7.total_ref
  82.3 2.4 %shape.1 = s16[2304,128]{1,0:T(8,128)(2,1)S(1)} custom-call(bf16[512,512]{1,0:T(8,128)(2,1)S(1)} %get-tuple-element.10.high_ref, bf16[512,512]{1,0:T(8,128)(2,1)S(1)} %get-tuple-element.11.low_ref, f32[512,512]{1,0:T(8,128)S(1)} %get-tuple-element.12.left_ref, f32[512,512]{1,0:T(8,128)S(1)} %get-tuple-element.13.right_ref, ...), custom_call_target="tpu_custom_call" | custom-call | tf_op jit(solution)/shard_map/shape/pallas_call | solution.py:301
  84.7 26.6 %all_to_all.23 = s16[32,72,128]{2,1,0:T(8,128)(2,1)S(1)} all-to-all(s16[32,72,128]{2,1,0:T(8,128)(2,1)S(1)} %bitcast.30), channel_id=1, replica_groups=mesh['dp'=8,'shard'=32] {'shard'}, dimensions={0} | all-to-all | bytes 1179648 | tf_op jit(solution)/shard_map/all_to_all | solution.py:310
  111.4 1.7 %update.1 = f32[32,16,512]{2,1,0:T(8,128)} custom-call(s32[32]{0:T(128)S(1)} %fusion.order_ref.refs_0_, s16[2304,128]{1,0:T(8,128)(2,1)S(1)} %bitcast.29), custom_call_target="tpu_custom_call" | custom-call | tf_op jit(solution)/shard_map/update/pallas_call | solution.py:311
  (2 shorter events, 0.0 us)
Async XLA Ops:
  0.6 15.8 %copy-start = (s32[8,32]{1,0:T(8,128)S(1)}, s32[8,32]{1,0:T(8,128)}, u32[]{:S(2)}) copy-start(s32[8,32]{1,0:T(8,128)} %param.5) | copy-start | bytes 3076
  3.5 1.9 %collective-permute-start.1 = (bf16[32,16,512]{2,1,0:T(8,128)(2,1)S(1)}, bf16[32,16,512]{2,1,0:T(8,128)(2,1)S(1)}, u32[]{:S(2)}, u32[]{:S(2)}) collective-permute-start(bf16[32,16,512]{2,1,0:T(8,128)(2,1)S(1)} %get-tuple-element.19), channel_id=1, source_target_pairs={{0,32},{32,0},{64,96},{96,64},{128,160},{160,128},{192,224},{224,1... | collective-permute-start | bytes 1572872 | tf_op jit(solution)/shard_map/ppermute | solution.py:243
  3.5 7.6 %collective-permute-start.3 = (bf16[32,16,512]{2,1,0:T(8,128)(2,1)S(1)}, bf16[32,16,512]{2,1,0:T(8,128)(2,1)S(1)}, u32[]{:S(2)}, u32[]{:S(2)}) collective-permute-start(bf16[32,16,512]{2,1,0:T(8,128)(2,1)S(1)} %get-tuple-element.18), channel_id=1, source_target_pairs={{0,32},{32,0},{64,96},{96,64},{128,160},{160,128},{192,224},{224,1... | collective-permute-start | bytes 1572872 | tf_op jit(solution)/shard_map/ppermute | solution.py:243
  4.0 8.1 %collective-permute-start.5 = (bf16[32,16,512]{2,1,0:T(8,128)(2,1)}, bf16[32,16,512]{2,1,0:T(8,128)(2,1)S(1)}, u32[]{:S(2)}, u32[]{:S(2)}) collective-permute-start(bf16[32,16,512]{2,1,0:T(8,128)(2,1)} %get-tuple-element.17), channel_id=1, source_target_pairs={{0,32},{32,0},{64,96},{96,64},{128,160},{160,128},{192,224},{224,1... | collective-permute-start | bytes 1572872 | tf_op jit(solution)/shard_map/ppermute | solution.py:243
  5.4 2.2 %copy-start.1 = (bf16[1,256,16,512]{3,2,1,0:T(8,128)(2,1)S(1)}, bf16[1,256,16,512]{3,2,1,0:T(8,128)(2,1)}, u32[]{:S(2)}) copy-start(bf16[1,256,16,512]{3,2,1,0:T(8,128)(2,1)} %param.4) | copy-start | bytes 12582916
  8.0 17.8 %collective-permute-start.2 = (s16[2304,128]{1,0:T(8,128)(2,1)S(1)}, s16[2304,128]{1,0:T(8,128)(2,1)S(1)}, u32[]{:S(2)}, u32[]{:S(2)}) collective-permute-start(s16[2304,128]{1,0:T(8,128)(2,1)S(1)} %pair_2.1), channel_id=1, source_target_pairs={{0,128},{32,160},{64,192},{96,224},{128,0},{160,32},{192,64},{224,... | collective-permute-start | bytes 1769480 | tf_op jit(solution)/shard_map/ppermute | solution.py:260
  11.5 26.1 %collective-permute-start.4 = (s16[2304,128]{1,0:T(8,128)(2,1)S(1)}, s16[2304,128]{1,0:T(8,128)(2,1)S(1)}, u32[]{:S(2)}, u32[]{:S(2)}) collective-permute-start(s16[2304,128]{1,0:T(8,128)(2,1)S(1)} %pair_1.1), channel_id=1, source_target_pairs={{0,64},{32,96},{64,128},{96,160},{128,192},{160,224},{192,0},{224,... | collective-permute-start | bytes 1769480 | tf_op jit(solution)/shard_map/ppermute | solution.py:260
  13.7 57.8 %copy-start.2 = (f32[1,1,512,512]{3,2,1,0:T(8,128)S(1)}, f32[1,1,512,512]{3,2,1,0:T(8,128)}, u32[]{:S(2)}) copy-start(f32[1,1,512,512]{3,2,1,0:T(8,128)} %param.6) | copy-start | bytes 3145732
  13.7 24.1 %collective-permute-start.6 = (s16[2304,128]{1,0:T(8,128)(2,1)}, s16[2304,128]{1,0:T(8,128)(2,1)}, u32[]{:S(2)}, u32[]{:S(2)}) collective-permute-start(s16[2304,128]{1,0:T(8,128)(2,1)} %pair_3.1), channel_id=1, source_target_pairs={{0,192},{32,224},{64,0},{96,32},{128,64},{160,96},{192,128},{224,1... | collective-permute-start | bytes 1769480 | tf_op jit(solution)/shard_map/ppermute | solution.py:260
  16.4 2.3 %collective-permute-start = (bf16[32,16,512]{2,1,0:T(8,128)(2,1)}, bf16[32,16,512]{2,1,0:T(8,128)(2,1)}, u32[]{:S(2)}, u32[]{:S(2)}) collective-permute-start(bf16[32,16,512]{2,1,0:T(8,128)(2,1)} %get-tuple-element.20), channel_id=1, source_target_pairs={{0,32},{32,0},{64,96},{96,64},{128,160},{160,128},{192,224},{224,1... | collective-permute-start | bytes 1572872 | tf_op jit(solution)/shard_map/ppermute | solution.py:243
  37.8 40.2 %copy-start.3 = (f32[1,1,512,512]{3,2,1,0:T(8,128)S(1)}, f32[1,1,512,512]{3,2,1,0:T(8,128)}, u32[]{:S(2)}) copy-start(f32[1,1,512,512]{3,2,1,0:T(8,128)} %param.7) | copy-start | bytes 3145732
  75.9 6.4 %collective-permute-start.7 = (f32[8,128]{1,0:T(8,128)S(1)}, f32[8,128]{1,0:T(8,128)S(1)}, u32[]{:S(2)}, u32[]{:S(2)}) collective-permute-start(f32[8,128]{1,0:T(8,128)S(1)} %slice.3), channel_id=1, source_target_pairs={{0,0},{33,1},{66,2},{99,3},{132,4},{165,5},{198,6},{231,7},{8,8},{... | collective-permute-start | bytes 12296 | tf_op jit(solution)/shard_map/ppermute | solution.py:291

commit v3 on v2

--- a/solution.py
+++ b/solution.py
@@ -15,8 +15,8 @@
 SMEM = pl.BlockSpec(memory_space=pltpu.SMEM)
 
 
-def params(**more):
-    return pltpu.CompilerParams(vmem_limit_bytes=48 << 20, **more)
+def params(limit=40 << 20):
+    return pltpu.CompilerParams(vmem_limit_bytes=limit)
 
 
 def upper_rows():
@@ -117,14 +117,20 @@
     lax.fori_loop(0, order_ref.shape[0], step, 0)
 
 
-def pair_kernel(pick_ref, own_ref, other_ref, out_ref):
+def pair_kernel(own_ref, other_ref, *refs):
     for p in range(other_ref.shape[0] // 2):
-        coded = [encode(own_ref[0, b].astype(f32) + other_ref[b].astype(f32)) for b in (2 * p, 2 * p + 1)]
-        store(out_ref, p, *coded)
-
-
-def sum_kernel(pick_ref, order_ref, own_ref, other_ref, *refs):
-    part_refs, (out_ref, slot_ref, coded_ref, square_ref) = refs[:-4], refs[-4:]
+        part = load(refs[0], p) if len(refs) > 1 else None
+        coded = []
+        for i in range(2):
+            strip = own_ref[2 * p + i].astype(f32) + other_ref[2 * p + i].astype(f32)
+            if part is not None:
+                strip += jnp.concatenate(decode(part[i]), axis=1)
+            coded.append(encode(strip))
+        store(refs[-1], p, *coded)
+
+
+def sum_kernel(order_ref, own_ref, other_ref, *refs):
+    part_refs, (out_ref, slot_ref, coded_ref, square_ref) = refs[:4], refs[4:]
     step, steps = pl.program_id(0), pl.num_programs(0)
     count = other_ref.shape[0]
 
@@ -133,22 +139,23 @@
         invert(order_ref, slot_ref)
         square_ref[...] = jnp.zeros_like(square_ref)
 
-    total = jnp.zeros((8, 128), f32)
-    for p in range(count // 2):
-        parts = [load(ref, p) for ref in part_refs]
-        for i in range(2):
-            b = 2 * p + i
-            strip = own_ref[0, b].astype(f32) + other_ref[b].astype(f32)
-            pieces = [decode(part[i]) for part in parts]
-            columns = [
-                strip[:, 128 * c : 128 * c + 128] + sum(piece[c] for piece in pieces[1:]) + pieces[0][c]
-                for c in range(4)
-            ]
-            for column in columns:
-                square = column * column
-                total += square[:8] + square[8:]
-            coded_ref[slot_ref[step * count + b]] = encode(jnp.concatenate(columns, axis=1))
-    square_ref[...] += total
+    def add(parts_of_half):
+        total = jnp.zeros((8, 128), f32)
+        for p in range(count // 2):
+            parts = [load(ref, p) for ref in parts_of_half]
+            for i in range(2):
+                b = 2 * p + i
+                strip = own_ref[b].astype(f32) + other_ref[b].astype(f32)
+                first, second = [decode(part[i]) for part in parts]
+                columns = [strip[:, 128 * c : 128 * c + 128] + (first[c] + second[c]) for c in range(4)]
+                for column in columns:
+                    square = column * column
+                    total += square[:8] + square[8:]
+                coded_ref[slot_ref[step * count + b]] = encode(jnp.concatenate(columns, axis=1))
+        square_ref[...] += total
+
+    pl.when(step < steps // 2)(lambda: add(part_refs[:2]))
+    pl.when(step >= steps // 2)(lambda: add(part_refs[2:]))
 
     @pl.when(step == steps - 1)
     def _():
@@ -232,38 +239,53 @@
     grouped = grads[0].reshape(groups, shards, strip, width)
     swap = [(d, d ^ 1) for d in range(groups)]
     chunk = 8
-    own_block = pl.BlockSpec((1, chunk, strip, width), lambda i, pick, *_: (pick[0], i, 0, 0))
-    other_block = pl.BlockSpec((chunk, strip, width), lambda i, *_: (i, 0, 0))
-    wire_block = pl.BlockSpec((chunk * ROWS, 128), lambda i, *_: (i, 0))
-
-    received = []
-    for ahead in (2, 1, 3, 0):
-        target = 2 * ((chip + ahead) % chips)
-        other = lax.dynamic_index_in_dim(grouped, target + 1 - core, 0, keepdims=False)
-        other = lax.ppermute(other, "dp", swap)
-        pick = (target + core).reshape(1)
-        if ahead == 0:
-            break
-        sums = pl.pallas_call(
+    steps = shards // chunk
+    half_wire = jax.ShapeDtypeStruct((shards * ROWS // 2, 128), jnp.int16)
+    half_block = pl.BlockSpec((chunk * ROWS, 128), lambda i, *_: (i, 0))
+
+    def cut(ahead, source):
+        index = 2 * ((chip + ahead) % chips)
+        return [lax.dynamic_index_in_dim(source, index + k, 0, keepdims=False) for k in (core, 1 - core)]
+
+    def partner(array):
+        return lax.ppermute(array, "dp", swap)
+
+    def along(ahead, array):
+        return lax.ppermute(array, "dp", [(d, (d + 2 * ahead) % groups) for d in range(groups)])
+
+    def pair_sum(half, own, other, *parts):
+        first = half * steps // 2
+        strips_block = pl.BlockSpec((chunk, strip, width), lambda i: (i + first, 0, 0))
+        return pl.pallas_call(
             pair_kernel,
-            grid_spec=pltpu.PrefetchScalarGridSpec(
-                num_scalar_prefetch=1,
-                grid=(shards // chunk,),
-                in_specs=[own_block, other_block],
-                out_specs=wire_block,
-            ),
-            out_shape=wire,
+            grid=(steps // 2,),
+            in_specs=[strips_block] * 2 + [half_block] * len(parts),
+            out_specs=half_block,
+            out_shape=half_wire,
             compiler_params=params(),
-            name=f"pair_{ahead}",
-        )(pick, grouped, other)
-        along = [(d, (d + 2 * ahead) % groups) for d in range(groups)]
-        received.append(lax.ppermute(sums, "dp", along))
+            name=f"pair_{half}_{len(parts)}",
+        )(own, other, *parts)
+
+    held, far = lax.optimization_barrier((grouped, cut(2, grouped)))
+    ahead, behind, mine_ = [cut(k, held) for k in (1, -1, 0)]
+    for pair in (far, ahead, behind, mine_):
+        pair[1] = partner(pair[1])
+    left_relay = along(1, pair_sum(0, *far))
+    right_relay = along(-1, pair_sum(1, *far))
+    left_direct, right_direct = pair_sum(1, *ahead), pair_sum(0, *behind)
+    ahead, behind, _, _ = lax.optimization_barrier((ahead, behind, left_direct, right_direct))
+    left_direct, right_direct = along(1, left_direct), along(-1, right_direct)
+    left_summed = along(1, pair_sum(0, *ahead, left_relay))
+    right_summed = along(-1, pair_sum(1, *behind, right_relay))
+    strips_block = pl.BlockSpec((chunk, strip, width), lambda i, *_: (i, 0, 0))
+    lower = pl.BlockSpec((chunk * ROWS, 128), lambda i, *_: (jnp.minimum(i, steps // 2 - 1), 0))
+    upper = pl.BlockSpec((chunk * ROWS, 128), lambda i, *_: (jnp.maximum(i - steps // 2, 0), 0))
     strips = pl.pallas_call(
         sum_kernel,
         grid_spec=pltpu.PrefetchScalarGridSpec(
-            num_scalar_prefetch=2,
-            grid=(shards // chunk,),
-            in_specs=[own_block, other_block] + [wire_block] * len(received),
+            num_scalar_prefetch=1,
+            grid=(steps,),
+            in_specs=[strips_block, strips_block, lower, lower, upper, upper],
             out_specs=pl.BlockSpec((shards * ROWS, 128), lambda i, *_: (0, 0)),
             scratch_shapes=[
                 pltpu.SMEM((shards,), jnp.int32),
@@ -274,7 +296,7 @@
         out_shape=wire,
         compiler_params=params(),
         name="sum_strips",
-    )(pick, mine, grouped, other, *received)
+    )(mine, *mine_, left_summed, right_direct, left_direct, right_summed)
     strips = lax.all_to_all(strips, "shard", split_axis=0, concat_axis=0, tiled=True)
     high, low, left_fresh, left_root, sums = pl.pallas_call(
         left_kernel,

time: 113 us -> 103 us (0.912)
  waiting for transfers between devices: 22.8 us -> 11.3 us
  starting transfers between devices: 9.07 us -> 11.2 us
    ppermute x7 -> x10, waiting for transfers between devices: 22.8 us -> 11.3 us  [the longest x6 11.3 us: along(): lax.ppermute(array, 'dp', [(d, (d + 2 * ahead) % groups) for d in range(g...]
    ppermute x7 -> x10, starting transfers between devices: 6.94 us -> 9.26 us  [the longest x6 8.65 us: along(): lax.ppermute(array, 'dp', [(d, (d + 2 * ahead) % groups) for d in range(g...]
    unnamed x8 -> x6, local copies, waits for them, and re-layouts: 2.2 us -> 0.02 us
    pallas_call x1, Pallas kernels: 3.57 us -> 1.81 us  [body(): pl.pallas_call(sum_kernel, grid_spec=pltpu.PrefetchScalarGridSpec(num_sca...]
    squeeze x1 -> x2, local copies, waits for them, and re-layouts: 2.74 us -> 4.5 us  [cut(): lax.dynamic_index_in_dim(source, index + k, 0, keepdims=False)]
    pallas_call x3 -> x6, Pallas kernels: 2.33 us -> 3.92 us  [pair_sum(): pl.pallas_call(pair_kernel, grid=(steps // 2,), in_specs=[strips_block] *...]
  transfers between devices with their start and end apart: 8 -> 11, of which waited for: 5 -> 4; matrix products, arithmetic and copies ran while one was open for 0% -> 3% of each run, Pallas kernels for 6% -> 8%
where the time goes in v3:
time: 103 us
  blocking collectives  56.3 us (55%)
  Pallas kernels  18.4 us (18%)
  waiting for transfers between devices  11.3 us (11%)
  starting transfers between devices  11.2 us (11%)
  local copies, waits for them, and re-layouts  4.52 us (4%)
    all_to_all x1, blocking collectives, body(): lax.all_to_all(strips, 'shard', split_axis=0, concat_axis=0, tiled=True)  29.7 us
    all_to_all x1, blocking collectives, body(): lax.all_to_all(pieces, 'shard', split_axis=0, concat_axis=0, tiled=True)  26.6 us
    ppermute x6, waiting for transfers between devices, along(): lax.ppermute(array, 'dp', [(d, (d + 2 * ahead) % groups) for d in range(g...  11.3 us
    ppermute x6, starting transfers between devices, along(): lax.ppermute(array, 'dp', [(d, (d + 2 * ahead) % groups) for d in range(g...  8.65 us
    squeeze x2, local copies, waits for them, and re-layouts, cut(): lax.dynamic_index_in_dim(source, index + k, 0, keepdims=False)  4.5 us
    pallas_call x1, Pallas kernels, body(): pl.pallas_call(left_kernel, in_specs=[VMEM, VMEM], out_specs=[VMEM] * 5,...  4.36 us
    pallas_call x1, Pallas kernels, body(): pl.pallas_call(right_kernel, in_specs=[VMEM] * 3, out_specs=[VMEM] * 2, o...  4.25 us
    pallas_call x6, Pallas kernels, pair_sum(): pl.pallas_call(pair_kernel, grid=(steps // 2,), in_specs=[strips_block] *...  3.92 us
  transfers between devices with their start and end apart: 11, of which 4 were waited for; matrix products, arithmetic and copies ran while one was open for 3% of the time, Pallas kernels for 8%

profile of v3, /device:TPU:32, one launch (start us, length us, event | category | flops | bytes accessed | tf_op | source)
XLA Modules:
  0.0 102.5 jit_solution(11966522172614892122)
XLA Ops:
  0.6 0.0 copy-start
  0.7 1.3 %dynamic-slice_bitcast_fusion.6 = (bf16[32,16,512]{2,1,0:T(8,128)(2,1)S(1)}, bf16[32,16,512]{2,1,0:T(8,128)(2,1)S(1)}) fusion(bf16[8,32,16,512]{3,2,1,0:T(8,128)(2,1)} %bitcast.33, s32[]{:T(128)S(6)} %select_n.61, s32[]{:T(128)S(6)} %select_n.60), kind=kLoop, calls=%fused_computation.6 | loop fusion | bytes 2097160 | tf_op jit(solution)/shard_map/jit(dynamic_index_in_dim)/squeeze | solution.py:248
  2.0 0.1 collective-permute-start.3
  2.2 3.2 %dynamic-slice_bitcast_fusion = (bf16[32,16,512]{2,1,0:T(8,128)(2,1)S(1)}, bf16[32,16,512]{2,1,0:T(8,128)(2,1)S(1)}, bf16[32,16,512]{2,1,0:T(8,128)(2,1)S(1)}, b...) fusion(bf16[8,32,16,512]{3,2,1,0:T(8,128)(2,1)} %bitcast.34, ...), kind=kLoop, calls=%fused_computation | loop fusion | bytes 6291480 | tf_op jit(solution)/shard_map/jit(dynamic_index_in_dim)/squeeze | solution.py:248
  5.4 0.4 collective-permute-start.2
  5.8 0.1 collective-permute-start.1
  5.9 0.0 collective-permute-done.3.other_ref
  5.9 0.2 pair_0_0.3
  6.1 1.6 %collective-permute-start.4 = (s16[1152,128]{1,0:T(8,128)(2,1)S(1)}, s16[1152,128]{1,0:T(8,128)(2,1)S(1)}, u32[]{:S(2)}, u32[]{:S(2)}) collective-permute-start(s16[1152,128]{1,0:T(8,128)(2,1)S(1)} %pair_0_0.3), channel_id=1, source_target_pairs={{0,64},{32,96},{64,128},{96,160},{128,192},{160,224},{192,0},{224,... | collective-permute-start | bytes 884744 | tf_op jit(solution)/shard_map/ppermute | solution.py:254
  7.7 0.2 pair_1_0.3
  7.9 1.8 %collective-permute-start.8 = (s16[1152,128]{1,0:T(8,128)(2,1)S(1)}, s16[1152,128]{1,0:T(8,128)(2,1)S(1)}, u32[]{:S(2)}, u32[]{:S(2)}) collective-permute-start(s16[1152,128]{1,0:T(8,128)(2,1)S(1)} %pair_1_0.3), channel_id=1, source_target_pairs={{0,192},{32,224},{64,0},{96,32},{128,64},{160,96},{192,128},{224,1... | collective-permute-start | bytes 884744 | tf_op jit(solution)/shard_map/ppermute | solution.py:254
  9.7 0.0 collective-permute-start
  9.7 0.0 collective-permute-done.2.other_ref
  9.7 0.8 pair_0_0.2
  10.5 1.5 %collective-permute-start.6 = (s16[1152,128]{1,0:T(8,128)(2,1)}, s16[1152,128]{1,0:T(8,128)(2,1)S(1)}, u32[]{:S(2)}, u32[]{:S(2)}) collective-permute-start(s16[1152,128]{1,0:T(8,128)(2,1)} %pair_0_0.2), channel_id=1, source_target_pairs={{0,192},{32,224},{64,0},{96,32},{128,64},{160,96},{192,128},{224,1... | collective-permute-start | bytes 884744 | tf_op jit(solution)/shard_map/ppermute | solution.py:254
  12.1 0.0 collective-permute-done.1.other_ref
  12.1 0.0 copy-start.1
  12.1 0.8 pair_1_0.2
  12.9 0.5 collective-permute-start.7
  13.4 3.3 %collective-permute-done.4.refs_0_ = s16[1152,128]{1,0:T(8,128)(2,1)S(1)} collective-permute-done((s16[1152,128]{1,0:T(8,128)(2,1)S(1)}, s16[1152,128]{1,0:T(8,128)(2,1)S(1)}, u32[]{:S(2)}, u32[]{:S(2)}) %collective-permute-start.4) | collective-permute-done | bytes 294944 | tf_op jit(solution)/shard_map/ppermute | solution.py:254
  16.7 0.9 pair_0_1.1
  17.7 0.7 collective-permute-start.5
  18.4 0.0 collective-permute-done.8.refs_0_
  18.4 0.9 pair_1_1.1
  19.3 2.5 %collective-permute-start.9 = (s16[1152,128]{1,0:T(8,128)(2,1)}, s16[1152,128]{1,0:T(8,128)(2,1)S(1)}, u32[]{:S(2)}, u32[]{:S(2)}) collective-permute-start(s16[1152,128]{1,0:T(8,128)(2,1)} %pair_1_1.1), channel_id=1, source_target_pairs={{0,192},{32,224},{64,0},{96,32},{128,64},{160,96},{192,128},{224,1... | collective-permute-start | bytes 884744 | tf_op jit(solution)/shard_map/ppermute | solution.py:254
  21.8 0.0 copy-done
  21.8 0.0 copy-start.2
  21.8 0.0 collective-permute-done.other_ref
  21.8 2.3 %collective-permute-done.6.refs_1_ = s16[1152,128]{1,0:T(8,128)(2,1)S(1)} collective-permute-done((s16[1152,128]{1,0:T(8,128)(2,1)}, s16[1152,128]{1,0:T(8,128)(2,1)S(1)}, u32[]{:S(2)}, u32[]{:S(2)}) %collective-permute-start.6) | collective-permute-done | bytes 294944 | tf_op jit(solution)/shard_map/ppermute | solution.py:254
  24.1 0.1 collective-permute-done.7.refs_2_
  24.2 5.6 %collective-permute-done.5.refs_0_ = s16[1152,128]{1,0:T(8,128)(2,1)S(1)} collective-permute-done((s16[1152,128]{1,0:T(8,128)(2,1)}, s16[1152,128]{1,0:T(8,128)(2,1)S(1)}, u32[]{:S(2)}, u32[]{:S(2)}) %collective-permute-start.5) | collective-permute-done | bytes 294944 | tf_op jit(solution)/shard_map/ppermute | solution.py:254
  29.8 0.0 collective-permute-done.9.refs_3_
  29.8 1.8 %sum_strips.1 = s16[2304,128]{1,0:T(8,128)(2,1)S(1)} custom-call(s32[32]{0:T(128)S(1)} %fusion.order_ref.refs_0_, bf16[32,16,512]{2,1,0:T(8,128)(2,1)S(1)} %get-tuple-element.36.own_ref, bf16[32,16,512]{2,1,0:T(8,128)(2,1)S(1)} %collective-permute-done.other_ref, s16[1152,128]{1,0:T(8,128)(2,1)S(1)} %collective-permute-done.5.refs_0_, ...), custom_call_target="tpu_custom_call" | custom-call | tf_op jit(solution)/shard_map/sum_strips/pallas_call | solution.py:283
  31.6 29.7 %all_to_all.22 = s16[32,72,128]{2,1,0:T(8,128)(2,1)S(1)} all-to-all(s16[32,72,128]{2,1,0:T(8,128)(2,1)S(1)} %bitcast.29), channel_id=1, replica_groups=mesh['dp'=8,'shard'=32] {'shard'}, dimensions={0} | all-to-all | bytes 1179648 | tf_op jit(solution)/shard_map/all_to_all | solution.py:300
  61.3 0.0 copy-done.1
  61.3 4.4 %left.1 = (bf16[512,512]{1,0:T(8,128)(2,1)S(1)}, bf16[512,512]{1,0:T(8,128)(2,1)S(1)}, f32[512,512]{1,0:T(8,128)}, f32[512,512]{1,0:T(8,128)S(1)}, f32[16,128]{1,0:T(8,128)S(1)}) custom-call(s16[2304,128]{1,0:T(8,128)(2,1)S(1)} %bitcast.27, f32[512,512]{1,0:T(8,128)S(1)} %bitcast.31), custom_call_target="tpu_custom_call" | custom-call | tf_op jit(solution)/shard_map/left/pallas_call | solution.py:301
  65.7 1.9 %collective-permute-start.10 = (f32[8,128]{1,0:T(8,128)S(1)}, f32[8,128]{1,0:T(8,128)S(1)}, u32[]{:S(2)}, u32[]{:S(2)}) collective-permute-start(f32[8,128]{1,0:T(8,128)S(1)} %slice.3), channel_id=1, source_target_pairs={{0,0},{33,1},{66,2},{99,3},{132,4},{165,5},{198,6},{231,7},{8,8},{... | collective-permute-start | bytes 12296 | tf_op jit(solution)/shard_map/ppermute | solution.py:313
  67.6 0.0 copy-done.2
  67.6 4.2 %right.1 = (f32[512,512]{1,0:T(8,128)}, f32[512,512]{1,0:T(8,128)S(1)}) custom-call(bf16[512,512]{1,0:T(8,128)(2,1)S(1)} %get-tuple-element.24.high_ref, bf16[512,512]{1,0:T(8,128)(2,1)S(1)} %get-tuple-element.25.low_ref, f32[512,512]{1,0:T(8,128)S(1)} %bitcast.32), custom_call_target="tpu_custom_call" | custom-call | flops 2684354560 | bytes 5242880 | tf_op jit(solution)/shard_map/right/pallas_call | solution.py:314
  71.9 0.0 collective-permute-done.10.total_ref
  71.9 2.4 %shape.1 = s16[2304,128]{1,0:T(8,128)(2,1)S(1)} custom-call(bf16[512,512]{1,0:T(8,128)(2,1)S(1)} %get-tuple-element.24.high_ref, bf16[512,512]{1,0:T(8,128)(2,1)S(1)} %get-tuple-element.25.low_ref, f32[512,512]{1,0:T(8,128)S(1)} %get-tuple-element.26.left_ref, f32[512,512]{1,0:T(8,128)S(1)} %get-tuple-element.27.right_ref, ...), custom_call_target="tpu_custom_call" | custom-call | tf_op jit(solution)/shard_map/shape/pallas_call | solution.py:323
  74.3 26.6 %all_to_all.23 = s16[32,72,128]{2,1,0:T(8,128)(2,1)S(1)} all-to-all(s16[32,72,128]{2,1,0:T(8,128)(2,1)S(1)} %bitcast.30), channel_id=1, replica_groups=mesh['dp'=8,'shard'=32] {'shard'}, dimensions={0} | all-to-all | bytes 1179648 | tf_op jit(solution)/shard_map/all_to_all | solution.py:332
  100.9 1.7 %update.1 = f32[32,16,512]{2,1,0:T(8,128)} custom-call(s32[32]{0:T(128)S(1)} %fusion.order_ref.refs_0_, s16[2304,128]{1,0:T(8,128)(2,1)S(1)} %bitcast.28), custom_call_target="tpu_custom_call" | custom-call | tf_op jit(solution)/shard_map/update/pallas_call | solution.py:333
  (2 shorter events, 0.0 us)
Async XLA Ops:
  0.6 21.2 %copy-start = (s32[8,32]{1,0:T(8,128)S(1)}, s32[8,32]{1,0:T(8,128)}, u32[]{:S(2)}) copy-start(s32[8,32]{1,0:T(8,128)} %param.5) | copy-start | bytes 3076
  2.0 3.9 %collective-permute-start.3 = (bf16[32,16,512]{2,1,0:T(8,128)(2,1)S(1)}, bf16[32,16,512]{2,1,0:T(8,128)(2,1)S(1)}, u32[]{:S(2)}, u32[]{:S(2)}) collective-permute-start(bf16[32,16,512]{2,1,0:T(8,128)(2,1)S(1)} %get-tuple-element.21), channel_id=1, source_target_pairs={{0,32},{32,0},{64,96},{96,64},{128,160},{160,128},{192,224},{224,1... | collective-permute-start | bytes 1572872 | tf_op jit(solution)/shard_map/ppermute | solution.py:251
  5.4 4.3 %collective-permute-start.2 = (bf16[32,16,512]{2,1,0:T(8,128)(2,1)S(1)}, bf16[32,16,512]{2,1,0:T(8,128)(2,1)S(1)}, u32[]{:S(2)}, u32[]{:S(2)}) collective-permute-start(bf16[32,16,512]{2,1,0:T(8,128)(2,1)S(1)} %get-tuple-element.31), channel_id=1, source_target_pairs={{0,32},{32,0},{64,96},{96,64},{128,160},{160,128},{192,224},{224,1... | collective-permute-start | bytes 1572872 | tf_op jit(solution)/shard_map/ppermute | solution.py:251
  5.8 6.3 %collective-permute-start.1 = (bf16[32,16,512]{2,1,0:T(8,128)(2,1)S(1)}, bf16[32,16,512]{2,1,0:T(8,128)(2,1)S(1)}, u32[]{:S(2)}, u32[]{:S(2)}) collective-permute-start(bf16[32,16,512]{2,1,0:T(8,128)(2,1)S(1)} %get-tuple-element.33), channel_id=1, source_target_pairs={{0,32},{32,0},{64,96},{96,64},{128,160},{160,128},{192,224},{224,1... | collective-permute-start | bytes 1572872 | tf_op jit(solution)/shard_map/ppermute | solution.py:251
  6.1 10.6 %collective-permute-start.4 = (s16[1152,128]{1,0:T(8,128)(2,1)S(1)}, s16[1152,128]{1,0:T(8,128)(2,1)S(1)}, u32[]{:S(2)}, u32[]{:S(2)}) collective-permute-start(s16[1152,128]{1,0:T(8,128)(2,1)S(1)} %pair_0_0.3), channel_id=1, source_target_pairs={{0,64},{32,96},{64,128},{96,160},{128,192},{160,224},{192,0},{224,... | collective-permute-start | bytes 884744 | tf_op jit(solution)/shard_map/ppermute | solution.py:254
  7.9 10.6 %collective-permute-start.8 = (s16[1152,128]{1,0:T(8,128)(2,1)S(1)}, s16[1152,128]{1,0:T(8,128)(2,1)S(1)}, u32[]{:S(2)}, u32[]{:S(2)}) collective-permute-start(s16[1152,128]{1,0:T(8,128)(2,1)S(1)} %pair_1_0.3), channel_id=1, source_target_pairs={{0,192},{32,224},{64,0},{96,32},{128,64},{160,96},{192,128},{224,1... | collective-permute-start | bytes 884744 | tf_op jit(solution)/shard_map/ppermute | solution.py:254
  9.7 12.2 %collective-permute-start = (bf16[32,16,512]{2,1,0:T(8,128)(2,1)}, bf16[32,16,512]{2,1,0:T(8,128)(2,1)S(1)}, u32[]{:S(2)}, u32[]{:S(2)}) collective-permute-start(bf16[32,16,512]{2,1,0:T(8,128)(2,1)} %get-tuple-element.35), channel_id=1, source_target_pairs={{0,32},{32,0},{64,96},{96,64},{128,160},{160,128},{192,224},{224,1... | collective-permute-start | bytes 1572872 | tf_op jit(solution)/shard_map/ppermute | solution.py:251
  10.5 13.6 %collective-permute-start.6 = (s16[1152,128]{1,0:T(8,128)(2,1)}, s16[1152,128]{1,0:T(8,128)(2,1)S(1)}, u32[]{:S(2)}, u32[]{:S(2)}) collective-permute-start(s16[1152,128]{1,0:T(8,128)(2,1)} %pair_0_0.2), channel_id=1, source_target_pairs={{0,192},{32,224},{64,0},{96,32},{128,64},{160,96},{192,128},{224,1... | collective-permute-start | bytes 884744 | tf_op jit(solution)/shard_map/ppermute | solution.py:254
  12.1 49.2 %copy-start.1 = (f32[1,1,512,512]{3,2,1,0:T(8,128)S(1)}, f32[1,1,512,512]{3,2,1,0:T(8,128)}, u32[]{:S(2)}) copy-start(f32[1,1,512,512]{3,2,1,0:T(8,128)} %param.6) | copy-start | bytes 3145732
  12.9 11.3 %collective-permute-start.7 = (s16[1152,128]{1,0:T(8,128)(2,1)}, s16[1152,128]{1,0:T(8,128)(2,1)S(1)}, u32[]{:S(2)}, u32[]{:S(2)}) collective-permute-start(s16[1152,128]{1,0:T(8,128)(2,1)} %pair_1_0.2), channel_id=1, source_target_pairs={{0,64},{32,96},{64,128},{96,160},{128,192},{160,224},{192,0},{224,... | collective-permute-start | bytes 884744 | tf_op jit(solution)/shard_map/ppermute | solution.py:254
  17.7 12.1 %collective-permute-start.5 = (s16[1152,128]{1,0:T(8,128)(2,1)}, s16[1152,128]{1,0:T(8,128)(2,1)S(1)}, u32[]{:S(2)}, u32[]{:S(2)}) collective-permute-start(s16[1152,128]{1,0:T(8,128)(2,1)} %pair_0_1.1), channel_id=1, source_target_pairs={{0,64},{32,96},{64,128},{96,160},{128,192},{160,224},{192,0},{224,... | collective-permute-start | bytes 884744 | tf_op jit(solution)/shard_map/ppermute | solution.py:254
  19.3 10.5 %collective-permute-start.9 = (s16[1152,128]{1,0:T(8,128)(2,1)}, s16[1152,128]{1,0:T(8,128)(2,1)S(1)}, u32[]{:S(2)}, u32[]{:S(2)}) collective-permute-start(s16[1152,128]{1,0:T(8,128)(2,1)} %pair_1_1.1), channel_id=1, source_target_pairs={{0,192},{32,224},{64,0},{96,32},{128,64},{160,96},{192,128},{224,1... | collective-permute-start | bytes 884744 | tf_op jit(solution)/shard_map/ppermute | solution.py:254
  21.8 45.8 %copy-start.2 = (f32[1,1,512,512]{3,2,1,0:T(8,128)S(1)}, f32[1,1,512,512]{3,2,1,0:T(8,128)}, u32[]{:S(2)}) copy-start(f32[1,1,512,512]{3,2,1,0:T(8,128)} %param.7) | copy-start | bytes 3145732
  65.7 6.2 %collective-permute-start.10 = (f32[8,128]{1,0:T(8,128)S(1)}, f32[8,128]{1,0:T(8,128)S(1)}, u32[]{:S(2)}, u32[]{:S(2)}) collective-permute-start(f32[8,128]{1,0:T(8,128)S(1)} %slice.3), channel_id=1, source_target_pairs={{0,0},{33,1},{66,2},{99,3},{132,4},{165,5},{198,6},{231,7},{8,8},{... | collective-permute-start | bytes 12296 | tf_op jit(solution)/shard_map/ppermute | solution.py:313

commit v4 on v3

v4 whole, which is shorter than its diff:
```python
import jax
import jax.numpy as jnp
from jax import lax
from jax.experimental import pallas as pl
from jax.experimental.pallas import tpu as pltpu
from jax.sharding import PartitionSpec as P

ROWS = 72
QUAD = 272
LIMIT = 32700.0
STEPS = 128.0
K = 1.25**6
EPS = 1e-06
f32, bf16 = jnp.float32, jnp.bfloat16
VMEM = pl.BlockSpec(memory_space=pltpu.VMEM)
SMEM = pl.BlockSpec(memory_space=pltpu.SMEM)
ANY = pl.BlockSpec(memory_space=pl.ANY)


def params(mebibytes):
    return pltpu.CompilerParams(vmem_limit_bytes=mebibytes << 20)


def upper_rows():
    return lax.broadcasted_iota(jnp.int32, (8, 128), 0) < 4


def encode_parts(strip):
    columns = [strip[:, c : c + 128] for c in range(0, strip.shape[1], 128)]
    top = jnp.abs(columns[0])
    for column in columns[1:]:
        top = jnp.maximum(top, jnp.abs(column))
    top = jnp.maximum(top[:8], top[8:])
    top = jnp.maximum(jnp.maximum(top, pltpu.roll(top, 4, 0)), 1e-30)
    code = jnp.ceil(jnp.log2(top) * STEPS)
    gain = jnp.exp2(code * (-1.0 / STEPS)) * LIMIT
    gain = jnp.concatenate([gain, gain], axis=0)
    return [jnp.round(column * gain) for column in columns], code


def encode(strip, number=None):
    coded, code = encode_parts(strip)
    tail = code if number is None else jnp.where(upper_rows(), code, number)
    return jnp.concatenate(coded + [tail], axis=0).astype(jnp.int32)


def encode_four(strips):
    coded, codes = zip(*[encode_parts(strip) for strip in strips])
    tails = [jnp.where(upper_rows(), codes[i], codes[i + 1]) for i in (0, 2)]
    return jnp.concatenate([c for part in coded for c in part] + tails, axis=0).astype(jnp.int32).astype(jnp.int16)


def decode_four(ref, quad):
    coded = ref[QUAD * quad : QUAD * (quad + 1), :].astype(jnp.int32).astype(f32)
    out = []
    for i in range(4):
        tail = coded[256 + 8 * (i // 2) : 264 + 8 * (i // 2)]
        gain = decode_gain(tail if i % 2 == 0 else pltpu.roll(tail, 4, 0))
        out.append([coded[r : r + 16] * gain for r in range(64 * i, 64 * i + 64, 16)])
    return out


def decode_gain(tail):
    code = jnp.where(upper_rows(), tail, pltpu.roll(tail, 4, 0))
    gain = jnp.exp2(code * (1.0 / STEPS)) * (1.0 / LIMIT)
    return jnp.concatenate([gain, gain], axis=0)


def decode(coded, factor=None):
    gain = decode_gain(coded[64:])
    if factor is not None:
        gain = gain * factor
    return [coded[r : r + 16] * gain for r in range(0, 64, 16)]


def load(ref, pair):
    both = ref[2 * ROWS * pair : 2 * ROWS * (pair + 1), :].astype(jnp.int32).astype(f32)
    return both[:ROWS], both[ROWS:]


def store(ref, pair, first, second):
    both = jnp.concatenate([first, second], axis=0)
    ref[2 * ROWS * pair : 2 * ROWS * (pair + 1), :] = both.astype(jnp.int16)


def encode_number(number):
    power = jnp.ceil(jnp.log2(jnp.maximum(number, 1e-30))) + 1.0
    digits = number * jnp.exp2(-power) * 16384.0
    high = jnp.floor(digits)
    low = jnp.floor((digits - high) * 16384.0)
    row = lax.broadcasted_iota(jnp.int32, number.shape, 0)
    return jnp.where(row == 4, power, jnp.where(row == 5, high, low))


def decode_number(tail):
    power, high, low = tail[4:5], tail[5:6], tail[6:7]
    return (high + low * (1.0 / 16384.0)) * (1.0 / 16384.0) * jnp.exp2(power)


def split(matrix):
    high = matrix.astype(bf16)
    return high, (matrix - high.astype(f32)).astype(bf16)


def dot3(left, right, dims=((1,), (0,))):
    dims = (dims, ((), ()))
    lh, ll = left
    rh, rl = right
    out = lax.dot_general(lh, rl, dims, preferred_element_type=f32)
    out += lax.dot_general(ll, rh, dims, preferred_element_type=f32)
    return out + lax.dot_general(lh, rh, dims, preferred_element_type=f32)


def eye_like(matrix):
    row = lax.broadcasted_iota(jnp.int32, matrix.shape, 0)
    column = lax.broadcasted_iota(jnp.int32, matrix.shape, 1)
    return row == column


def inverse_root(stat):
    diagonal = eye_like(stat)
    shifted = stat + jnp.where(diagonal, EPS, 0.0)
    norm = jnp.sqrt(jnp.sum(shifted * shifted, keepdims=True))
    u = shifted * (0.2 / norm)
    us = split(u)
    u2 = dot3(us, us)
    u2s = split(u2)
    rest = jnp.dot(u2s[0], (K * u2 - 5.0 * K * u).astype(bf16), preferred_element_type=f32)
    inner = 10.0 * K * (u2 - u) + rest
    outer = jnp.where(diagonal, 1.5625, 0.0) - (1.5625 + K) * u + 5.0 * K * u2
    root = outer + dot3(u2s, split(inner))
    return root * lax.rsqrt(jnp.sqrt(norm))


def invert(order_ref, slot_ref):
    def step(j, _):
        slot_ref[order_ref[j]] = j
        return 0

    lax.fori_loop(0, order_ref.shape[0], step, 0)


def cut_kernel(aheads, source_ref, *refs):
    group, (*outs, done) = lax.axis_index("dp"), refs
    chips = source_ref.shape[0] // 2
    copies = []
    for n, ahead in enumerate(aheads):
        base = 2 * ((group // 2 + ahead) % chips)
        for k, core in enumerate((group % 2, 1 - group % 2)):
            copies.append(pltpu.make_async_copy(source_ref.at[base + core], outs[2 * n + k], done.at[2 * n + k]))
    for copy in copies:
        copy.start()
    for copy in copies:
        copy.wait()


def pair_kernel(first, own_ref, other_ref, *refs):
    for q in range(refs[-1].shape[0] // QUAD):
        blocks = range(first + 4 * q, first + 4 * q + 4)
        strips = [own_ref[b].astype(f32) + other_ref[b].astype(f32) for b in blocks]
        if len(refs) > 1:
            parts = decode_four(refs[0], q)
            strips = [strip + jnp.concatenate(part, axis=1) for strip, part in zip(strips, parts)]
        refs[-1][QUAD * q : QUAD * (q + 1), :] = encode_four(strips)


def sum_kernel(order_ref, own_ref, other_ref, *refs):
    part_refs, (out_ref, square_ref, slot_ref, coded_ref) = refs[:4], refs[4:]
    invert(order_ref, slot_ref)
    total = jnp.zeros((8, 128), f32)
    quads = own_ref.shape[0] // 4
    for q in range(quads):
        lower = q < quads // 2
        parts = [decode_four(ref, q % (quads // 2)) for ref in (part_refs[:2] if lower else part_refs[2:])]
        for i in range(4):
            b = 4 * q + i
            strip = own_ref[b].astype(f32) + other_ref[b].astype(f32)
            first, second = [part[i] for part in parts]
            columns = [strip[:, 128 * c : 128 * c + 128] + (first[c] + second[c]) for c in range(4)]
            for column in columns:
                square = column * column
                total += square[:8] + square[8:]
            coded_ref[slot_ref[b]] = encode(jnp.concatenate(columns, axis=1))
    square_ref[...] = jnp.broadcast_to(jnp.sum(total, keepdims=True), total.shape)
    for p in range(coded_ref.shape[0] // 2):
        store(out_ref, p, coded_ref[2 * p], coded_ref[2 * p + 1])


def owner_kernel(coded_ref, left_in, right_in, total_ref, left_out, right_out, out_ref, *scratch):
    grad_ref, left_ref, right_ref, done = scratch
    order = grad_ref.shape[0]
    reads = [pltpu.make_async_copy(a, b, done.at[i]) for i, (a, b) in enumerate([(left_in, left_ref), (right_in, right_ref)])]
    for copy in reads:
        copy.start()
    square = jnp.zeros((16, 128), f32)
    for p in range(order // 32):
        for i, coded in enumerate(load(coded_ref, p)):
            row = 16 * (2 * p + i)
            for c, piece in enumerate(decode(coded)):
                square += piece * piece
                grad_ref[row : row + 16, 128 * c : 128 * c + 128] = piece
    grad = split(grad_ref[...])
    for copy in reads:
        copy.wait()
    left_ref[...] = 0.95 * left_ref[...] + dot3(grad, grad, ((1,), (1,))) * (1.0 / order)
    right_ref[...] = 0.95 * right_ref[...] + dot3(grad, grad, ((0,), (0,))) * (1.0 / order)
    writes = [pltpu.make_async_copy(a, b, done.at[i]) for i, (a, b) in enumerate([(left_ref, left_out), (right_ref, right_out)])]
    for copy in writes:
        copy.start()
    half = dot3(split(inverse_root(left_ref[...])), grad)
    shaped = dot3(split(half), split(inverse_root(right_ref[...])))
    cells = 1.0 / (order * order)
    mean = jnp.sum(shaped * shaped, keepdims=True) * cells
    graft = jnp.sqrt(jnp.sum(square, keepdims=True) * cells + EPS) / jnp.sqrt(mean + EPS)
    grad_ref[...] = shaped * graft
    number = encode_number(total_ref[...])
    for p in range(order // 32):
        rows = 32 * p
        store(
            out_ref,
            p,
            encode(grad_ref[rows : rows + 16, :], number),
            encode(grad_ref[rows + 16 : rows + 32, :], number),
        )
    for copy in writes:
        copy.wait()


def update_kernel(cells, order_ref, coded_ref, out_ref, wide_ref, done):
    total = jnp.zeros((1, 128), f32)
    for p in range(wide_ref.shape[0] // 2):
        base = 2 * ROWS * p
        first = coded_ref[base + 64 : base + 80, :].astype(jnp.int32).astype(f32)[:8]
        second = coded_ref[base + 128 : base + 144, :].astype(jnp.int32).astype(f32)[8:]
        total += decode_number(first) + decode_number(second)
    layer = 1.0 / jnp.sqrt(total * (1.0 / cells) + EPS)
    copies = []
    for p in range(wide_ref.shape[0] // 2):
        for i, coded in enumerate(load(coded_ref, p)):
            j = 2 * p + i
            for c, piece in enumerate(decode(coded, layer)):
                wide_ref[j, :, 128 * c : 128 * c + 128] = piece
            copies.append(pltpu.make_async_copy(wide_ref.at[j], out_ref.at[order_ref[j]], done.at[j]))
            copies[-1].start()
    for copy in copies:
        copy.wait()


def body(grads, owned, left_stat, right_stat):
    shards, groups = lax.axis_size("shard"), lax.axis_size("dp")
    group = lax.axis_index("dp")
    blocks, strip, width = grads.shape[1:]
    core, chip, chips = group % 2, group // 2, groups // 2
    mine = lax.dynamic_index_in_dim(owned, group, 0, keepdims=False)
    square = jax.ShapeDtypeStruct((width, width), f32)
    halves = jax.ShapeDtypeStruct((width, width), bf16)
    wire = jax.ShapeDtypeStruct((shards * ROWS, 128), jnp.int16)
    grouped = grads[0].reshape(groups, shards, strip, width)
    swap = [(d, d ^ 1) for d in range(groups)]
    half_wire = pltpu.VMEM((shards // 8 * QUAD, 128), jnp.int16)
    number = jax.ShapeDtypeStruct((8, 128), f32)

    def cut(source, *aheads):
        return pl.pallas_call(
            lambda *refs: cut_kernel([ahead % chips for ahead in aheads], *refs),
            in_specs=[pl.BlockSpec(memory_space=pltpu.HBM)],
            out_specs=[VMEM] * (2 * len(aheads)),
            out_shape=[pltpu.VMEM((shards, strip, width), bf16)] * (2 * len(aheads)),
            scratch_shapes=[pltpu.SemaphoreType.DMA((2 * len(aheads),))],
            compiler_params=params(4),
            name=f"cut_{len(aheads)}",
        )(source)

    def partner(array):
        return lax.ppermute(array, "dp", swap)

    def along(ahead, array):
        return lax.ppermute(array, "dp", [(d, (d + 2 * ahead) % groups) for d in range(groups)])

    def pair_sum(half, own, other, *parts):
        return pl.pallas_call(
            lambda *refs: pair_kernel(half * shards // 2, *refs),
            in_specs=[VMEM] * (2 + len(parts)),
            out_specs=VMEM,
            out_shape=half_wire,
            compiler_params=params(4),
            name=f"pair_{half}_{len(parts)}",
        )(own, other, *parts)

    held, far = lax.optimization_barrier((grouped, cut(grouped, 2)))
    far = far[0], partner(far[1])
    rest = cut(held, 1, -1, 0)
    others = [partner(rest[2 * n + 1]) for n in range(3)]
    left_relay, right_relay = pair_sum(0, *far), pair_sum(1, *far)
    owns, left_relay, right_relay = lax.optimization_barrier((rest[::2], left_relay, right_relay))
    ahead, behind, here = zip(owns, others)
    left_relay, right_relay = along(1, left_relay), along(-1, right_relay)
    left_direct, right_direct = pair_sum(1, *ahead), pair_sum(0, *behind)
    ahead, behind, _, _ = lax.optimization_barrier((ahead, behind, left_direct, right_direct))
    left_direct, right_direct = along(1, left_direct), along(-1, right_direct)
    left_summed = along(1, pair_sum(0, *ahead, left_relay))
    right_summed = along(-1, pair_sum(1, *behind, right_relay))
    strips, total = pl.pallas_call(
        sum_kernel,
        in_specs=[SMEM] + [VMEM] * 6,
        out_specs=[VMEM] * 2,
        scratch_shapes=[pltpu.SMEM((shards,), jnp.int32), pltpu.VMEM((shards, ROWS, 128), jnp.int32)],
        out_shape=[wire, number],
        compiler_params=params(8),
        name="sum_strips",
    )(mine, *here, left_summed, right_direct, left_direct, right_summed)
    strips = lax.all_to_all(strips, "shard", split_axis=0, concat_axis=0, tiled=True)
    for bit in (1, 2, 4):
        total += lax.ppermute(total, "dp", [(d, d ^ bit) for d in range(groups)])
    left_fresh, right_fresh, pieces = pl.pallas_call(
        owner_kernel,
        in_specs=[VMEM, ANY, ANY, VMEM],
        out_specs=[ANY, ANY, VMEM],
        out_shape=[square, square, wire],
        scratch_shapes=[pltpu.VMEM((width, width), f32)] * 3 + [pltpu.SemaphoreType.DMA((2,))],
        compiler_params=params(24),
        name="owner",
    )(strips, left_stat[0, 0], right_stat[0, 0], total)
    pieces = lax.all_to_all(pieces, "shard", split_axis=0, concat_axis=0, tiled=True)
    update = pl.pallas_call(
        lambda *refs: update_kernel(blocks * width * width, *refs),
        in_specs=[SMEM, VMEM],
        out_specs=ANY,
        out_shape=jax.ShapeDtypeStruct((shards, strip, width), f32),
        scratch_shapes=[pltpu.VMEM((shards, strip, width), f32), pltpu.SemaphoreType.DMA((shards,))],
        compiler_params=params(8),
        name="update",
    )(mine, pieces)
    return update, left_fresh[None, None], right_fresh[None, None]


def solution(mesh):
    return jax.shard_map(
        body,
        mesh=mesh,
        in_specs=(
            P("dp", None, "shard", None),
            P(),
            P("dp", "shard", None, None),
            P("dp", "shard", None, None),
        ),
        out_specs=(
            P("dp", "shard", None),
            P("dp", "shard", None, None),
            P("dp", "shard", None, None),
        ),
        check_vma=False,
    )
```

time: 103 us -> 94.8 us (0.920)
  blocking collectives: 56.3 us -> 21.4 us
  waiting for transfers between devices: 11.3 us -> 28.6 us
  starting transfers between devices: 11.2 us -> 22 us
  local copies, waits for them, and re-layouts: 4.52 us -> 2.21 us
    all_to_all x1 -> x0, blocking collectives: 29.7 us -> none  [body(): lax.all_to_all(strips, 'shard', split_axis=0, concat_axis=0, tiled=True)]
    all_to_all x0 -> x1, starting transfers between devices: none -> 11.4 us  [body(): lax.all_to_all(strips, 'shard', split_axis=0, concat_axis=0, tiled=True)]
    ppermute x1 -> x3, waiting for transfers between devices: 0.01 us -> 9.87 us  [body(): total += lax.ppermute(total, 'dp', [(d, d ^ bit) for d in range(groups)])]
    all_to_all x0 -> x1, waiting for transfers between devices: none -> 7.33 us  [body(): lax.all_to_all(strips, 'shard', split_axis=0, concat_axis=0, tiled=True)]
    all_to_all x1, blocking collectives: 26.6 us -> 21.4 us  [body(): lax.all_to_all(pieces, 'shard', split_axis=0, concat_axis=0, tiled=True)]
    squeeze x2 -> x0, local copies, waits for them, and re-layouts: 4.5 us -> none  [cut(): lax.dynamic_index_in_dim(source, index + k, 0, keepdims=False)]
    unnamed x6 -> x8, local copies, waits for them, and re-layouts: 0.02 us -> 2.2 us
    ppermute x1 -> x3, starting transfers between devices: 1.92 us -> 0.1 us  [body(): total += lax.ppermute(total, 'dp', [(d, d ^ bit) for d in range(groups)])]
  transfers between devices with their start and end apart: 11 -> 14, of which waited for: 4 -> 10; matrix products, arithmetic and copies ran while one was open for 3% -> 0% of each run, Pallas kernels for 8% -> 5%
where the time goes in v4:
time: 94.8 us; the launch traced here: 94.2 us
  waiting for transfers between devices  28.6 us (30%)
  starting transfers between devices  22 us (23%)
  blocking collectives  21.4 us (23%)
  Pallas kernels  19.1 us (20%)
  local copies, waits for them, and re-layouts  2.21 us (2%)
    all_to_all x1, blocking collectives, body(): lax.all_to_all(pieces, 'shard', split_axis=0, concat_axis=0, tiled=True)  21.4 us
    all_to_all x1, starting transfers between devices, body(): lax.all_to_all(strips, 'shard', split_axis=0, concat_axis=0, tiled=True)  11.4 us
    ppermute x6, waiting for transfers between devices, along(): lax.ppermute(array, 'dp', [(d, (d + 2 * ahead) % groups) for d in range(g...  11.2 us
    ppermute x3, waiting for transfers between devices, body(): total += lax.ppermute(total, 'dp', [(d, d ^ bit) for d in range(groups)])  9.87 us
    ppermute x6, starting transfers between devices, along(): lax.ppermute(array, 'dp', [(d, (d + 2 * ahead) % groups) for d in range(g...  9.77 us
    pallas_call x1, Pallas kernels, body(): pl.pallas_call(owner_kernel, in_specs=[VMEM, ANY, ANY, VMEM], out_specs=[...  9.14 us
    all_to_all x1, waiting for transfers between devices, body(): lax.all_to_all(strips, 'shard', split_axis=0, concat_axis=0, tiled=True)  7.33 us
    pallas_call x6, Pallas kernels, pair_sum(): pl.pallas_call(lambda *refs: pair_kernel(half * shards // 2, *refs), in_s...  3.93 us
  transfers between devices with their start and end apart: 14, of which 10 were waited for; matrix products, arithmetic and copies ran while one was open for 0% of the time, Pallas kernels for 5%

profile of v4, /device:TPU:32, one launch (start us, length us, event | category | flops | bytes accessed | tf_op | source)
XLA Modules:
  0.0 94.2 jit_solution(582501306341996388)
XLA Ops:
  0.6 0.0 copy-start
  0.6 0.0 copy-start.1
  0.7 2.2 %copy-done.1 = bf16[1,256,16,512]{3,2,1,0:T(8,128)(2,1)S(1)} copy-done((bf16[1,256,16,512]{3,2,1,0:T(8,128)(2,1)S(1)}, bf16[1,256,16,512]{3,2,1,0:T(8,128)(2,1)}, u32[]{:S(2)}) %copy-start.1) | copy-done | bytes 4194328
  2.8 0.1 cut_1.1
  2.9 0.1 collective-permute-start
  3.0 1.1 %cut_3.1 = (bf16[32,16,512]{2,1,0:T(8,128)(2,1)S(1)}, bf16[32,16,512]{2,1,0:T(8,128)(2,1)S(1)}, bf16[32,16,512]{2,1,0:T(8,128)(2,1)S(1)}, bf16[32,16,512]{2,1,0:...) custom-call(bf16[8,32,16,512]{3,2,1,0:T(8,128)(2,1)S(1)} %bitcast.12), custom_call_target="tpu_custom_call" | custom-call | tf_op jit(solution)/shard_map/cut_3/pallas_call | solution.py:264
  4.1 0.6 collective-permute-start.3
  4.7 0.1 collective-permute-start.2
  4.8 0.1 collective-permute-done.refs_1_
  4.9 0.2 pair_0_0.2
  5.1 0.2 pair_1_0.2
  5.3 2.8 %collective-permute-start.8 = (s16[1088,128]{1,0:T(8,128)(2,1)S(1)}, s16[1088,128]{1,0:T(8,128)(2,1)S(1)}, u32[]{:S(2)}, u32[]{:S(2)}) collective-permute-start(s16[1088,128]{1,0:T(8,128)(2,1)S(1)} %pair_1_0.2), channel_id=1, source_target_pairs={{0,192},{32,224},{64,0},{96,32},{128,64},{160,96},{192,128},{224,1... | collective-permute-start | bytes 835592 | tf_op jit(solution)/shard_map/ppermute | solution.py:278
  8.1 0.0 collective-permute-start.4
  8.1 0.0 collective-permute-start.1
  8.1 0.0 collective-permute-done.3.refs_1_
  8.1 0.9 pair_0_0.3
  9.0 0.0 copy-start.2
  9.0 0.0 copy-start.3
  9.0 3.2 %collective-permute-start.6 = (s16[1088,128]{1,0:T(8,128)(2,1)}, s16[1088,128]{1,0:T(8,128)(2,1)S(1)}, u32[]{:S(2)}, u32[]{:S(2)}) collective-permute-start(s16[1088,128]{1,0:T(8,128)(2,1)} %pair_0_0.3), channel_id=1, source_target_pairs={{0,192},{32,224},{64,0},{96,32},{128,64},{160,96},{192,128},{224,1... | collective-permute-start | bytes 835592 | tf_op jit(solution)/shard_map/ppermute | solution.py:278
  12.2 0.0 collective-permute-done.2.refs_1_
  12.2 0.9 pair_1_0.3
  13.1 0.0 collective-permute-start.7
  13.1 2.0 %collective-permute-done.8.refs_2_ = s16[1088,128]{1,0:T(8,128)(2,1)S(1)} collective-permute-done((s16[1088,128]{1,0:T(8,128)(2,1)S(1)}, s16[1088,128]{1,0:T(8,128)(2,1)S(1)}, u32[]{:S(2)}, u32[]{:S(2)}) %collective-permute-start.8) | collective-permute-done | bytes 278560 | tf_op jit(solution)/shard_map/ppermute | solution.py:278
  15.1 1.0 %pair_1_1.1 = s16[1088,128]{1,0:T(8,128)(2,1)} custom-call(bf16[32,16,512]{2,1,0:T(8,128)(2,1)S(1)} %get-tuple-element.45.refs_0_, bf16[32,16,512]{2,1,0:T(8,128)(2,1)S(1)} %collective-permute-done.3.refs_1_, s16[1088,128]{1,0:T(8,128)(2,1)S(1)} %collective-permute-done.8.refs_2_), custom_call_target="tpu_custom_call" | custom-call | tf_op jit(solution)/shard_map/pair_1_1/pallas_call | solution.py:281
  16.0 3.7 %collective-permute-start.9 = (s16[1088,128]{1,0:T(8,128)(2,1)}, s16[1088,128]{1,0:T(8,128)(2,1)}, u32[]{:S(2)}, u32[]{:S(2)}) collective-permute-start(s16[1088,128]{1,0:T(8,128)(2,1)} %pair_1_1.1), channel_id=1, source_target_pairs={{0,192},{32,224},{64,0},{96,32},{128,64},{160,96},{192,128},{224,1... | collective-permute-start | bytes 835592 | tf_op jit(solution)/shard_map/ppermute | solution.py:278
  19.7 0.0 collective-permute-done.4.refs_2_
  19.7 0.9 %pair_0_1.1 = s16[1088,128]{1,0:T(8,128)(2,1)} custom-call(bf16[32,16,512]{2,1,0:T(8,128)(2,1)S(1)} %get-tuple-element.42.refs_0_, bf16[32,16,512]{2,1,0:T(8,128)(2,1)S(1)} %collective-permute-done.2.refs_1_, s16[1088,128]{1,0:T(8,128)(2,1)S(1)} %collective-permute-done.4.refs_2_), custom_call_target="tpu_custom_call" | custom-call | tf_op jit(solution)/shard_map/pair_0_1/pallas_call | solution.py:281
  20.7 0.0 collective-permute-start.5
  20.7 0.0 copy-done
  20.7 0.0 collective-permute-done.1.other_ref
  20.7 0.5 collective-permute-done.6.refs_1_
  21.2 3.3 %collective-permute-done.7.refs_2_ = s16[1088,128]{1,0:T(8,128)(2,1)} collective-permute-done((s16[1088,128]{1,0:T(8,128)(2,1)}, s16[1088,128]{1,0:T(8,128)(2,1)}, u32[]{:S(2)}, u32[]{:S(2)}) %collective-permute-start.7) | collective-permute-done | bytes 278560 | tf_op jit(solution)/shard_map/ppermute | solution.py:278
  24.4 2.1 %collective-permute-done.9.refs_3_ = s16[1088,128]{1,0:T(8,128)(2,1)} collective-permute-done((s16[1088,128]{1,0:T(8,128)(2,1)}, s16[1088,128]{1,0:T(8,128)(2,1)}, u32[]{:S(2)}, u32[]{:S(2)}) %collective-permute-start.9) | collective-permute-done | bytes 278560 | tf_op jit(solution)/shard_map/ppermute | solution.py:278
  26.5 3.4 %collective-permute-done.5.refs_0_ = s16[1088,128]{1,0:T(8,128)(2,1)} collective-permute-done((s16[1088,128]{1,0:T(8,128)(2,1)}, s16[1088,128]{1,0:T(8,128)(2,1)}, u32[]{:S(2)}, u32[]{:S(2)}) %collective-permute-start.5) | collective-permute-done | bytes 278560 | tf_op jit(solution)/shard_map/ppermute | solution.py:278
  29.9 3.0 %sum_strips.1 = (s16[2304,128]{1,0:T(8,128)(2,1)}, f32[8,128]{1,0:T(8,128)S(1)}) custom-call(s32[32]{0:T(128)S(1)} %dynamic-slice_bitcast_fusion.order_ref.refs_0_, bf16[32,16,512]{2,1,0:T(8,128)(2,1)S(1)} %get-tuple-element.36.own_ref, bf16[32,16,512]{2,1,0:T(8,128)(2,1)S(1)} %collective-permute-done.1.other_ref, ...), custom_call_target="tpu_custom_call" | custom-call | tf_op jit(solution)/shard_map/sum_strips/pallas_call | solution.py:303
  32.9 11.4 %all-to-all-start = ((s16[32,72,128]{2,1,0:T(8,128)(2,1)}), s16[32,72,128]{2,1,0:T(8,128)(2,1)S(1)}, u32[]{:S(2)}, u32[]{:S(2)}) async-start(s16[32,72,128]{2,1,0:T(8,128)(2,1)} %bitcast.2), calls=%async_computation | async-start | bytes 1179648 | tf_op jit(solution)/shard_map/all_to_all | solution.py:312
  44.3 0.1 collective-permute-start.10
  44.4 1.2 %collective-permute-done.10 = f32[8,128]{1,0:T(8,128)S(1)} collective-permute-done((f32[8,128]{1,0:T(8,128)S(1)}, f32[8,128]{1,0:T(8,128)S(1)}, u32[]{:S(2)}, u32[]{:S(2)}) %collective-permute-start.10) | collective-permute-done | bytes 4128 | tf_op jit(solution)/shard_map/ppermute | solution.py:314
  45.5 0.0 collective-permute-start.11
  45.6 3.6 %collective-permute-done.11 = f32[8,128]{1,0:T(8,128)S(1)} collective-permute-done((f32[8,128]{1,0:T(8,128)S(1)}, f32[8,128]{1,0:T(8,128)S(1)}, u32[]{:S(2)}, u32[]{:S(2)}) %collective-permute-start.11) | collective-permute-done | bytes 4128 | tf_op jit(solution)/shard_map/ppermute | solution.py:314
  49.2 0.0 collective-permute-start.12
  49.2 5.1 %collective-permute-done.12 = f32[8,128]{1,0:T(8,128)S(1)} collective-permute-done((f32[8,128]{1,0:T(8,128)S(1)}, f32[8,128]{1,0:T(8,128)S(1)}, u32[]{:S(2)}, u32[]{:S(2)}) %collective-permute-start.12) | collective-permute-done | bytes 4128 | tf_op jit(solution)/shard_map/ppermute | solution.py:314
  54.3 7.3 %all-to-all-done = s16[32,72,128]{2,1,0:T(8,128)(2,1)S(1)} async-done(((s16[32,72,128]{2,1,0:T(8,128)(2,1)}), s16[32,72,128]{2,1,0:T(8,128)(2,1)S(1)}, u32[]{:S(2)}, u32[]{:S(2)}) %all-to-all-start) | async-done | bytes 589856 | tf_op jit(solution)/shard_map/all_to_all | solution.py:312
  61.6 0.0 copy-done.2
  61.6 0.0 copy-done.3
  61.6 9.1 %owner.1 = (f32[512,512]{1,0:T(8,128)}, f32[512,512]{1,0:T(8,128)}, s16[2304,128]{1,0:T(8,128)(2,1)S(1)}) custom-call(s16[2304,128]{1,0:T(8,128)(2,1)S(1)} %bitcast.14, f32[512,512]{1,0:T(8,128)S(1)} %bitcast.15, f32[512,512]{1,0:T(8,128)S(1)} %bitcast.16, f32[8,128]{1,0:T(8,128)S(1)} %add.16.total_ref), custom_call_target="tpu_custom_call" | custom-call | tf_op jit(solution)/shard_map/owner/pallas_call | solution.py:315
  70.8 21.4 %all_to_all.22 = s16[32,72,128]{2,1,0:T(8,128)(2,1)S(1)} all-to-all(s16[32,72,128]{2,1,0:T(8,128)(2,1)S(1)} %bitcast.17), channel_id=1, replica_groups=mesh['dp'=8,'shard'=32] {'shard'}, dimensions={0} | all-to-all | bytes 1179648 | tf_op jit(solution)/shard_map/all_to_all | solution.py:324
  92.2 1.8 %update.1 = f32[32,16,512]{2,1,0:T(8,128)} custom-call(s32[32]{0:T(128)S(1)} %dynamic-slice_bitcast_fusion.order_ref.refs_0_, s16[2304,128]{1,0:T(8,128)(2,1)S(1)} %bitcast.13), custom_call_target="tpu_custom_call" | custom-call | tf_op jit(solution)/shard_map/update/pallas_call | solution.py:325
  (4 shorter events, 0.0 us)
Async XLA Ops:
  0.6 20.1 %copy-start = (s32[8,32]{1,0:T(8,128)S(1)}, s32[8,32]{1,0:T(8,128)}, u32[]{:S(2)}) copy-start(s32[8,32]{1,0:T(8,128)} %param.5) | copy-start | bytes 3076
  0.6 2.2 %copy-start.1 = (bf16[1,256,16,512]{3,2,1,0:T(8,128)(2,1)S(1)}, bf16[1,256,16,512]{3,2,1,0:T(8,128)(2,1)}, u32[]{:S(2)}) copy-start(bf16[1,256,16,512]{3,2,1,0:T(8,128)(2,1)} %param.4) | copy-start | bytes 12582916
  2.9 2.0 %collective-permute-start = (bf16[32,16,512]{2,1,0:T(8,128)(2,1)S(1)}, bf16[32,16,512]{2,1,0:T(8,128)(2,1)S(1)}, u32[]{:S(2)}, u32[]{:S(2)}) collective-permute-start(bf16[32,16,512]{2,1,0:T(8,128)(2,1)S(1)} %get-tuple-element.35), channel_id=1, source_target_pairs={{0,32},{32,0},{64,96},{96,64},{128,160},{160,128},{192,224},{224,1... | collective-permute-start | bytes 1572872 | tf_op jit(solution)/shard_map/ppermute | solution.py:275
  4.1 3.9 %collective-permute-start.3 = (bf16[32,16,512]{2,1,0:T(8,128)(2,1)S(1)}, bf16[32,16,512]{2,1,0:T(8,128)(2,1)S(1)}, u32[]{:S(2)}, u32[]{:S(2)}) collective-permute-start(bf16[32,16,512]{2,1,0:T(8,128)(2,1)S(1)} %get-tuple-element.41), channel_id=1, source_target_pairs={{0,32},{32,0},{64,96},{96,64},{128,160},{160,128},{192,224},{224,1... | collective-permute-start | bytes 1572872 | tf_op jit(solution)/shard_map/ppermute | solution.py:275
  4.7 7.5 %collective-permute-start.2 = (bf16[32,16,512]{2,1,0:T(8,128)(2,1)S(1)}, bf16[32,16,512]{2,1,0:T(8,128)(2,1)S(1)}, u32[]{:S(2)}, u32[]{:S(2)}) collective-permute-start(bf16[32,16,512]{2,1,0:T(8,128)(2,1)S(1)} %get-tuple-element.39), channel_id=1, source_target_pairs={{0,32},{32,0},{64,96},{96,64},{128,160},{160,128},{192,224},{224,1... | collective-permute-start | bytes 1572872 | tf_op jit(solution)/shard_map/ppermute | solution.py:275
  5.3 9.8 %collective-permute-start.8 = (s16[1088,128]{1,0:T(8,128)(2,1)S(1)}, s16[1088,128]{1,0:T(8,128)(2,1)S(1)}, u32[]{:S(2)}, u32[]{:S(2)}) collective-permute-start(s16[1088,128]{1,0:T(8,128)(2,1)S(1)} %pair_1_0.2), channel_id=1, source_target_pairs={{0,192},{32,224},{64,0},{96,32},{128,64},{160,96},{192,128},{224,1... | collective-permute-start | bytes 835592 | tf_op jit(solution)/shard_map/ppermute | solution.py:278
  8.1 11.7 %collective-permute-start.4 = (s16[1088,128]{1,0:T(8,128)(2,1)S(1)}, s16[1088,128]{1,0:T(8,128)(2,1)S(1)}, u32[]{:S(2)}, u32[]{:S(2)}) collective-permute-start(s16[1088,128]{1,0:T(8,128)(2,1)S(1)} %pair_0_0.2), channel_id=1, source_target_pairs={{0,64},{32,96},{64,128},{96,160},{128,192},{160,224},{192,0},{224,... | collective-permute-start | bytes 835592 | tf_op jit(solution)/shard_map/ppermute | solution.py:278
  8.1 12.6 %collective-permute-start.1 = (bf16[32,16,512]{2,1,0:T(8,128)(2,1)}, bf16[32,16,512]{2,1,0:T(8,128)(2,1)S(1)}, u32[]{:S(2)}, u32[]{:S(2)}) collective-permute-start(bf16[32,16,512]{2,1,0:T(8,128)(2,1)} %get-tuple-element.37), channel_id=1, source_target_pairs={{0,32},{32,0},{64,96},{96,64},{128,160},{160,128},{192,224},{224,1... | collective-permute-start | bytes 1572872 | tf_op jit(solution)/shard_map/ppermute | solution.py:275
  9.0 52.6 %copy-start.2 = (f32[1,1,512,512]{3,2,1,0:T(8,128)S(1)}, f32[1,1,512,512]{3,2,1,0:T(8,128)}, u32[]{:S(2)}) copy-start(f32[1,1,512,512]{3,2,1,0:T(8,128)} %param.6) | copy-start | bytes 3145732
  9.0 52.6 %copy-start.3 = (f32[1,1,512,512]{3,2,1,0:T(8,128)S(1)}, f32[1,1,512,512]{3,2,1,0:T(8,128)}, u32[]{:S(2)}) copy-start(f32[1,1,512,512]{3,2,1,0:T(8,128)} %param.7) | copy-start | bytes 3145732
  9.0 12.2 %collective-permute-start.6 = (s16[1088,128]{1,0:T(8,128)(2,1)}, s16[1088,128]{1,0:T(8,128)(2,1)S(1)}, u32[]{:S(2)}, u32[]{:S(2)}) collective-permute-start(s16[1088,128]{1,0:T(8,128)(2,1)} %pair_0_0.3), channel_id=1, source_target_pairs={{0,192},{32,224},{64,0},{96,32},{128,64},{160,96},{192,128},{224,1... | collective-permute-start | bytes 835592 | tf_op jit(solution)/shard_map/ppermute | solution.py:278
  13.1 11.4 %collective-permute-start.7 = (s16[1088,128]{1,0:T(8,128)(2,1)}, s16[1088,128]{1,0:T(8,128)(2,1)}, u32[]{:S(2)}, u32[]{:S(2)}) collective-permute-start(s16[1088,128]{1,0:T(8,128)(2,1)} %pair_1_0.3), channel_id=1, source_target_pairs={{0,64},{32,96},{64,128},{96,160},{128,192},{160,224},{192,0},{224,... | collective-permute-start | bytes 835592 | tf_op jit(solution)/shard_map/ppermute | solution.py:278
  16.0 10.4 %collective-permute-start.9 = (s16[1088,128]{1,0:T(8,128)(2,1)}, s16[1088,128]{1,0:T(8,128)(2,1)}, u32[]{:S(2)}, u32[]{:S(2)}) collective-permute-start(s16[1088,128]{1,0:T(8,128)(2,1)} %pair_1_1.1), channel_id=1, source_target_pairs={{0,192},{32,224},{64,0},{96,32},{128,64},{160,96},{192,128},{224,1... | collective-permute-start | bytes 835592 | tf_op jit(solution)/shard_map/ppermute | solution.py:278
  20.7 9.2 %collective-permute-start.5 = (s16[1088,128]{1,0:T(8,128)(2,1)}, s16[1088,128]{1,0:T(8,128)(2,1)}, u32[]{:S(2)}, u32[]{:S(2)}) collective-permute-start(s16[1088,128]{1,0:T(8,128)(2,1)} %pair_0_1.1), channel_id=1, source_target_pairs={{0,64},{32,96},{64,128},{96,160},{128,192},{160,224},{192,0},{224,... | collective-permute-start | bytes 835592 | tf_op jit(solution)/shard_map/ppermute | solution.py:278
  32.9 28.7 %all-to-all-start = ((s16[32,72,128]{2,1,0:T(8,128)(2,1)}), s16[32,72,128]{2,1,0:T(8,128)(2,1)S(1)}, u32[]{:S(2)}, u32[]{:S(2)}) async-start(s16[32,72,128]{2,1,0:T(8,128)(2,1)} %bitcast.2), calls=%async_computation | async-start | bytes 1179648 | tf_op jit(solution)/shard_map/all_to_all | solution.py:312
  44.3 1.3 %collective-permute-start.10 = (f32[8,128]{1,0:T(8,128)S(1)}, f32[8,128]{1,0:T(8,128)S(1)}, u32[]{:S(2)}, u32[]{:S(2)}) collective-permute-start(f32[8,128]{1,0:T(8,128)S(1)} %get-tuple-element.49), channel_id=1, source_target_pairs={{0,32},{32,0},{64,96},{96,64},{128,160},{160,128},{192,224},{224,1... | collective-permute-start | bytes 12296 | tf_op jit(solution)/shard_map/ppermute | solution.py:314
  45.5 3.6 %collective-permute-start.11 = (f32[8,128]{1,0:T(8,128)S(1)}, f32[8,128]{1,0:T(8,128)S(1)}, u32[]{:S(2)}, u32[]{:S(2)}) collective-permute-start(f32[8,128]{1,0:T(8,128)S(1)} %add.14), channel_id=1, source_target_pairs={{0,64},{32,96},{64,0},{96,32},{128,192},{160,224},{192,128},{224,1... | collective-permute-start | bytes 12296 | tf_op jit(solution)/shard_map/ppermute | solution.py:314
  49.2 5.1 %collective-permute-start.12 = (f32[8,128]{1,0:T(8,128)S(1)}, f32[8,128]{1,0:T(8,128)S(1)}, u32[]{:S(2)}, u32[]{:S(2)}) collective-permute-start(f32[8,128]{1,0:T(8,128)S(1)} %add.15), channel_id=1, source_target_pairs={{0,128},{32,160},{64,192},{96,224},{128,0},{160,32},{192,64},{224,... | collective-permute-start | bytes 12296 | tf_op jit(solution)/shard_map/ppermute | solution.py:314

commit v5 on v4

--- a/solution.py
+++ b/solution.py
@@ -25,21 +25,23 @@
     return lax.broadcasted_iota(jnp.int32, (8, 128), 0) < 4
 
 
-def encode_parts(strip):
+def encode_parts(strip, factor=None):
     columns = [strip[:, c : c + 128] for c in range(0, strip.shape[1], 128)]
     top = jnp.abs(columns[0])
     for column in columns[1:]:
         top = jnp.maximum(top, jnp.abs(column))
     top = jnp.maximum(top[:8], top[8:])
-    top = jnp.maximum(jnp.maximum(top, pltpu.roll(top, 4, 0)), 1e-30)
+    top = jnp.maximum(top, pltpu.roll(top, 4, 0))
+    top = jnp.maximum(top if factor is None else top * factor, 1e-30)
     code = jnp.ceil(jnp.log2(top) * STEPS)
     gain = jnp.exp2(code * (-1.0 / STEPS)) * LIMIT
+    gain = gain if factor is None else gain * factor
     gain = jnp.concatenate([gain, gain], axis=0)
     return [jnp.round(column * gain) for column in columns], code
 
 
-def encode(strip, number=None):
-    coded, code = encode_parts(strip)
+def encode(strip, number=None, factor=None):
+    coded, code = encode_parts(strip, factor)
     tail = code if number is None else jnp.where(upper_rows(), code, number)
     return jnp.concatenate(coded + [tail], axis=0).astype(jnp.int32)
 
@@ -103,12 +105,30 @@
 
 
 def dot3(left, right, dims=((1,), (0,))):
+    (lh, ll), (rh, rl) = left, right
+    axis = 1 - dims[0][0]
+    rows = lh.shape[axis]
     dims = (dims, ((), ()))
-    lh, ll = left
-    rh, rl = right
-    out = lax.dot_general(lh, rl, dims, preferred_element_type=f32)
-    out += lax.dot_general(ll, rh, dims, preferred_element_type=f32)
-    return out + lax.dot_general(lh, rh, dims, preferred_element_type=f32)
+    both = lax.dot_general(jnp.concatenate([lh, ll], axis=axis), rh, dims, preferred_element_type=f32)
+    return both[:rows] + (both[rows:] + lax.dot_general(lh, rl, dims, preferred_element_type=f32))
+
+
+def symmetric(left, right, dims=((1,), (0,)), product=None):
+    product = product or dot3
+    (rows,), (columns,) = (1 - dims[0][0],), (1 - dims[1][0],)
+    half = left[0].shape[rows] // 2
+
+    def part(pair, axis, start):
+        return [lax.slice_in_dim(m, start, start + half, axis=axis) for m in pair]
+
+    top = product(part(left, rows, 0), right, dims)
+    corner = product(part(left, rows, half), part(right, columns, half), dims)
+    lower = jnp.concatenate([top[:, half:].T, corner], axis=1)
+    return jnp.concatenate([top, lower], axis=0)
+
+
+def dot1(left, right, dims):
+    return lax.dot_general(left[0], right[0], (dims, ((), ())), preferred_element_type=f32)
 
 
 def eye_like(matrix):
@@ -123,31 +143,22 @@
     norm = jnp.sqrt(jnp.sum(shifted * shifted, keepdims=True))
     u = shifted * (0.2 / norm)
     us = split(u)
-    u2 = dot3(us, us)
+    u2 = symmetric(us, us)
     u2s = split(u2)
-    rest = jnp.dot(u2s[0], (K * u2 - 5.0 * K * u).astype(bf16), preferred_element_type=f32)
+    rest = symmetric(u2s, [(K * u2 - 5.0 * K * u).astype(bf16)], product=dot1)
     inner = 10.0 * K * (u2 - u) + rest
     outer = jnp.where(diagonal, 1.5625, 0.0) - (1.5625 + K) * u + 5.0 * K * u2
-    root = outer + dot3(u2s, split(inner))
+    root = outer + symmetric(u2s, split(inner))
     return root * lax.rsqrt(jnp.sqrt(norm))
 
 
-def invert(order_ref, slot_ref):
-    def step(j, _):
-        slot_ref[order_ref[j]] = j
-        return 0
-
-    lax.fori_loop(0, order_ref.shape[0], step, 0)
-
-
-def cut_kernel(aheads, source_ref, *refs):
+def cut_kernel(wanted, source_ref, *refs):
     group, (*outs, done) = lax.axis_index("dp"), refs
     chips = source_ref.shape[0] // 2
     copies = []
-    for n, ahead in enumerate(aheads):
-        base = 2 * ((group // 2 + ahead) % chips)
-        for k, core in enumerate((group % 2, 1 - group % 2)):
-            copies.append(pltpu.make_async_copy(source_ref.at[base + core], outs[2 * n + k], done.at[2 * n + k]))
+    for n, (ahead, other) in enumerate(wanted):
+        index = 2 * ((group // 2 + ahead) % chips) + (group % 2 + other) % 2
+        copies.append(pltpu.make_async_copy(source_ref.at[index], outs[n], done.at[n]))
     for copy in copies:
         copy.start()
     for copy in copies:
@@ -164,9 +175,10 @@
         refs[-1][QUAD * q : QUAD * (q + 1), :] = encode_four(strips)
 
 
-def sum_kernel(order_ref, own_ref, other_ref, *refs):
-    part_refs, (out_ref, square_ref, slot_ref, coded_ref) = refs[:4], refs[4:]
-    invert(order_ref, slot_ref)
+def sum_kernel(owned_ref, own_ref, other_ref, *refs):
+    part_refs, (out_ref, square_ref, order_ref, coded_ref, done) = refs[:4], refs[4:]
+    fetch = pltpu.make_async_copy(owned_ref.at[lax.axis_index("dp")], order_ref, done)
+    fetch.start()
     total = jnp.zeros((8, 128), f32)
     quads = own_ref.shape[0] // 4
     for q in range(quads):
@@ -180,10 +192,11 @@
             for column in columns:
                 square = column * column
                 total += square[:8] + square[8:]
-            coded_ref[slot_ref[b]] = encode(jnp.concatenate(columns, axis=1))
+            coded_ref[b] = encode(jnp.concatenate(columns, axis=1))
     square_ref[...] = jnp.broadcast_to(jnp.sum(total, keepdims=True), total.shape)
+    fetch.wait()
     for p in range(coded_ref.shape[0] // 2):
-        store(out_ref, p, coded_ref[2 * p], coded_ref[2 * p + 1])
+        store(out_ref, p, coded_ref[order_ref[2 * p]], coded_ref[order_ref[2 * p + 1]])
 
 
 def owner_kernel(coded_ref, left_in, right_in, total_ref, left_out, right_out, out_ref, *scratch):
@@ -202,8 +215,8 @@
     grad = split(grad_ref[...])
     for copy in reads:
         copy.wait()
-    left_ref[...] = 0.95 * left_ref[...] + dot3(grad, grad, ((1,), (1,))) * (1.0 / order)
-    right_ref[...] = 0.95 * right_ref[...] + dot3(grad, grad, ((0,), (0,))) * (1.0 / order)
+    left_ref[...] = 0.95 * left_ref[...] + symmetric(grad, grad, ((1,), (1,))) * (1.0 / order)
+    right_ref[...] = 0.95 * right_ref[...] + symmetric(grad, grad, ((0,), (0,))) * (1.0 / order)
     writes = [pltpu.make_async_copy(a, b, done.at[i]) for i, (a, b) in enumerate([(left_ref, left_out), (right_ref, right_out)])]
     for copy in writes:
         copy.start()
@@ -212,21 +225,27 @@
     cells = 1.0 / (order * order)
     mean = jnp.sum(shaped * shaped, keepdims=True) * cells
     graft = jnp.sqrt(jnp.sum(square, keepdims=True) * cells + EPS) / jnp.sqrt(mean + EPS)
-    grad_ref[...] = shaped * graft
+    grad_ref[...] = shaped
     number = encode_number(total_ref[...])
     for p in range(order // 32):
         rows = 32 * p
         store(
             out_ref,
             p,
-            encode(grad_ref[rows : rows + 16, :], number),
-            encode(grad_ref[rows + 16 : rows + 32, :], number),
+            encode(grad_ref[rows : rows + 16, :], number, graft),
+            encode(grad_ref[rows + 16 : rows + 32, :], number, graft),
         )
     for copy in writes:
         copy.wait()
 
 
-def update_kernel(cells, order_ref, coded_ref, out_ref, wide_ref, done):
+def add_kernel(first_ref, second_ref, out_ref):
+    out_ref[...] = first_ref[...] + second_ref[...]
+
+
+def update_kernel(cells, owned_ref, coded_ref, out_ref, order_ref, wide_ref, done, fetched):
+    fetch = pltpu.make_async_copy(owned_ref.at[lax.axis_index("dp")], order_ref, fetched)
+    fetch.start()
     total = jnp.zeros((1, 128), f32)
     for p in range(wide_ref.shape[0] // 2):
         base = 2 * ROWS * p
@@ -234,6 +253,7 @@
         second = coded_ref[base + 128 : base + 144, :].astype(jnp.int32).astype(f32)[8:]
         total += decode_number(first) + decode_number(second)
     layer = 1.0 / jnp.sqrt(total * (1.0 / cells) + EPS)
+    fetch.wait()
     copies = []
     for p in range(wide_ref.shape[0] // 2):
         for i, coded in enumerate(load(coded_ref, p)):
@@ -248,27 +268,24 @@
 
 def body(grads, owned, left_stat, right_stat):
     shards, groups = lax.axis_size("shard"), lax.axis_size("dp")
-    group = lax.axis_index("dp")
     blocks, strip, width = grads.shape[1:]
-    core, chip, chips = group % 2, group // 2, groups // 2
-    mine = lax.dynamic_index_in_dim(owned, group, 0, keepdims=False)
+    chips = groups // 2
     square = jax.ShapeDtypeStruct((width, width), f32)
-    halves = jax.ShapeDtypeStruct((width, width), bf16)
     wire = jax.ShapeDtypeStruct((shards * ROWS, 128), jnp.int16)
     grouped = grads[0].reshape(groups, shards, strip, width)
     swap = [(d, d ^ 1) for d in range(groups)]
     half_wire = pltpu.VMEM((shards // 8 * QUAD, 128), jnp.int16)
     number = jax.ShapeDtypeStruct((8, 128), f32)
 
-    def cut(source, *aheads):
+    def cut(mebibytes, source, *wanted):
         return pl.pallas_call(
-            lambda *refs: cut_kernel([ahead % chips for ahead in aheads], *refs),
-            in_specs=[pl.BlockSpec(memory_space=pltpu.HBM)],
-            out_specs=[VMEM] * (2 * len(aheads)),
-            out_shape=[pltpu.VMEM((shards, strip, width), bf16)] * (2 * len(aheads)),
-            scratch_shapes=[pltpu.SemaphoreType.DMA((2 * len(aheads),))],
-            compiler_params=params(4),
-            name=f"cut_{len(aheads)}",
+            lambda *refs: cut_kernel([(ahead % chips, other) for ahead, other in wanted], *refs),
+            in_specs=[ANY],
+            out_specs=[VMEM] * len(wanted),
+            out_shape=[pltpu.VMEM((shards, strip, width), bf16)] * len(wanted),
+            scratch_shapes=[pltpu.SemaphoreType.DMA((len(wanted),))],
+            compiler_params=params(mebibytes),
+            name=f"cut_{len(wanted)}",
         )(source)
 
     def partner(array):
@@ -287,12 +304,12 @@
             name=f"pair_{half}_{len(parts)}",
         )(own, other, *parts)
 
-    held, far = lax.optimization_barrier((grouped, cut(grouped, 2)))
-    far = far[0], partner(far[1])
-    rest = cut(held, 1, -1, 0)
-    others = [partner(rest[2 * n + 1]) for n in range(3)]
-    left_relay, right_relay = pair_sum(0, *far), pair_sum(1, *far)
-    owns, left_relay, right_relay = lax.optimization_barrier((rest[::2], left_relay, right_relay))
+    held, far = lax.optimization_barrier((grouped, cut(60, grouped, (2, 1))))
+    far = partner(*far)
+    own, *rest = cut(57, held, (2, 0), (1, 1), (-1, 1), (0, 1), (1, 0), (-1, 0), (0, 0))
+    others = [partner(array) for array in rest[:3]]
+    left_relay, right_relay = pair_sum(0, own, far), pair_sum(1, own, far)
+    owns, left_relay, right_relay = lax.optimization_barrier((rest[3:], left_relay, right_relay))
     ahead, behind, here = zip(owns, others)
     left_relay, right_relay = along(1, left_relay), along(-1, right_relay)
     left_direct, right_direct = pair_sum(1, *ahead), pair_sum(0, *behind)
@@ -302,16 +319,28 @@
     right_summed = along(-1, pair_sum(1, *behind, right_relay))
     strips, total = pl.pallas_call(
         sum_kernel,
-        in_specs=[SMEM] + [VMEM] * 6,
+        in_specs=[ANY] + [VMEM] * 6,
         out_specs=[VMEM] * 2,
-        scratch_shapes=[pltpu.SMEM((shards,), jnp.int32), pltpu.VMEM((shards, ROWS, 128), jnp.int32)],
-        out_shape=[wire, number],
+        scratch_shapes=[
+            pltpu.SMEM((shards,), jnp.int32),
+            pltpu.VMEM((shards, ROWS, 128), jnp.int32),
+            pltpu.SemaphoreType.DMA,
+        ],
+        out_shape=[pltpu.VMEM(wire.shape, wire.dtype), number],
         compiler_params=params(8),
         name="sum_strips",
-    )(mine, *here, left_summed, right_direct, left_direct, right_summed)
+    )(owned, *here, left_summed, right_direct, left_direct, right_summed)
     strips = lax.all_to_all(strips, "shard", split_axis=0, concat_axis=0, tiled=True)
     for bit in (1, 2, 4):
-        total += lax.ppermute(total, "dp", [(d, d ^ bit) for d in range(groups)])
+        other = lax.ppermute(total, "dp", [(d, d ^ bit) for d in range(groups)])
+        total = pl.pallas_call(
+            add_kernel,
+            in_specs=[VMEM] * 2,
+            out_specs=VMEM,
+            out_shape=number,
+            compiler_params=params(1),
+            name=f"add_{bit}",
+        )(total, other)
     left_fresh, right_fresh, pieces = pl.pallas_call(
         owner_kernel,
         in_specs=[VMEM, ANY, ANY, VMEM],
@@ -324,13 +353,18 @@
     pieces = lax.all_to_all(pieces, "shard", split_axis=0, concat_axis=0, tiled=True)
     update = pl.pallas_call(
         lambda *refs: update_kernel(blocks * width * width, *refs),
-        in_specs=[SMEM, VMEM],
+        in_specs=[ANY, VMEM],
         out_specs=ANY,
         out_shape=jax.ShapeDtypeStruct((shards, strip, width), f32),
-        scratch_shapes=[pltpu.VMEM((shards, strip, width), f32), pltpu.SemaphoreType.DMA((shards,))],
+        scratch_shapes=[
+            pltpu.SMEM((shards,), jnp.int32),
+            pltpu.VMEM((shards, strip, width), f32),
+            pltpu.SemaphoreType.DMA((shards,)),
+            pltpu.SemaphoreType.DMA,
+        ],
         compiler_params=params(8),
         name="update",
-    )(mine, pieces)
+    )(owned, pieces)
     return update, left_fresh[None, None], right_fresh[None, None]
 
 

time: 94.8 us -> 94.5 us (level)
  waiting for transfers between devices: 28.6 us -> 32.1 us
  Pallas kernels: 19.1 us -> 16.1 us
  local copies, waits for them, and re-layouts: 2.21 us -> 0.02 us
  blocking collectives: 21.4 us -> 22.9 us
    pallas_call x6, Pallas kernels: 3.93 us -> 1.1 us  [pair_sum(): pl.pallas_call(lambda *refs: pair_kernel(half * shards // 2, *refs), in_s...]
    ppermute x6, waiting for transfers between devices: 11.2 us -> 13.7 us  [along(): lax.ppermute(array, 'dp', [(d, (d + 2 * ahead) % groups) for d in range(g...]
    unnamed x8 -> x6, local copies, waits for them, and re-layouts: 2.2 us -> 0.02 us
    all_to_all x1, blocking collectives: 21.4 us -> 22.9 us  [body(): lax.all_to_all(pieces, 'shard', split_axis=0, concat_axis=0, tiled=True)]
    all_to_all x1, waiting for transfers between devices: 7.33 us -> 8.45 us  [body(): lax.all_to_all(strips, 'shard', split_axis=0, concat_axis=0, tiled=True)]
    pallas_call x1, Pallas kernels: 9.14 us -> 8.06 us  [body(): pl.pallas_call(owner_kernel, in_specs=[VMEM, ANY, ANY, VMEM], out_specs=[...]
    pallas_call x3 -> x6, Pallas kernels: 4.21 us -> 5.14 us  [the longest x2 3.15 us: cut(): pl.pallas_call(lambda *refs: cut_kernel([(ahead % chips, other) for ahead...]
  transfers between devices with their start and end apart: 14 -> 14, of which waited for: 10 -> 9; matrix products, arithmetic and copies ran while one was open for 0% -> 0% of each run, Pallas kernels for 5% -> 3%
where the time goes in v5:
time: 94.5 us; the launch traced here: 94.3 us
  waiting for transfers between devices  32.1 us (34%)
  blocking collectives  22.9 us (24%)
  starting transfers between devices  22.3 us (24%)
  Pallas kernels  16.1 us (17%)
    all_to_all x1, blocking collectives, body(): lax.all_to_all(pieces, 'shard', split_axis=0, concat_axis=0, tiled=True)  22.9 us
    ppermute x6, waiting for transfers between devices, along(): lax.ppermute(array, 'dp', [(d, (d + 2 * ahead) % groups) for d in range(g...  13.7 us
    all_to_all x1, starting transfers between devices, body(): lax.all_to_all(strips, 'shard', split_axis=0, concat_axis=0, tiled=True)  11.4 us
    ppermute x6, starting transfers between devices, along(): lax.ppermute(array, 'dp', [(d, (d + 2 * ahead) % groups) for d in range(g...  9.94 us
    ppermute x3, waiting for transfers between devices, body(): other = lax.ppermute(total, 'dp', [(d, d ^ bit) for d in range(groups)])  9.87 us
    all_to_all x1, waiting for transfers between devices, body(): lax.all_to_all(strips, 'shard', split_axis=0, concat_axis=0, tiled=True)  8.45 us
    pallas_call x1, Pallas kernels, body(): pl.pallas_call(owner_kernel, in_specs=[VMEM, ANY, ANY, VMEM], out_specs=[...  8.06 us
    pallas_call x2, Pallas kernels, cut(): pl.pallas_call(lambda *refs: cut_kernel([(ahead % chips, other) for ahead...  3.15 us
  transfers between devices with their start and end apart: 14, of which 9 were waited for; matrix products, arithmetic and copies ran while one was open for 0% of the time, Pallas kernels for 3%

profile of v5, /device:TPU:32, one launch (start us, length us, event | category | flops | bytes accessed | tf_op | source)
XLA Modules:
  0.0 94.3 jit_solution(10832648788046894055)
XLA Ops:
  0.6 1.1 %cut_1.1 = bf16[32,16,512]{2,1,0:T(8,128)(2,1)S(1)} custom-call(bf16[8,32,16,512]{3,2,1,0:T(8,128)(2,1)} %bitcast.14), custom_call_target="tpu_custom_call" | custom-call | tf_op jit(solution)/shard_map/cut_1/pallas_call | solution.py:281
  1.7 0.1 collective-permute-start
  1.8 2.1 %cut_7.1 = (bf16[32,16,512]{2,1,0:T(8,128)(2,1)S(1)}, bf16[32,16,512]{2,1,0:T(8,128)(2,1)S(1)}, bf16[32,16,512]{2,1,0:T(8,128)(2,1)S(1)}, bf16[32,16,512]{2,1,0:...) custom-call(bf16[8,32,16,512]{3,2,1,0:T(8,128)(2,1)} %bitcast.15), custom_call_target="tpu_custom_call" | custom-call | tf_op jit(solution)/shard_map/cut_7/pallas_call | solution.py:281
  3.9 0.6 collective-permute-start.3
  4.4 0.1 collective-permute-start.2
  4.5 0.0 collective-permute-done.refs_1_
  4.6 0.0 copy-start.2
  4.6 0.2 pair_1_0.2
  4.7 0.2 pair_0_0.2
  4.9 2.8 %collective-permute-start.8 = (s16[1088,128]{1,0:T(8,128)(2,1)S(1)}, s16[1088,128]{1,0:T(8,128)(2,1)S(1)}, u32[]{:S(2)}, u32[]{:S(2)}) collective-permute-start(s16[1088,128]{1,0:T(8,128)(2,1)S(1)} %pair_1_0.2), channel_id=1, source_target_pairs={{0,192},{32,224},{64,0},{96,32},{128,64},{160,96},{192,128},{224,1... | collective-permute-start | bytes 835592 | tf_op jit(solution)/shard_map/ppermute | solution.py:295
  7.7 0.0 collective-permute-start.4
  7.7 0.1 collective-permute-start.1
  7.9 0.0 collective-permute-done.3.refs_1_
  7.9 0.2 pair_0_0.3
  8.0 0.0 copy-start
  8.0 0.0 copy-start.1
  8.0 3.2 %collective-permute-start.6 = (s16[1088,128]{1,0:T(8,128)(2,1)S(1)}, s16[1088,128]{1,0:T(8,128)(2,1)S(1)}, u32[]{:S(2)}, u32[]{:S(2)}) collective-permute-start(s16[1088,128]{1,0:T(8,128)(2,1)S(1)} %pair_0_0.3), channel_id=1, source_target_pairs={{0,192},{32,224},{64,0},{96,32},{128,64},{160,96},{192,128},{224,1... | collective-permute-start | bytes 835592 | tf_op jit(solution)/shard_map/ppermute | solution.py:295
  11.2 0.0 collective-permute-done.2.refs_1_
  11.2 0.2 pair_1_0.3
  11.4 0.1 collective-permute-start.7
  11.5 3.2 %collective-permute-done.8.refs_2_ = s16[1088,128]{1,0:T(8,128)(2,1)S(1)} collective-permute-done((s16[1088,128]{1,0:T(8,128)(2,1)S(1)}, s16[1088,128]{1,0:T(8,128)(2,1)S(1)}, u32[]{:S(2)}, u32[]{:S(2)}) %collective-permute-start.8) | collective-permute-done | bytes 278560 | tf_op jit(solution)/shard_map/ppermute | solution.py:295
  14.7 0.2 pair_1_1.1
  14.9 3.8 %collective-permute-start.9 = (s16[1088,128]{1,0:T(8,128)(2,1)S(1)}, s16[1088,128]{1,0:T(8,128)(2,1)S(1)}, u32[]{:S(2)}, u32[]{:S(2)}) collective-permute-start(s16[1088,128]{1,0:T(8,128)(2,1)S(1)} %pair_1_1.1), channel_id=1, source_target_pairs={{0,192},{32,224},{64,0},{96,32},{128,64},{160,96},{192,128},{224,1... | collective-permute-start | bytes 835592 | tf_op jit(solution)/shard_map/ppermute | solution.py:295
  18.7 0.0 collective-permute-done.4.refs_2_
  18.7 0.2 pair_0_1.1
  19.0 0.1 collective-permute-start.5
  19.0 0.0 collective-permute-done.1.other_ref
  19.1 1.6 %collective-permute-done.6.refs_1_ = s16[1088,128]{1,0:T(8,128)(2,1)S(1)} collective-permute-done((s16[1088,128]{1,0:T(8,128)(2,1)S(1)}, s16[1088,128]{1,0:T(8,128)(2,1)S(1)}, u32[]{:S(2)}, u32[]{:S(2)}) %collective-permute-start.6) | collective-permute-done | bytes 278560 | tf_op jit(solution)/shard_map/ppermute | solution.py:295
  20.7 3.7 %collective-permute-done.7.refs_2_ = s16[1088,128]{1,0:T(8,128)(2,1)S(1)} collective-permute-done((s16[1088,128]{1,0:T(8,128)(2,1)S(1)}, s16[1088,128]{1,0:T(8,128)(2,1)S(1)}, u32[]{:S(2)}, u32[]{:S(2)}) %collective-permute-start.7) | collective-permute-done | bytes 278560 | tf_op jit(solution)/shard_map/ppermute | solution.py:295
  24.4 1.8 %collective-permute-done.9.refs_3_ = s16[1088,128]{1,0:T(8,128)(2,1)S(1)} collective-permute-done((s16[1088,128]{1,0:T(8,128)(2,1)S(1)}, s16[1088,128]{1,0:T(8,128)(2,1)S(1)}, u32[]{:S(2)}, u32[]{:S(2)}) %collective-permute-start.9) | collective-permute-done | bytes 278560 | tf_op jit(solution)/shard_map/ppermute | solution.py:295
  26.2 3.4 %collective-permute-done.5.refs_0_ = s16[1088,128]{1,0:T(8,128)(2,1)S(1)} collective-permute-done((s16[1088,128]{1,0:T(8,128)(2,1)S(1)}, s16[1088,128]{1,0:T(8,128)(2,1)S(1)}, u32[]{:S(2)}, u32[]{:S(2)}) %collective-permute-start.5) | collective-permute-done | bytes 278560 | tf_op jit(solution)/shard_map/ppermute | solution.py:295
  29.6 0.0 copy-done.2
  29.6 2.0 %sum_strips.1 = (s16[2304,128]{1,0:T(8,128)(2,1)}, f32[8,128]{1,0:T(8,128)S(1)}) custom-call(s32[8,32]{1,0:T(8,128)S(1)} %copy-done.2, bf16[32,16,512]{2,1,0:T(8,128)(2,1)S(1)} %get-tuple-element.32.own_ref, bf16[32,16,512]{2,1,0:T(8,128)(2,1)S(1)} %collective-permute-done.1.other_ref, s16[1088,128]{1,0:T(8,128)(2,1)S(1)} %collective-permute-done.5.refs_0_, ...), custom_call_target="tpu_custom_call" | custom-call | tf_op jit(solution)/shard_map/sum_strips/pallas_call | solution.py:320
  31.6 11.4 %all-to-all-start = ((s16[32,72,128]{2,1,0:T(8,128)(2,1)}), s16[32,72,128]{2,1,0:T(8,128)(2,1)S(1)}, u32[]{:S(2)}, u32[]{:S(2)}) async-start(s16[32,72,128]{2,1,0:T(8,128)(2,1)} %bitcast.1), calls=%async_computation | async-start | bytes 1179648 | tf_op jit(solution)/shard_map/all_to_all | solution.py:333
  42.9 0.1 collective-permute-start.10
  43.0 1.2 %collective-permute-done.10.second_ref = f32[8,128]{1,0:T(8,128)S(1)} collective-permute-done((f32[8,128]{1,0:T(8,128)S(1)}, f32[8,128]{1,0:T(8,128)S(1)}, u32[]{:S(2)}, u32[]{:S(2)}) %collective-permute-start.10) | collective-permute-done | bytes 4128 | tf_op jit(solution)/shard_map/ppermute | solution.py:335
  44.2 0.0 collective-permute-start.11
  44.2 3.6 %collective-permute-done.11.second_ref = f32[8,128]{1,0:T(8,128)S(1)} collective-permute-done((f32[8,128]{1,0:T(8,128)S(1)}, f32[8,128]{1,0:T(8,128)S(1)}, u32[]{:S(2)}, u32[]{:S(2)}) %collective-permute-start.11) | collective-permute-done | bytes 4128 | tf_op jit(solution)/shard_map/ppermute | solution.py:335
  47.8 0.0 collective-permute-start.12
  47.8 5.1 %collective-permute-done.12.second_ref = f32[8,128]{1,0:T(8,128)S(1)} collective-permute-done((f32[8,128]{1,0:T(8,128)S(1)}, f32[8,128]{1,0:T(8,128)S(1)}, u32[]{:S(2)}, u32[]{:S(2)}) %collective-permute-start.12) | collective-permute-done | bytes 4128 | tf_op jit(solution)/shard_map/ppermute | solution.py:335
  52.9 8.4 %all-to-all-done = s16[32,72,128]{2,1,0:T(8,128)(2,1)S(1)} async-done(((s16[32,72,128]{2,1,0:T(8,128)(2,1)}), s16[32,72,128]{2,1,0:T(8,128)(2,1)S(1)}, u32[]{:S(2)}, u32[]{:S(2)}) %all-to-all-start) | async-done | bytes 589856 | tf_op jit(solution)/shard_map/all_to_all | solution.py:333
  61.4 0.0 copy-done
  61.4 0.0 copy-done.1
  61.4 8.1 %owner.1 = (f32[512,512]{1,0:T(8,128)}, f32[512,512]{1,0:T(8,128)}, s16[2304,128]{1,0:T(8,128)(2,1)S(1)}) custom-call(s16[2304,128]{1,0:T(8,128)(2,1)S(1)} %bitcast.10, f32[512,512]{1,0:T(8,128)S(1)} %bitcast.11, f32[512,512]{1,0:T(8,128)S(1)} %bitcast.12, f32[8,128]{1,0:T(8,128)S(1)} %add_4.1.total_ref), custom_call_target="tpu_custom_call" | custom-call | tf_op jit(solution)/shard_map/owner/pallas_call | solution.py:344
  69.4 22.9 %all_to_all.22 = s16[32,72,128]{2,1,0:T(8,128)(2,1)S(1)} all-to-all(s16[32,72,128]{2,1,0:T(8,128)(2,1)S(1)} %bitcast.13), channel_id=1, replica_groups=mesh['dp'=8,'shard'=32] {'shard'}, dimensions={0} | all-to-all | bytes 1179648 | tf_op jit(solution)/shard_map/all_to_all | solution.py:353
  92.3 1.8 %update.1 = f32[32,16,512]{2,1,0:T(8,128)} custom-call(s32[8,32]{1,0:T(8,128)S(1)} %copy-done.2, s16[2304,128]{1,0:T(8,128)(2,1)S(1)} %bitcast.9), custom_call_target="tpu_custom_call" | custom-call | tf_op jit(solution)/shard_map/update/pallas_call | solution.py:354
  (3 shorter events, 0.0 us)
Async XLA Ops:
  1.7 2.8 %collective-permute-start = (bf16[32,16,512]{2,1,0:T(8,128)(2,1)S(1)}, bf16[32,16,512]{2,1,0:T(8,128)(2,1)S(1)}, u32[]{:S(2)}, u32[]{:S(2)}) collective-permute-start(bf16[32,16,512]{2,1,0:T(8,128)(2,1)S(1)} %cut_1.1), channel_id=1, source_target_pairs={{0,32},{32,0},{64,96},{96,64},{128,160},{160,128},{192,224},{224,1... | collective-permute-start | bytes 1572872 | tf_op jit(solution)/shard_map/ppermute | solution.py:292
  3.9 4.0 %collective-permute-start.3 = (bf16[32,16,512]{2,1,0:T(8,128)(2,1)S(1)}, bf16[32,16,512]{2,1,0:T(8,128)(2,1)S(1)}, u32[]{:S(2)}, u32[]{:S(2)}) collective-permute-start(bf16[32,16,512]{2,1,0:T(8,128)(2,1)S(1)} %get-tuple-element.37), channel_id=1, source_target_pairs={{0,32},{32,0},{64,96},{96,64},{128,160},{160,128},{192,224},{224,1... | collective-permute-start | bytes 1572872 | tf_op jit(solution)/shard_map/ppermute | solution.py:292
  4.4 6.8 %collective-permute-start.2 = (bf16[32,16,512]{2,1,0:T(8,128)(2,1)S(1)}, bf16[32,16,512]{2,1,0:T(8,128)(2,1)S(1)}, u32[]{:S(2)}, u32[]{:S(2)}) collective-permute-start(bf16[32,16,512]{2,1,0:T(8,128)(2,1)S(1)} %get-tuple-element.35), channel_id=1, source_target_pairs={{0,32},{32,0},{64,96},{96,64},{128,160},{160,128},{192,224},{224,1... | collective-permute-start | bytes 1572872 | tf_op jit(solution)/shard_map/ppermute | solution.py:292
  4.6 25.0 %copy-start.2 = (s32[8,32]{1,0:T(8,128)S(1)}, s32[8,32]{1,0:T(8,128)}, u32[]{:S(2)}) copy-start(s32[8,32]{1,0:T(8,128)} %refs_0_.1) | copy-start | bytes 3076
  4.9 9.8 %collective-permute-start.8 = (s16[1088,128]{1,0:T(8,128)(2,1)S(1)}, s16[1088,128]{1,0:T(8,128)(2,1)S(1)}, u32[]{:S(2)}, u32[]{:S(2)}) collective-permute-start(s16[1088,128]{1,0:T(8,128)(2,1)S(1)} %pair_1_0.2), channel_id=1, source_target_pairs={{0,192},{32,224},{64,0},{96,32},{128,64},{160,96},{192,128},{224,1... | collective-permute-start | bytes 835592 | tf_op jit(solution)/shard_map/ppermute | solution.py:295
  7.7 11.0 %collective-permute-start.4 = (s16[1088,128]{1,0:T(8,128)(2,1)S(1)}, s16[1088,128]{1,0:T(8,128)(2,1)S(1)}, u32[]{:S(2)}, u32[]{:S(2)}) collective-permute-start(s16[1088,128]{1,0:T(8,128)(2,1)S(1)} %pair_0_0.2), channel_id=1, source_target_pairs={{0,64},{32,96},{64,128},{96,160},{128,192},{160,224},{192,0},{224,... | collective-permute-start | bytes 835592 | tf_op jit(solution)/shard_map/ppermute | solution.py:295
  7.7 11.3 %collective-permute-start.1 = (bf16[32,16,512]{2,1,0:T(8,128)(2,1)S(1)}, bf16[32,16,512]{2,1,0:T(8,128)(2,1)S(1)}, u32[]{:S(2)}, u32[]{:S(2)}) collective-permute-start(bf16[32,16,512]{2,1,0:T(8,128)(2,1)S(1)} %get-tuple-element.33), channel_id=1, source_target_pairs={{0,32},{32,0},{64,96},{96,64},{128,160},{160,128},{192,224},{224,1... | collective-permute-start | bytes 1572872 | tf_op jit(solution)/shard_map/ppermute | solution.py:292
  8.0 53.4 %copy-start = (f32[1,1,512,512]{3,2,1,0:T(8,128)S(1)}, f32[1,1,512,512]{3,2,1,0:T(8,128)}, u32[]{:S(2)}) copy-start(f32[1,1,512,512]{3,2,1,0:T(8,128)} %param.6) | copy-start | bytes 3145732
  8.0 53.4 %copy-start.1 = (f32[1,1,512,512]{3,2,1,0:T(8,128)S(1)}, f32[1,1,512,512]{3,2,1,0:T(8,128)}, u32[]{:S(2)}) copy-start(f32[1,1,512,512]{3,2,1,0:T(8,128)} %param.7) | copy-start | bytes 3145732
  8.0 12.6 %collective-permute-start.6 = (s16[1088,128]{1,0:T(8,128)(2,1)S(1)}, s16[1088,128]{1,0:T(8,128)(2,1)S(1)}, u32[]{:S(2)}, u32[]{:S(2)}) collective-permute-start(s16[1088,128]{1,0:T(8,128)(2,1)S(1)} %pair_0_0.3), channel_id=1, source_target_pairs={{0,192},{32,224},{64,0},{96,32},{128,64},{160,96},{192,128},{224,1... | collective-permute-start | bytes 835592 | tf_op jit(solution)/shard_map/ppermute | solution.py:295
  11.4 13.0 %collective-permute-start.7 = (s16[1088,128]{1,0:T(8,128)(2,1)S(1)}, s16[1088,128]{1,0:T(8,128)(2,1)S(1)}, u32[]{:S(2)}, u32[]{:S(2)}) collective-permute-start(s16[1088,128]{1,0:T(8,128)(2,1)S(1)} %pair_1_0.3), channel_id=1, source_target_pairs={{0,64},{32,96},{64,128},{96,160},{128,192},{160,224},{192,0},{224,... | collective-permute-start | bytes 835592 | tf_op jit(solution)/shard_map/ppermute | solution.py:295
  14.9 11.2 %collective-permute-start.9 = (s16[1088,128]{1,0:T(8,128)(2,1)S(1)}, s16[1088,128]{1,0:T(8,128)(2,1)S(1)}, u32[]{:S(2)}, u32[]{:S(2)}) collective-permute-start(s16[1088,128]{1,0:T(8,128)(2,1)S(1)} %pair_1_1.1), channel_id=1, source_target_pairs={{0,192},{32,224},{64,0},{96,32},{128,64},{160,96},{192,128},{224,1... | collective-permute-start | bytes 835592 | tf_op jit(solution)/shard_map/ppermute | solution.py:295
  19.0 10.6 %collective-permute-start.5 = (s16[1088,128]{1,0:T(8,128)(2,1)S(1)}, s16[1088,128]{1,0:T(8,128)(2,1)S(1)}, u32[]{:S(2)}, u32[]{:S(2)}) collective-permute-start(s16[1088,128]{1,0:T(8,128)(2,1)S(1)} %pair_0_1.1), channel_id=1, source_target_pairs={{0,64},{32,96},{64,128},{96,160},{128,192},{160,224},{192,0},{224,... | collective-permute-start | bytes 835592 | tf_op jit(solution)/shard_map/ppermute | solution.py:295
  31.6 29.8 %all-to-all-start = ((s16[32,72,128]{2,1,0:T(8,128)(2,1)}), s16[32,72,128]{2,1,0:T(8,128)(2,1)S(1)}, u32[]{:S(2)}, u32[]{:S(2)}) async-start(s16[32,72,128]{2,1,0:T(8,128)(2,1)} %bitcast.1), calls=%async_computation | async-start | bytes 1179648 | tf_op jit(solution)/shard_map/all_to_all | solution.py:333
  42.9 1.3 %collective-permute-start.10 = (f32[8,128]{1,0:T(8,128)S(1)}, f32[8,128]{1,0:T(8,128)S(1)}, u32[]{:S(2)}, u32[]{:S(2)}) collective-permute-start(f32[8,128]{1,0:T(8,128)S(1)} %get-tuple-element.45.first_ref), channel_id=1, source_target_pairs={{0,32},{32,0},{64,96},{96,64},{128,160},{160,128},{192,224},{224,1... | collective-permute-start | bytes 12296 | tf_op jit(solution)/shard_map/ppermute | solution.py:335
  44.2 3.6 %collective-permute-start.11 = (f32[8,128]{1,0:T(8,128)S(1)}, f32[8,128]{1,0:T(8,128)S(1)}, u32[]{:S(2)}, u32[]{:S(2)}) collective-permute-start(f32[8,128]{1,0:T(8,128)S(1)} %add_1.1.first_ref), channel_id=1, source_target_pairs={{0,64},{32,96},{64,0},{96,32},{128,192},{160,224},{192,128},{224,1... | collective-permute-start | bytes 12296 | tf_op jit(solution)/shard_map/ppermute | solution.py:335
  47.8 5.1 %collective-permute-start.12 = (f32[8,128]{1,0:T(8,128)S(1)}, f32[8,128]{1,0:T(8,128)S(1)}, u32[]{:S(2)}, u32[]{:S(2)}) collective-permute-start(f32[8,128]{1,0:T(8,128)S(1)} %add_2.1.first_ref), channel_id=1, source_target_pairs={{0,128},{32,160},{64,192},{96,224},{128,0},{160,32},{192,64},{224,... | collective-permute-start | bytes 12296 | tf_op jit(solution)/shard_map/ppermute | solution.py:335

commit v6 on v5

--- a/solution.py
+++ b/solution.py
@@ -176,7 +176,7 @@
 
 
 def sum_kernel(owned_ref, own_ref, other_ref, *refs):
-    part_refs, (out_ref, square_ref, order_ref, coded_ref, done) = refs[:4], refs[4:]
+    part_refs, (out_ref, square_ref, order_ref, coded_ref, packed_ref, done, sent) = refs[:4], refs[4:]
     fetch = pltpu.make_async_copy(owned_ref.at[lax.axis_index("dp")], order_ref, done)
     fetch.start()
     total = jnp.zeros((8, 128), f32)
@@ -195,8 +195,15 @@
             coded_ref[b] = encode(jnp.concatenate(columns, axis=1))
     square_ref[...] = jnp.broadcast_to(jnp.sum(total, keepdims=True), total.shape)
     fetch.wait()
+    copies = []
     for p in range(coded_ref.shape[0] // 2):
-        store(out_ref, p, coded_ref[order_ref[2 * p]], coded_ref[order_ref[2 * p + 1]])
+        store(packed_ref, p, coded_ref[order_ref[2 * p]], coded_ref[order_ref[2 * p + 1]])
+        if p % 4 == 3:
+            rows = pl.ds(2 * ROWS * (p - 3), 8 * ROWS)
+            copies.append(pltpu.make_async_copy(packed_ref.at[rows], out_ref.at[rows], sent.at[p // 4]))
+            copies[-1].start()
+    for copy in copies:
+        copy.wait()
 
 
 def owner_kernel(coded_ref, left_in, right_in, total_ref, left_out, right_out, out_ref, *scratch):
@@ -313,20 +320,23 @@
     ahead, behind, here = zip(owns, others)
     left_relay, right_relay = along(1, left_relay), along(-1, right_relay)
     left_direct, right_direct = pair_sum(1, *ahead), pair_sum(0, *behind)
-    ahead, behind, _, _ = lax.optimization_barrier((ahead, behind, left_direct, right_direct))
-    left_direct, right_direct = along(1, left_direct), along(-1, right_direct)
-    left_summed = along(1, pair_sum(0, *ahead, left_relay))
-    right_summed = along(-1, pair_sum(1, *behind, right_relay))
+    left_direct = along(1, left_direct)
+    left_summed, right_summed = pair_sum(0, *ahead, left_relay), pair_sum(1, *behind, right_relay)
+    left_summed, right_summed, right_direct = lax.optimization_barrier((left_summed, right_summed, right_direct))
+    left_summed, right_summed = along(1, left_summed), along(-1, right_summed)
+    right_direct = along(-1, right_direct)
     strips, total = pl.pallas_call(
         sum_kernel,
         in_specs=[ANY] + [VMEM] * 6,
-        out_specs=[VMEM] * 2,
+        out_specs=[ANY, VMEM],
         scratch_shapes=[
             pltpu.SMEM((shards,), jnp.int32),
             pltpu.VMEM((shards, ROWS, 128), jnp.int32),
+            pltpu.VMEM(wire.shape, wire.dtype),
             pltpu.SemaphoreType.DMA,
+            pltpu.SemaphoreType.DMA((shards // 8,)),
         ],
-        out_shape=[pltpu.VMEM(wire.shape, wire.dtype), number],
+        out_shape=[wire, number],
         compiler_params=params(8),
         name="sum_strips",
     )(owned, *here, left_summed, right_direct, left_direct, right_summed)

time: 94.5 us -> 93.1 us (0.985)
  waiting for transfers between devices: 32.1 us -> 29.8 us
  starting transfers between devices: 22.3 us -> 24.4 us
  blocking collectives: 22.9 us -> 21.4 us
    ppermute x3, waiting for transfers between devices: 9.87 us -> 5.7 us  [body(): other = lax.ppermute(total, 'dp', [(d, d ^ bit) for d in range(groups)])]
    ppermute x3, starting transfers between devices: 0.1 us -> 4.26 us  [body(): other = lax.ppermute(total, 'dp', [(d, d ^ bit) for d in range(groups)])]
    ppermute x6, waiting for transfers between devices: 13.7 us -> 16.8 us  [along(): lax.ppermute(array, 'dp', [(d, (d + 2 * ahead) % groups) for d in range(g...]
    ppermute x6, starting transfers between devices: 9.94 us -> 8 us  [along(): lax.ppermute(array, 'dp', [(d, (d + 2 * ahead) % groups) for d in range(g...]
    all_to_all x1, blocking collectives: 22.9 us -> 21.4 us  [body(): lax.all_to_all(pieces, 'shard', split_axis=0, concat_axis=0, tiled=True)]
    all_to_all x1, waiting for transfers between devices: 8.45 us -> 7.25 us  [body(): lax.all_to_all(strips, 'shard', split_axis=0, concat_axis=0, tiled=True)]
  transfers between devices with their start and end apart: 14 -> 14, of which waited for: 9 -> 8; matrix products, arithmetic and copies ran while one was open for 0% -> 0% of each run, Pallas kernels for 3% -> 3%
where the time goes in v6:
time: 93.1 us; the launch traced here: 92.6 us
  waiting for transfers between devices  29.8 us (32%)
  starting transfers between devices  24.4 us (26%)
  blocking collectives  21.4 us (23%)
  Pallas kernels  16.1 us (17%)
    all_to_all x1, blocking collectives, body(): lax.all_to_all(pieces, 'shard', split_axis=0, concat_axis=0, tiled=True)  21.4 us
    ppermute x6, waiting for transfers between devices, along(): lax.ppermute(array, 'dp', [(d, (d + 2 * ahead) % groups) for d in range(g...  16.8 us
    all_to_all x1, starting transfers between devices, body(): lax.all_to_all(strips, 'shard', split_axis=0, concat_axis=0, tiled=True)  11.4 us
    pallas_call x1, Pallas kernels, body(): pl.pallas_call(owner_kernel, in_specs=[VMEM, ANY, ANY, VMEM], out_specs=[...  8.06 us
    ppermute x6, starting transfers between devices, along(): lax.ppermute(array, 'dp', [(d, (d + 2 * ahead) % groups) for d in range(g...  8 us
    all_to_all x1, waiting for transfers between devices, body(): lax.all_to_all(strips, 'shard', split_axis=0, concat_axis=0, tiled=True)  7.25 us
    ppermute x3, waiting for transfers between devices, body(): other = lax.ppermute(total, 'dp', [(d, d ^ bit) for d in range(groups)])  5.7 us
    ppermute x3, starting transfers between devices, body(): other = lax.ppermute(total, 'dp', [(d, d ^ bit) for d in range(groups)])  4.26 us
  transfers between devices with their start and end apart: 14, of which 8 were waited for; matrix products, arithmetic and copies ran while one was open for 0% of the time, Pallas kernels for 3%

profile of v6, /device:TPU:32, one launch (start us, length us, event | category | flops | bytes accessed | tf_op | source)
XLA Modules:
  0.0 92.6 jit_solution(13428282242580716338)
XLA Ops:
  0.6 1.1 %cut_1.1 = bf16[32,16,512]{2,1,0:T(8,128)(2,1)S(1)} custom-call(bf16[8,32,16,512]{3,2,1,0:T(8,128)(2,1)} %bitcast.14), custom_call_target="tpu_custom_call" | custom-call | tf_op jit(solution)/shard_map/cut_1/pallas_call | solution.py:288
  1.7 0.1 collective-permute-start
  1.8 2.1 %cut_7.1 = (bf16[32,16,512]{2,1,0:T(8,128)(2,1)S(1)}, bf16[32,16,512]{2,1,0:T(8,128)(2,1)S(1)}, bf16[32,16,512]{2,1,0:T(8,128)(2,1)S(1)}, bf16[32,16,512]{2,1,0:...) custom-call(bf16[8,32,16,512]{3,2,1,0:T(8,128)(2,1)} %bitcast.15), custom_call_target="tpu_custom_call" | custom-call | tf_op jit(solution)/shard_map/cut_7/pallas_call | solution.py:288
  3.9 0.6 collective-permute-start.2
  4.4 0.1 collective-permute-start.4
  4.5 0.0 collective-permute-done.refs_1_
  4.6 0.0 copy-start.2
  4.6 0.2 pair_1_0.2
  4.7 0.2 pair_0_0.2
  4.9 1.6 %collective-permute-start.3 = (s16[1088,128]{1,0:T(8,128)(2,1)S(1)}, s16[1088,128]{1,0:T(8,128)(2,1)S(1)}, u32[]{:S(2)}, u32[]{:S(2)}) collective-permute-start(s16[1088,128]{1,0:T(8,128)(2,1)S(1)} %pair_0_0.2), channel_id=1, source_target_pairs={{0,64},{32,96},{64,128},{96,160},{128,192},{160,224},{192,0},{224,... | collective-permute-start | bytes 835592 | tf_op jit(solution)/shard_map/ppermute | solution.py:302
  6.4 1.7 %collective-permute-start.5 = (s16[1088,128]{1,0:T(8,128)(2,1)S(1)}, s16[1088,128]{1,0:T(8,128)(2,1)S(1)}, u32[]{:S(2)}, u32[]{:S(2)}) collective-permute-start(s16[1088,128]{1,0:T(8,128)(2,1)S(1)} %pair_1_0.2), channel_id=1, source_target_pairs={{0,192},{32,224},{64,0},{96,32},{128,64},{160,96},{192,128},{224,1... | collective-permute-start | bytes 835592 | tf_op jit(solution)/shard_map/ppermute | solution.py:302
  8.2 0.0 collective-permute-start.1
  8.2 0.0 collective-permute-done.2.refs_1_
  8.2 0.2 pair_1_0.3
  8.3 0.0 copy-start
  8.4 0.0 copy-start.1
  8.4 0.4 collective-permute-start.8
  8.7 0.0 collective-permute-done.4.refs_1_
  8.7 0.2 pair_0_0.3
  8.9 6.7 %collective-permute-done.3.refs_2_ = s16[1088,128]{1,0:T(8,128)(2,1)S(1)} collective-permute-done((s16[1088,128]{1,0:T(8,128)(2,1)S(1)}, s16[1088,128]{1,0:T(8,128)(2,1)S(1)}, u32[]{:S(2)}, u32[]{:S(2)}) %collective-permute-start.3) | collective-permute-done | bytes 278560 | tf_op jit(solution)/shard_map/ppermute | solution.py:302
  15.6 0.2 pair_0_1.1
  15.9 0.0 collective-permute-done.5.refs_2_
  15.9 0.2 pair_1_1.1
  16.1 0.8 collective-permute-start.6
  17.0 2.5 %collective-permute-start.7 = (s16[1088,128]{1,0:T(8,128)(2,1)S(1)}, s16[1088,128]{1,0:T(8,128)(2,1)S(1)}, u32[]{:S(2)}, u32[]{:S(2)}) collective-permute-start(s16[1088,128]{1,0:T(8,128)(2,1)S(1)} %pair_0_0.3), channel_id=1, source_target_pairs={{0,192},{32,224},{64,0},{96,32},{128,64},{160,96},{192,128},{224,1... | collective-permute-start | bytes 835592 | tf_op jit(solution)/shard_map/ppermute | solution.py:302
  19.4 1.0 %collective-permute-start.9 = (s16[1088,128]{1,0:T(8,128)(2,1)S(1)}, s16[1088,128]{1,0:T(8,128)(2,1)S(1)}, u32[]{:S(2)}, u32[]{:S(2)}) collective-permute-start(s16[1088,128]{1,0:T(8,128)(2,1)S(1)} %pair_1_1.1), channel_id=1, source_target_pairs={{0,192},{32,224},{64,0},{96,32},{128,64},{160,96},{192,128},{224,1... | collective-permute-start | bytes 835592 | tf_op jit(solution)/shard_map/ppermute | solution.py:302
  20.5 0.0 collective-permute-done.1.other_ref
  20.5 1.1 %collective-permute-done.8.refs_2_ = s16[1088,128]{1,0:T(8,128)(2,1)S(1)} collective-permute-done((s16[1088,128]{1,0:T(8,128)(2,1)S(1)}, s16[1088,128]{1,0:T(8,128)(2,1)S(1)}, u32[]{:S(2)}, u32[]{:S(2)}) %collective-permute-start.8) | collective-permute-done | bytes 278560 | tf_op jit(solution)/shard_map/ppermute | solution.py:302
  21.6 5.5 %collective-permute-done.6.refs_0_ = s16[1088,128]{1,0:T(8,128)(2,1)S(1)} collective-permute-done((s16[1088,128]{1,0:T(8,128)(2,1)S(1)}, s16[1088,128]{1,0:T(8,128)(2,1)S(1)}, u32[]{:S(2)}, u32[]{:S(2)}) %collective-permute-start.6) | collective-permute-done | bytes 278560 | tf_op jit(solution)/shard_map/ppermute | solution.py:302
  27.1 0.0 collective-permute-done.7.refs_1_
  27.1 3.4 %collective-permute-done.9.refs_3_ = s16[1088,128]{1,0:T(8,128)(2,1)S(1)} collective-permute-done((s16[1088,128]{1,0:T(8,128)(2,1)S(1)}, s16[1088,128]{1,0:T(8,128)(2,1)S(1)}, u32[]{:S(2)}, u32[]{:S(2)}) %collective-permute-start.9) | collective-permute-done | bytes 278560 | tf_op jit(solution)/shard_map/ppermute | solution.py:302
  30.5 0.0 copy-done.2
  30.5 2.0 %sum_strips.1 = (s16[2304,128]{1,0:T(8,128)(2,1)}, f32[8,128]{1,0:T(8,128)S(1)}) custom-call(s32[8,32]{1,0:T(8,128)S(1)} %copy-done.2, bf16[32,16,512]{2,1,0:T(8,128)(2,1)S(1)} %get-tuple-element.31.own_ref, bf16[32,16,512]{2,1,0:T(8,128)(2,1)S(1)} %collective-permute-done.1.other_ref, s16[1088,128]{1,0:T(8,128)(2,1)S(1)} %collective-permute-done.6.refs_0_, ...), custom_call_target="tpu_custom_call" | custom-call | tf_op jit(solution)/shard_map/sum_strips/pallas_call | solution.py:328
  32.5 11.4 %all-to-all-start = ((s16[32,72,128]{2,1,0:T(8,128)(2,1)}), s16[32,72,128]{2,1,0:T(8,128)(2,1)S(1)}, u32[]{:S(2)}, u32[]{:S(2)}) async-start(s16[32,72,128]{2,1,0:T(8,128)(2,1)} %bitcast.1), calls=%async_computation | async-start | bytes 1179648 | tf_op jit(solution)/shard_map/all_to_all | solution.py:343
  43.9 0.1 collective-permute-start.10
  44.0 1.2 %collective-permute-done.10.second_ref = f32[8,128]{1,0:T(8,128)S(1)} collective-permute-done((f32[8,128]{1,0:T(8,128)S(1)}, f32[8,128]{1,0:T(8,128)S(1)}, u32[]{:S(2)}, u32[]{:S(2)}) %collective-permute-start.10) | collective-permute-done | bytes 4128 | tf_op jit(solution)/shard_map/ppermute | solution.py:345
  45.1 1.2 %collective-permute-start.11 = (f32[8,128]{1,0:T(8,128)S(1)}, f32[8,128]{1,0:T(8,128)S(1)}, u32[]{:S(2)}, u32[]{:S(2)}) collective-permute-start(f32[8,128]{1,0:T(8,128)S(1)} %add_1.1.first_ref), channel_id=1, source_target_pairs={{0,64},{32,96},{64,0},{96,32},{128,192},{160,224},{192,128},{224,1... | collective-permute-start | bytes 12296 | tf_op jit(solution)/shard_map/ppermute | solution.py:345
  46.3 2.4 %collective-permute-done.11.second_ref = f32[8,128]{1,0:T(8,128)S(1)} collective-permute-done((f32[8,128]{1,0:T(8,128)S(1)}, f32[8,128]{1,0:T(8,128)S(1)}, u32[]{:S(2)}, u32[]{:S(2)}) %collective-permute-start.11) | collective-permute-done | bytes 4128 | tf_op jit(solution)/shard_map/ppermute | solution.py:345
  48.7 3.0 %collective-permute-start.12 = (f32[8,128]{1,0:T(8,128)S(1)}, f32[8,128]{1,0:T(8,128)S(1)}, u32[]{:S(2)}, u32[]{:S(2)}) collective-permute-start(f32[8,128]{1,0:T(8,128)S(1)} %add_2.1.first_ref), channel_id=1, source_target_pairs={{0,128},{32,160},{64,192},{96,224},{128,0},{160,32},{192,64},{224,... | collective-permute-start | bytes 12296 | tf_op jit(solution)/shard_map/ppermute | solution.py:345
  51.7 2.1 %collective-permute-done.12.second_ref = f32[8,128]{1,0:T(8,128)S(1)} collective-permute-done((f32[8,128]{1,0:T(8,128)S(1)}, f32[8,128]{1,0:T(8,128)S(1)}, u32[]{:S(2)}, u32[]{:S(2)}) %collective-permute-start.12) | collective-permute-done | bytes 4128 | tf_op jit(solution)/shard_map/ppermute | solution.py:345
  53.9 7.2 %all-to-all-done = s16[32,72,128]{2,1,0:T(8,128)(2,1)S(1)} async-done(((s16[32,72,128]{2,1,0:T(8,128)(2,1)}), s16[32,72,128]{2,1,0:T(8,128)(2,1)S(1)}, u32[]{:S(2)}, u32[]{:S(2)}) %all-to-all-start) | async-done | bytes 589856 | tf_op jit(solution)/shard_map/all_to_all | solution.py:343
  61.1 0.0 copy-done
  61.1 0.0 copy-done.1
  61.1 8.1 %owner.1 = (f32[512,512]{1,0:T(8,128)}, f32[512,512]{1,0:T(8,128)}, s16[2304,128]{1,0:T(8,128)(2,1)S(1)}) custom-call(s16[2304,128]{1,0:T(8,128)(2,1)S(1)} %bitcast.10, f32[512,512]{1,0:T(8,128)S(1)} %bitcast.11, f32[512,512]{1,0:T(8,128)S(1)} %bitcast.12, f32[8,128]{1,0:T(8,128)S(1)} %add_4.1.total_ref), custom_call_target="tpu_custom_call" | custom-call | tf_op jit(solution)/shard_map/owner/pallas_call | solution.py:354
  69.2 21.4 %all_to_all.22 = s16[32,72,128]{2,1,0:T(8,128)(2,1)S(1)} all-to-all(s16[32,72,128]{2,1,0:T(8,128)(2,1)S(1)} %bitcast.13), channel_id=1, replica_groups=mesh['dp'=8,'shard'=32] {'shard'}, dimensions={0} | all-to-all | bytes 1179648 | tf_op jit(solution)/shard_map/all_to_all | solution.py:363
  90.6 1.8 %update.1 = f32[32,16,512]{2,1,0:T(8,128)} custom-call(s32[8,32]{1,0:T(8,128)S(1)} %copy-done.2, s16[2304,128]{1,0:T(8,128)(2,1)S(1)} %bitcast.9), custom_call_target="tpu_custom_call" | custom-call | tf_op jit(solution)/shard_map/update/pallas_call | solution.py:364
  (3 shorter events, 0.0 us)
Async XLA Ops:
  1.7 2.8 %collective-permute-start = (bf16[32,16,512]{2,1,0:T(8,128)(2,1)S(1)}, bf16[32,16,512]{2,1,0:T(8,128)(2,1)S(1)}, u32[]{:S(2)}, u32[]{:S(2)}) collective-permute-start(bf16[32,16,512]{2,1,0:T(8,128)(2,1)S(1)} %cut_1.1), channel_id=1, source_target_pairs={{0,32},{32,0},{64,96},{96,64},{128,160},{160,128},{192,224},{224,1... | collective-permute-start | bytes 1572872 | tf_op jit(solution)/shard_map/ppermute | solution.py:299
  3.9 4.3 %collective-permute-start.2 = (bf16[32,16,512]{2,1,0:T(8,128)(2,1)S(1)}, bf16[32,16,512]{2,1,0:T(8,128)(2,1)S(1)}, u32[]{:S(2)}, u32[]{:S(2)}) collective-permute-start(bf16[32,16,512]{2,1,0:T(8,128)(2,1)S(1)} %get-tuple-element.34), channel_id=1, source_target_pairs={{0,32},{32,0},{64,96},{96,64},{128,160},{160,128},{192,224},{224,1... | collective-permute-start | bytes 1572872 | tf_op jit(solution)/shard_map/ppermute | solution.py:299
  4.4 4.3 %collective-permute-start.4 = (bf16[32,16,512]{2,1,0:T(8,128)(2,1)S(1)}, bf16[32,16,512]{2,1,0:T(8,128)(2,1)S(1)}, u32[]{:S(2)}, u32[]{:S(2)}) collective-permute-start(bf16[32,16,512]{2,1,0:T(8,128)(2,1)S(1)} %get-tuple-element.37), channel_id=1, source_target_pairs={{0,32},{32,0},{64,96},{96,64},{128,160},{160,128},{192,224},{224,1... | collective-permute-start | bytes 1572872 | tf_op jit(solution)/shard_map/ppermute | solution.py:299
  4.6 26.0 %copy-start.2 = (s32[8,32]{1,0:T(8,128)S(1)}, s32[8,32]{1,0:T(8,128)}, u32[]{:S(2)}) copy-start(s32[8,32]{1,0:T(8,128)} %refs_0_.1) | copy-start | bytes 3076
  4.9 10.8 %collective-permute-start.3 = (s16[1088,128]{1,0:T(8,128)(2,1)S(1)}, s16[1088,128]{1,0:T(8,128)(2,1)S(1)}, u32[]{:S(2)}, u32[]{:S(2)}) collective-permute-start(s16[1088,128]{1,0:T(8,128)(2,1)S(1)} %pair_0_0.2), channel_id=1, source_target_pairs={{0,64},{32,96},{64,128},{96,160},{128,192},{160,224},{192,0},{224,... | collective-permute-start | bytes 835592 | tf_op jit(solution)/shard_map/ppermute | solution.py:302
  6.4 9.4 %collective-permute-start.5 = (s16[1088,128]{1,0:T(8,128)(2,1)S(1)}, s16[1088,128]{1,0:T(8,128)(2,1)S(1)}, u32[]{:S(2)}, u32[]{:S(2)}) collective-permute-start(s16[1088,128]{1,0:T(8,128)(2,1)S(1)} %pair_1_0.2), channel_id=1, source_target_pairs={{0,192},{32,224},{64,0},{96,32},{128,64},{160,96},{192,128},{224,1... | collective-permute-start | bytes 835592 | tf_op jit(solution)/shard_map/ppermute | solution.py:302
  8.2 12.3 %collective-permute-start.1 = (bf16[32,16,512]{2,1,0:T(8,128)(2,1)S(1)}, bf16[32,16,512]{2,1,0:T(8,128)(2,1)S(1)}, u32[]{:S(2)}, u32[]{:S(2)}) collective-permute-start(bf16[32,16,512]{2,1,0:T(8,128)(2,1)S(1)} %get-tuple-element.32), channel_id=1, source_target_pairs={{0,32},{32,0},{64,96},{96,64},{128,160},{160,128},{192,224},{224,1... | collective-permute-start | bytes 1572872 | tf_op jit(solution)/shard_map/ppermute | solution.py:299
  8.3 52.8 %copy-start = (f32[1,1,512,512]{3,2,1,0:T(8,128)S(1)}, f32[1,1,512,512]{3,2,1,0:T(8,128)}, u32[]{:S(2)}) copy-start(f32[1,1,512,512]{3,2,1,0:T(8,128)} %param.6) | copy-start | bytes 3145732
  8.4 52.8 %copy-start.1 = (f32[1,1,512,512]{3,2,1,0:T(8,128)S(1)}, f32[1,1,512,512]{3,2,1,0:T(8,128)}, u32[]{:S(2)}) copy-start(f32[1,1,512,512]{3,2,1,0:T(8,128)} %param.7) | copy-start | bytes 3145732
  8.4 13.2 %collective-permute-start.8 = (s16[1088,128]{1,0:T(8,128)(2,1)S(1)}, s16[1088,128]{1,0:T(8,128)(2,1)S(1)}, u32[]{:S(2)}, u32[]{:S(2)}) collective-permute-start(s16[1088,128]{1,0:T(8,128)(2,1)S(1)} %pair_1_0.3), channel_id=1, source_target_pairs={{0,64},{32,96},{64,128},{96,160},{128,192},{160,224},{192,0},{224,... | collective-permute-start | bytes 835592 | tf_op jit(solution)/shard_map/ppermute | solution.py:302
  16.1 11.0 %collective-permute-start.6 = (s16[1088,128]{1,0:T(8,128)(2,1)S(1)}, s16[1088,128]{1,0:T(8,128)(2,1)S(1)}, u32[]{:S(2)}, u32[]{:S(2)}) collective-permute-start(s16[1088,128]{1,0:T(8,128)(2,1)S(1)} %pair_0_1.1), channel_id=1, source_target_pairs={{0,64},{32,96},{64,128},{96,160},{128,192},{160,224},{192,0},{224,... | collective-permute-start | bytes 835592 | tf_op jit(solution)/shard_map/ppermute | solution.py:302
  17.0 10.1 %collective-permute-start.7 = (s16[1088,128]{1,0:T(8,128)(2,1)S(1)}, s16[1088,128]{1,0:T(8,128)(2,1)S(1)}, u32[]{:S(2)}, u32[]{:S(2)}) collective-permute-start(s16[1088,128]{1,0:T(8,128)(2,1)S(1)} %pair_0_0.3), channel_id=1, source_target_pairs={{0,192},{32,224},{64,0},{96,32},{128,64},{160,96},{192,128},{224,1... | collective-permute-start | bytes 835592 | tf_op jit(solution)/shard_map/ppermute | solution.py:302
  19.4 11.1 %collective-permute-start.9 = (s16[1088,128]{1,0:T(8,128)(2,1)S(1)}, s16[1088,128]{1,0:T(8,128)(2,1)S(1)}, u32[]{:S(2)}, u32[]{:S(2)}) collective-permute-start(s16[1088,128]{1,0:T(8,128)(2,1)S(1)} %pair_1_1.1), channel_id=1, source_target_pairs={{0,192},{32,224},{64,0},{96,32},{128,64},{160,96},{192,128},{224,1... | collective-permute-start | bytes 835592 | tf_op jit(solution)/shard_map/ppermute | solution.py:302
  32.5 28.6 %all-to-all-start = ((s16[32,72,128]{2,1,0:T(8,128)(2,1)}), s16[32,72,128]{2,1,0:T(8,128)(2,1)S(1)}, u32[]{:S(2)}, u32[]{:S(2)}) async-start(s16[32,72,128]{2,1,0:T(8,128)(2,1)} %bitcast.1), calls=%async_computation | async-start | bytes 1179648 | tf_op jit(solution)/shard_map/all_to_all | solution.py:343
  43.9 1.3 %collective-permute-start.10 = (f32[8,128]{1,0:T(8,128)S(1)}, f32[8,128]{1,0:T(8,128)S(1)}, u32[]{:S(2)}, u32[]{:S(2)}) collective-permute-start(f32[8,128]{1,0:T(8,128)S(1)} %get-tuple-element.43.first_ref), channel_id=1, source_target_pairs={{0,32},{32,0},{64,96},{96,64},{128,160},{160,128},{192,224},{224,1... | collective-permute-start | bytes 12296 | tf_op jit(solution)/shard_map/ppermute | solution.py:345
  45.1 3.6 %collective-permute-start.11 = (f32[8,128]{1,0:T(8,128)S(1)}, f32[8,128]{1,0:T(8,128)S(1)}, u32[]{:S(2)}, u32[]{:S(2)}) collective-permute-start(f32[8,128]{1,0:T(8,128)S(1)} %add_1.1.first_ref), channel_id=1, source_target_pairs={{0,64},{32,96},{64,0},{96,32},{128,192},{160,224},{192,128},{224,1... | collective-permute-start | bytes 12296 | tf_op jit(solution)/shard_map/ppermute | solution.py:345
  48.7 5.1 %collective-permute-start.12 = (f32[8,128]{1,0:T(8,128)S(1)}, f32[8,128]{1,0:T(8,128)S(1)}, u32[]{:S(2)}, u32[]{:S(2)}) collective-permute-start(f32[8,128]{1,0:T(8,128)S(1)} %add_2.1.first_ref), channel_id=1, source_target_pairs={{0,128},{32,160},{64,192},{96,224},{128,0},{160,32},{192,64},{224,... | collective-permute-start | bytes 12296 | tf_op jit(solution)/shard_map/ppermute | solution.py:345

commit v7 on v6

--- a/solution.py
+++ b/solution.py
@@ -313,18 +313,19 @@
 
     held, far = lax.optimization_barrier((grouped, cut(60, grouped, (2, 1))))
     far = partner(*far)
-    own, *rest = cut(57, held, (2, 0), (1, 1), (-1, 1), (0, 1), (1, 0), (-1, 0), (0, 0))
-    others = [partner(array) for array in rest[:3]]
+    own, *others = cut(57, held, (2, 0), (1, 1), (-1, 1))
+    others = [partner(array) for array in others]
     left_relay, right_relay = pair_sum(0, own, far), pair_sum(1, own, far)
-    owns, left_relay, right_relay = lax.optimization_barrier((rest[3:], left_relay, right_relay))
-    ahead, behind, here = zip(owns, others)
+    held, left_relay, right_relay = lax.optimization_barrier((held, left_relay, right_relay))
     left_relay, right_relay = along(1, left_relay), along(-1, right_relay)
+    *owns, other = cut(57, held, (1, 0), (-1, 0), (0, 0), (0, 1))
+    ahead, behind, here = zip(owns, [*others, partner(other)])
     left_direct, right_direct = pair_sum(1, *ahead), pair_sum(0, *behind)
+    right_direct = along(-1, right_direct)
+    left_summed, right_summed = pair_sum(0, *ahead, left_relay), pair_sum(1, *behind, right_relay)
+    left_summed, right_summed, left_direct = lax.optimization_barrier((left_summed, right_summed, left_direct))
+    left_summed, right_summed = along(1, left_summed), along(-1, right_summed)
     left_direct = along(1, left_direct)
-    left_summed, right_summed = pair_sum(0, *ahead, left_relay), pair_sum(1, *behind, right_relay)
-    left_summed, right_summed, right_direct = lax.optimization_barrier((left_summed, right_summed, right_direct))
-    left_summed, right_summed = along(1, left_summed), along(-1, right_summed)
-    right_direct = along(-1, right_direct)
     strips, total = pl.pallas_call(
         sum_kernel,
         in_specs=[ANY] + [VMEM] * 6,

time: 93.1 us -> 93.7 us (level)
  Pallas kernels: 16.1 us -> 17.7 us
  starting transfers between devices: 24.4 us -> 23 us
    ppermute x3, starting transfers between devices: 4.26 us -> 1.04 us  [body(): other = lax.ppermute(total, 'dp', [(d, d ^ bit) for d in range(groups)])]
    ppermute x3, waiting for transfers between devices: 5.7 us -> 8.93 us  [body(): other = lax.ppermute(total, 'dp', [(d, d ^ bit) for d in range(groups)])]
    ppermute x6, waiting for transfers between devices: 16.8 us -> 14 us  [along(): lax.ppermute(array, 'dp', [(d, (d + 2 * ahead) % groups) for d in range(g...]
    ppermute x6, starting transfers between devices: 8 us -> 9.74 us  [along(): lax.ppermute(array, 'dp', [(d, (d + 2 * ahead) % groups) for d in range(g...]
    pallas_call x2 -> x3, Pallas kernels: 3.15 us -> 4.82 us  [cut(): pl.pallas_call(lambda *refs: cut_kernel([(ahead % chips, other) for ahead...]
  transfers between devices with their start and end apart: 14 -> 14, of which waited for: 8 -> 9; matrix products, arithmetic and copies ran while one was open for 0% -> 0% of each run, Pallas kernels for 3% -> 5%
where the time goes in v7:
time: 93.7 us; the launch traced here: 93.3 us
  waiting for transfers between devices  30.2 us (32%)
  starting transfers between devices  23 us (25%)
  blocking collectives  21.4 us (23%)
  Pallas kernels  17.7 us (19%)
    all_to_all x1, blocking collectives, body(): lax.all_to_all(pieces, 'shard', split_axis=0, concat_axis=0, tiled=True)  21.4 us
    ppermute x6, waiting for transfers between devices, along(): lax.ppermute(array, 'dp', [(d, (d + 2 * ahead) % groups) for d in range(g...  14 us
    all_to_all x1, starting transfers between devices, body(): lax.all_to_all(strips, 'shard', split_axis=0, concat_axis=0, tiled=True)  11.4 us
    ppermute x6, starting transfers between devices, along(): lax.ppermute(array, 'dp', [(d, (d + 2 * ahead) % groups) for d in range(g...  9.74 us
    ppermute x3, waiting for transfers between devices, body(): other = lax.ppermute(total, 'dp', [(d, d ^ bit) for d in range(groups)])  8.93 us
    pallas_call x1, Pallas kernels, body(): pl.pallas_call(owner_kernel, in_specs=[VMEM, ANY, ANY, VMEM], out_specs=[...  8.04 us
    all_to_all x1, waiting for transfers between devices, body(): lax.all_to_all(strips, 'shard', split_axis=0, concat_axis=0, tiled=True)  7.31 us
    pallas_call x3, Pallas kernels, cut(): pl.pallas_call(lambda *refs: cut_kernel([(ahead % chips, other) for ahead...  4.82 us
  transfers between devices with their start and end apart: 14, of which 9 were waited for; matrix products, arithmetic and copies ran while one was open for 0% of the time, Pallas kernels for 5%

profile of v7, /device:TPU:32, one launch (start us, length us, event | category | flops | bytes accessed | tf_op | source)
XLA Modules:
  0.0 93.3 jit_solution(18187903986134160672)
XLA Ops:
  0.6 1.1 %cut_1.1 = bf16[32,16,512]{2,1,0:T(8,128)(2,1)S(1)} custom-call(bf16[8,32,16,512]{3,2,1,0:T(8,128)(2,1)} %bitcast.14), custom_call_target="tpu_custom_call" | custom-call | tf_op jit(solution)/shard_map/cut_1/pallas_call | solution.py:288
  1.7 0.1 collective-permute-start
  1.8 2.2 %cut_3.1 = (bf16[32,16,512]{2,1,0:T(8,128)(2,1)S(1)}, bf16[32,16,512]{2,1,0:T(8,128)(2,1)}, bf16[32,16,512]{2,1,0:T(8,128)(2,1)S(1)}) custom-call(bf16[8,32,16,512]{3,2,1,0:T(8,128)(2,1)} %bitcast.15), custom_call_target="tpu_custom_call" | custom-call | tf_op jit(solution)/shard_map/cut_3/pallas_call | solution.py:288
  4.0 0.6 collective-permute-start.4
  4.6 0.1 collective-permute-start.2
  4.7 0.0 collective-permute-done.refs_1_
  4.7 0.2 pair_1_0.2
  4.8 0.2 pair_0_0.2
  5.0 0.0 copy-start.2
  5.0 1.6 %collective-permute-start.3 = (s16[1088,128]{1,0:T(8,128)(2,1)S(1)}, s16[1088,128]{1,0:T(8,128)(2,1)S(1)}, u32[]{:S(2)}, u32[]{:S(2)}) collective-permute-start(s16[1088,128]{1,0:T(8,128)(2,1)S(1)} %pair_0_0.2), channel_id=1, source_target_pairs={{0,64},{32,96},{64,128},{96,160},{128,192},{160,224},{192,0},{224,... | collective-permute-start | bytes 835592 | tf_op jit(solution)/shard_map/ppermute | solution.py:302
  6.6 1.7 %collective-permute-start.5 = (s16[1088,128]{1,0:T(8,128)(2,1)S(1)}, s16[1088,128]{1,0:T(8,128)(2,1)S(1)}, u32[]{:S(2)}, u32[]{:S(2)}) collective-permute-start(s16[1088,128]{1,0:T(8,128)(2,1)S(1)} %pair_1_0.2), channel_id=1, source_target_pairs={{0,192},{32,224},{64,0},{96,32},{128,64},{160,96},{192,128},{224,1... | collective-permute-start | bytes 835592 | tf_op jit(solution)/shard_map/ppermute | solution.py:302
  8.3 1.5 %cut_4.1 = (bf16[32,16,512]{2,1,0:T(8,128)(2,1)S(1)}, bf16[32,16,512]{2,1,0:T(8,128)(2,1)S(1)}, bf16[32,16,512]{2,1,0:T(8,128)(2,1)S(1)}, bf16[32,16,512]{2,1,0:T(8,128)(2,1)S(1)}) custom-call(bf16[8,32,16,512]{3,2,1,0:T(8,128)(2,1)} %bitcast.16), custom_call_target="tpu_custom_call" | custom-call | tf_op jit(solution)/shard_map/cut_4/pallas_call | solution.py:288
  9.9 0.1 collective-permute-start.1
  10.0 0.0 collective-permute-done.4.refs_1_
  10.0 0.2 pair_0_0.3
  10.1 0.0 copy-start
  10.2 0.0 copy-start.1
  10.2 1.6 %collective-permute-start.7 = (s16[1088,128]{1,0:T(8,128)(2,1)S(1)}, s16[1088,128]{1,0:T(8,128)(2,1)S(1)}, u32[]{:S(2)}, u32[]{:S(2)}) collective-permute-start(s16[1088,128]{1,0:T(8,128)(2,1)S(1)} %pair_0_0.3), channel_id=1, source_target_pairs={{0,192},{32,224},{64,0},{96,32},{128,64},{160,96},{192,128},{224,1... | collective-permute-start | bytes 835592 | tf_op jit(solution)/shard_map/ppermute | solution.py:302
  11.8 0.0 collective-permute-done.2.refs_1_
  11.8 0.2 pair_1_0.3
  12.0 3.3 %collective-permute-done.3.refs_2_ = s16[1088,128]{1,0:T(8,128)(2,1)S(1)} collective-permute-done((s16[1088,128]{1,0:T(8,128)(2,1)S(1)}, s16[1088,128]{1,0:T(8,128)(2,1)S(1)}, u32[]{:S(2)}, u32[]{:S(2)}) %collective-permute-start.3) | collective-permute-done | bytes 278560 | tf_op jit(solution)/shard_map/ppermute | solution.py:302
  15.3 0.2 pair_0_1.1
  15.5 0.5 collective-permute-done.5.refs_2_
  16.1 0.2 pair_1_1.1
  16.3 1.6 %collective-permute-start.6 = (s16[1088,128]{1,0:T(8,128)(2,1)S(1)}, s16[1088,128]{1,0:T(8,128)(2,1)S(1)}, u32[]{:S(2)}, u32[]{:S(2)}) collective-permute-start(s16[1088,128]{1,0:T(8,128)(2,1)S(1)} %pair_0_1.1), channel_id=1, source_target_pairs={{0,64},{32,96},{64,128},{96,160},{128,192},{160,224},{192,0},{224,... | collective-permute-start | bytes 835592 | tf_op jit(solution)/shard_map/ppermute | solution.py:302
  17.9 1.2 %collective-permute-start.8 = (s16[1088,128]{1,0:T(8,128)(2,1)S(1)}, s16[1088,128]{1,0:T(8,128)(2,1)S(1)}, u32[]{:S(2)}, u32[]{:S(2)}) collective-permute-start(s16[1088,128]{1,0:T(8,128)(2,1)S(1)} %pair_1_0.3), channel_id=1, source_target_pairs={{0,64},{32,96},{64,128},{96,160},{128,192},{160,224},{192,0},{224,... | collective-permute-start | bytes 835592 | tf_op jit(solution)/shard_map/ppermute | solution.py:302
  19.1 2.0 %collective-permute-start.9 = (s16[1088,128]{1,0:T(8,128)(2,1)S(1)}, s16[1088,128]{1,0:T(8,128)(2,1)S(1)}, u32[]{:S(2)}, u32[]{:S(2)}) collective-permute-start(s16[1088,128]{1,0:T(8,128)(2,1)S(1)} %pair_1_1.1), channel_id=1, source_target_pairs={{0,192},{32,224},{64,0},{96,32},{128,64},{160,96},{192,128},{224,1... | collective-permute-start | bytes 835592 | tf_op jit(solution)/shard_map/ppermute | solution.py:302
  21.1 0.9 collective-permute-done.7.refs_1_
  22.0 0.0 collective-permute-done.1.other_ref
  22.1 5.2 %collective-permute-done.6.refs_0_ = s16[1088,128]{1,0:T(8,128)(2,1)S(1)} collective-permute-done((s16[1088,128]{1,0:T(8,128)(2,1)S(1)}, s16[1088,128]{1,0:T(8,128)(2,1)S(1)}, u32[]{:S(2)}, u32[]{:S(2)}) %collective-permute-start.6) | collective-permute-done | bytes 278560 | tf_op jit(solution)/shard_map/ppermute | solution.py:302
  27.2 4.0 %collective-permute-done.8.refs_2_ = s16[1088,128]{1,0:T(8,128)(2,1)S(1)} collective-permute-done((s16[1088,128]{1,0:T(8,128)(2,1)S(1)}, s16[1088,128]{1,0:T(8,128)(2,1)S(1)}, u32[]{:S(2)}, u32[]{:S(2)}) %collective-permute-start.8) | collective-permute-done | bytes 278560 | tf_op jit(solution)/shard_map/ppermute | solution.py:302
  31.2 0.0 collective-permute-done.9.refs_3_
  31.3 0.0 copy-done.2
  31.3 2.0 %sum_strips.1 = (s16[2304,128]{1,0:T(8,128)(2,1)}, f32[8,128]{1,0:T(8,128)S(1)}) custom-call(s32[8,32]{1,0:T(8,128)S(1)} %copy-done.2, bf16[32,16,512]{2,1,0:T(8,128)(2,1)S(1)} %get-tuple-element.27.own_ref, bf16[32,16,512]{2,1,0:T(8,128)(2,1)S(1)} %collective-permute-done.1.other_ref, s16[1088,128]{1,0:T(8,128)(2,1)S(1)} %collective-permute-done.6.refs_0_, ...), custom_call_target="tpu_custom_call" | custom-call | tf_op jit(solution)/shard_map/sum_strips/pallas_call | solution.py:329
  33.2 11.4 %all-to-all-start = ((s16[32,72,128]{2,1,0:T(8,128)(2,1)}), s16[32,72,128]{2,1,0:T(8,128)(2,1)S(1)}, u32[]{:S(2)}, u32[]{:S(2)}) async-start(s16[32,72,128]{2,1,0:T(8,128)(2,1)} %bitcast.1), calls=%async_computation | async-start | bytes 1179648 | tf_op jit(solution)/shard_map/all_to_all | solution.py:344
  44.6 0.1 collective-permute-start.10
  44.7 1.2 %collective-permute-done.10.second_ref = f32[8,128]{1,0:T(8,128)S(1)} collective-permute-done((f32[8,128]{1,0:T(8,128)S(1)}, f32[8,128]{1,0:T(8,128)S(1)}, u32[]{:S(2)}, u32[]{:S(2)}) %collective-permute-start.10) | collective-permute-done | bytes 4128 | tf_op jit(solution)/shard_map/ppermute | solution.py:346
  45.9 0.0 collective-permute-start.11
  45.9 3.6 %collective-permute-done.11.second_ref = f32[8,128]{1,0:T(8,128)S(1)} collective-permute-done((f32[8,128]{1,0:T(8,128)S(1)}, f32[8,128]{1,0:T(8,128)S(1)}, u32[]{:S(2)}, u32[]{:S(2)}) %collective-permute-start.11) | collective-permute-done | bytes 4128 | tf_op jit(solution)/shard_map/ppermute | solution.py:346
  49.5 0.9 %collective-permute-start.12 = (f32[8,128]{1,0:T(8,128)S(1)}, f32[8,128]{1,0:T(8,128)S(1)}, u32[]{:S(2)}, u32[]{:S(2)}) collective-permute-start(f32[8,128]{1,0:T(8,128)S(1)} %add_2.1.first_ref), channel_id=1, source_target_pairs={{0,128},{32,160},{64,192},{96,224},{128,0},{160,32},{192,64},{224,... | collective-permute-start | bytes 12296 | tf_op jit(solution)/shard_map/ppermute | solution.py:346
  50.4 4.2 %collective-permute-done.12.second_ref = f32[8,128]{1,0:T(8,128)S(1)} collective-permute-done((f32[8,128]{1,0:T(8,128)S(1)}, f32[8,128]{1,0:T(8,128)S(1)}, u32[]{:S(2)}, u32[]{:S(2)}) %collective-permute-start.12) | collective-permute-done | bytes 4128 | tf_op jit(solution)/shard_map/ppermute | solution.py:346
  54.6 7.3 %all-to-all-done = s16[32,72,128]{2,1,0:T(8,128)(2,1)S(1)} async-done(((s16[32,72,128]{2,1,0:T(8,128)(2,1)}), s16[32,72,128]{2,1,0:T(8,128)(2,1)S(1)}, u32[]{:S(2)}, u32[]{:S(2)}) %all-to-all-start) | async-done | bytes 589856 | tf_op jit(solution)/shard_map/all_to_all | solution.py:344
  61.9 0.0 copy-done
  61.9 0.0 copy-done.1
  61.9 8.0 %owner.1 = (f32[512,512]{1,0:T(8,128)}, f32[512,512]{1,0:T(8,128)}, s16[2304,128]{1,0:T(8,128)(2,1)S(1)}) custom-call(s16[2304,128]{1,0:T(8,128)(2,1)S(1)} %bitcast.10, f32[512,512]{1,0:T(8,128)S(1)} %bitcast.11, f32[512,512]{1,0:T(8,128)S(1)} %bitcast.12, f32[8,128]{1,0:T(8,128)S(1)} %add_4.1.total_ref), custom_call_target="tpu_custom_call" | custom-call | tf_op jit(solution)/shard_map/owner/pallas_call | solution.py:355
  70.0 21.4 %all_to_all.22 = s16[32,72,128]{2,1,0:T(8,128)(2,1)S(1)} all-to-all(s16[32,72,128]{2,1,0:T(8,128)(2,1)S(1)} %bitcast.13), channel_id=1, replica_groups=mesh['dp'=8,'shard'=32] {'shard'}, dimensions={0} | all-to-all | bytes 1179648 | tf_op jit(solution)/shard_map/all_to_all | solution.py:364
  91.4 1.8 %update.1 = f32[32,16,512]{2,1,0:T(8,128)} custom-call(s32[8,32]{1,0:T(8,128)S(1)} %copy-done.2, s16[2304,128]{1,0:T(8,128)(2,1)S(1)} %bitcast.9), custom_call_target="tpu_custom_call" | custom-call | tf_op jit(solution)/shard_map/update/pallas_call | solution.py:365
  (3 shorter events, 0.0 us)
Async XLA Ops:
  1.7 3.0 %collective-permute-start = (bf16[32,16,512]{2,1,0:T(8,128)(2,1)S(1)}, bf16[32,16,512]{2,1,0:T(8,128)(2,1)S(1)}, u32[]{:S(2)}, u32[]{:S(2)}) collective-permute-start(bf16[32,16,512]{2,1,0:T(8,128)(2,1)S(1)} %cut_1.1), channel_id=1, source_target_pairs={{0,32},{32,0},{64,96},{96,64},{128,160},{160,128},{192,224},{224,1... | collective-permute-start | bytes 1572872 | tf_op jit(solution)/shard_map/ppermute | solution.py:299
  4.0 6.0 %collective-permute-start.4 = (bf16[32,16,512]{2,1,0:T(8,128)(2,1)S(1)}, bf16[32,16,512]{2,1,0:T(8,128)(2,1)S(1)}, u32[]{:S(2)}, u32[]{:S(2)}) collective-permute-start(bf16[32,16,512]{2,1,0:T(8,128)(2,1)S(1)} %get-tuple-element.33), channel_id=1, source_target_pairs={{0,32},{32,0},{64,96},{96,64},{128,160},{160,128},{192,224},{224,1... | collective-permute-start | bytes 1572872 | tf_op jit(solution)/shard_map/ppermute | solution.py:299
  4.6 7.2 %collective-permute-start.2 = (bf16[32,16,512]{2,1,0:T(8,128)(2,1)}, bf16[32,16,512]{2,1,0:T(8,128)(2,1)S(1)}, u32[]{:S(2)}, u32[]{:S(2)}) collective-permute-start(bf16[32,16,512]{2,1,0:T(8,128)(2,1)} %get-tuple-element.30), channel_id=1, source_target_pairs={{0,32},{32,0},{64,96},{96,64},{128,160},{160,128},{192,224},{224,1... | collective-permute-start | bytes 1572872 | tf_op jit(solution)/shard_map/ppermute | solution.py:299
  5.0 26.3 %copy-start.2 = (s32[8,32]{1,0:T(8,128)S(1)}, s32[8,32]{1,0:T(8,128)}, u32[]{:S(2)}) copy-start(s32[8,32]{1,0:T(8,128)} %refs_0_.1) | copy-start | bytes 3076
  5.0 10.3 %collective-permute-start.3 = (s16[1088,128]{1,0:T(8,128)(2,1)S(1)}, s16[1088,128]{1,0:T(8,128)(2,1)S(1)}, u32[]{:S(2)}, u32[]{:S(2)}) collective-permute-start(s16[1088,128]{1,0:T(8,128)(2,1)S(1)} %pair_0_0.2), channel_id=1, source_target_pairs={{0,64},{32,96},{64,128},{96,160},{128,192},{160,224},{192,0},{224,... | collective-permute-start | bytes 835592 | tf_op jit(solution)/shard_map/ppermute | solution.py:302
  6.6 9.5 %collective-permute-start.5 = (s16[1088,128]{1,0:T(8,128)(2,1)S(1)}, s16[1088,128]{1,0:T(8,128)(2,1)S(1)}, u32[]{:S(2)}, u32[]{:S(2)}) collective-permute-start(s16[1088,128]{1,0:T(8,128)(2,1)S(1)} %pair_1_0.2), channel_id=1, source_target_pairs={{0,192},{32,224},{64,0},{96,32},{128,64},{160,96},{192,128},{224,1... | collective-permute-start | bytes 835592 | tf_op jit(solution)/shard_map/ppermute | solution.py:302
  9.9 12.2 %collective-permute-start.1 = (bf16[32,16,512]{2,1,0:T(8,128)(2,1)S(1)}, bf16[32,16,512]{2,1,0:T(8,128)(2,1)S(1)}, u32[]{:S(2)}, u32[]{:S(2)}) collective-permute-start(bf16[32,16,512]{2,1,0:T(8,128)(2,1)S(1)} %get-tuple-element.28), channel_id=1, source_target_pairs={{0,32},{32,0},{64,96},{96,64},{128,160},{160,128},{192,224},{224,1... | collective-permute-start | bytes 1572872 | tf_op jit(solution)/shard_map/ppermute | solution.py:299
  10.1 51.7 %copy-start = (f32[1,1,512,512]{3,2,1,0:T(8,128)S(1)}, f32[1,1,512,512]{3,2,1,0:T(8,128)}, u32[]{:S(2)}) copy-start(f32[1,1,512,512]{3,2,1,0:T(8,128)} %param.6) | copy-start | bytes 3145732
  10.2 51.7 %copy-start.1 = (f32[1,1,512,512]{3,2,1,0:T(8,128)S(1)}, f32[1,1,512,512]{3,2,1,0:T(8,128)}, u32[]{:S(2)}) copy-start(f32[1,1,512,512]{3,2,1,0:T(8,128)} %param.7) | copy-start | bytes 3145732
  10.2 11.9 %collective-permute-start.7 = (s16[1088,128]{1,0:T(8,128)(2,1)S(1)}, s16[1088,128]{1,0:T(8,128)(2,1)S(1)}, u32[]{:S(2)}, u32[]{:S(2)}) collective-permute-start(s16[1088,128]{1,0:T(8,128)(2,1)S(1)} %pair_0_0.3), channel_id=1, source_target_pairs={{0,192},{32,224},{64,0},{96,32},{128,64},{160,96},{192,128},{224,1... | collective-permute-start | bytes 835592 | tf_op jit(solution)/shard_map/ppermute | solution.py:302
  16.3 10.9 %collective-permute-start.6 = (s16[1088,128]{1,0:T(8,128)(2,1)S(1)}, s16[1088,128]{1,0:T(8,128)(2,1)S(1)}, u32[]{:S(2)}, u32[]{:S(2)}) collective-permute-start(s16[1088,128]{1,0:T(8,128)(2,1)S(1)} %pair_0_1.1), channel_id=1, source_target_pairs={{0,64},{32,96},{64,128},{96,160},{128,192},{160,224},{192,0},{224,... | collective-permute-start | bytes 835592 | tf_op jit(solution)/shard_map/ppermute | solution.py:302
  17.9 13.4 %collective-permute-start.8 = (s16[1088,128]{1,0:T(8,128)(2,1)S(1)}, s16[1088,128]{1,0:T(8,128)(2,1)S(1)}, u32[]{:S(2)}, u32[]{:S(2)}) collective-permute-start(s16[1088,128]{1,0:T(8,128)(2,1)S(1)} %pair_1_0.3), channel_id=1, source_target_pairs={{0,64},{32,96},{64,128},{96,160},{128,192},{160,224},{192,0},{224,... | collective-permute-start | bytes 835592 | tf_op jit(solution)/shard_map/ppermute | solution.py:302
  19.1 12.2 %collective-permute-start.9 = (s16[1088,128]{1,0:T(8,128)(2,1)S(1)}, s16[1088,128]{1,0:T(8,128)(2,1)S(1)}, u32[]{:S(2)}, u32[]{:S(2)}) collective-permute-start(s16[1088,128]{1,0:T(8,128)(2,1)S(1)} %pair_1_1.1), channel_id=1, source_target_pairs={{0,192},{32,224},{64,0},{96,32},{128,64},{160,96},{192,128},{224,1... | collective-permute-start | bytes 835592 | tf_op jit(solution)/shard_map/ppermute | solution.py:302
  33.2 28.7 %all-to-all-start = ((s16[32,72,128]{2,1,0:T(8,128)(2,1)}), s16[32,72,128]{2,1,0:T(8,128)(2,1)S(1)}, u32[]{:S(2)}, u32[]{:S(2)}) async-start(s16[32,72,128]{2,1,0:T(8,128)(2,1)} %bitcast.1), calls=%async_computation | async-start | bytes 1179648 | tf_op jit(solution)/shard_map/all_to_all | solution.py:344
  44.6 1.3 %collective-permute-start.10 = (f32[8,128]{1,0:T(8,128)S(1)}, f32[8,128]{1,0:T(8,128)S(1)}, u32[]{:S(2)}, u32[]{:S(2)}) collective-permute-start(f32[8,128]{1,0:T(8,128)S(1)} %get-tuple-element.39.first_ref), channel_id=1, source_target_pairs={{0,32},{32,0},{64,96},{96,64},{128,160},{160,128},{192,224},{224,1... | collective-permute-start | bytes 12296 | tf_op jit(solution)/shard_map/ppermute | solution.py:346
  45.9 3.6 %collective-permute-start.11 = (f32[8,128]{1,0:T(8,128)S(1)}, f32[8,128]{1,0:T(8,128)S(1)}, u32[]{:S(2)}, u32[]{:S(2)}) collective-permute-start(f32[8,128]{1,0:T(8,128)S(1)} %add_1.1.first_ref), channel_id=1, source_target_pairs={{0,64},{32,96},{64,0},{96,32},{128,192},{160,224},{192,128},{224,1... | collective-permute-start | bytes 12296 | tf_op jit(solution)/shard_map/ppermute | solution.py:346
  49.5 5.1 %collective-permute-start.12 = (f32[8,128]{1,0:T(8,128)S(1)}, f32[8,128]{1,0:T(8,128)S(1)}, u32[]{:S(2)}, u32[]{:S(2)}) collective-permute-start(f32[8,128]{1,0:T(8,128)S(1)} %add_2.1.first_ref), channel_id=1, source_target_pairs={{0,128},{32,160},{64,192},{96,224},{128,0},{160,32},{192,64},{224,... | collective-permute-start | bytes 12296 | tf_op jit(solution)/shard_map/ppermute | solution.py:346
